TPU v7x, 32 devices: a whole 2x2x4 slice. The times are simulated.
32 devices in a mesh: layer: 2 (over y), prow: 4 (over x, core), pcol: 4 (over z).
Axes of the slice: x: 2, y: 2, z: 4, core: 2. Of those that a mesh axis runs over, the one named last changes fastest.
Arguments:
- subtree_right_hand: bfloat16 [2, 6144, 512], P('layer', ('prow', 'pcol')), may hold values from -6 to 6
- root_rhs: bfloat16 [2048, 512], P(('prow', 'pcol')), may hold values from -6 to 6
- blocks: bfloat16 [2, 6, 4, 4, 4, 4, 128, 128], P('layer', None, 'prow', 'pcol'), may hold values from -0.1875 to 0.1875
- pattern: int32 [2, 6, 4, 4, 4, 4], P('layer', None, 'prow', 'pcol'), may hold values 0 or 1
- forest_inverse: float32 [2, 3, 4, 4, 128, 128], P('layer', None, 'prow', 'pcol'), may hold values from -0.5 to 0.5
- root_inverse: float32 [4, 4, 128, 128], P('prow', 'pcol'), may hold values from -0.5 to 0.5
Outputs:
- forest_solution: bfloat16 [2, 6144, 512], P('layer', ('prow', 'pcol'))
- root_solution: bfloat16 [2048, 512], P(('prow', 'pcol'))
All inputs are finite; a program needn't handle non-finite values. No bound on the sum of `pattern` on one device may be relied on, other than what follows from the above.
Results may differ from a plain program's by a relative error of at most 0.0057.
Values may be sent and summed in bfloat16 or wider, within the bound.
No kernel may reach another device: no remote copies, remote signals or barrier semaphores. Data moves between devices by JAX's collectives and lax.ppermute only.
A program may use at most 64 MiB of HBM per device.

v0:
```python
import jax
import jax.numpy as jnp
from jax import lax
from jax.sharding import PartitionSpec as P


def pair_slot(source, target):
    return (0, 3, 5)[source] + target - source - 1


def shards(subtree_right_hand, root_rhs, blocks, pattern, forest_inverse, root_inverse):
    grid_size = lax.axis_size("prow")
    super_rows = blocks.shape[-1]
    rhs_cols = subtree_right_hand.shape[-1]
    slice_rows = super_rows // grid_size
    local_forest = subtree_right_hand.reshape(3, grid_size, slice_rows, rhs_cols)
    local_root = root_rhs.reshape(1, grid_size, slice_rows, rhs_cols)
    joined = jnp.concatenate([local_forest, local_root], axis=0)
    placed = lax.all_to_all(
        lax.all_to_all(joined, "prow", split_axis=1, concat_axis=1, tiled=True),
        "pcol",
        split_axis=1,
        concat_axis=1,
        tiled=True,
    )
    placed = placed.reshape(4, super_rows, rhs_cols)
    block_mask = pattern.reshape(6, grid_size, grid_size).astype(jnp.bfloat16)
    masked = (
        blocks.reshape(6, grid_size, grid_size, super_rows, super_rows)
        * block_mask[..., None, None]
    )
    inverses = forest_inverse.reshape(3, super_rows, super_rows)
    solved = []
    empty_rows = jnp.zeros((grid_size, super_rows, rhs_cols), jnp.float32)
    totals = (empty_rows, empty_rows, empty_rows, empty_rows)
    for tier_index in range(3):
        right_hand_side = placed[tier_index].astype(jnp.float32)
        if tier_index > 0:
            reduced = lax.psum_scatter(totals[tier_index], "pcol", scatter_dimension=0, tiled=True)
            right_hand_side = right_hand_side - reduced[0]
        answer = jnp.dot(
            inverses[tier_index],
            right_hand_side,
            precision=lax.Precision.HIGHEST,
            preferred_element_type=jnp.float32,
        ).astype(jnp.bfloat16)
        solved.append(answer)

        def update(running, block_pieces, first_row, tier_index=tier_index):
            count = block_pieces.shape[0]
            updated_rows = []
            for target in range(4):
                if target > tier_index:
                    factor_weights = masked[pair_slot(tier_index, target)]
                    term = jnp.einsum(
                        "jznv,zvs->jns",
                        factor_weights,
                        block_pieces,
                        preferred_element_type=jnp.float32,
                    )
                    updated_rows.append(running[target] + term)
                else:
                    updated_rows.append(running[target])
            return tuple(updated_rows)

        totals = update(
            totals, lax.all_gather(answer[None], "prow", axis=0, tiled=True), jnp.int32(0)
        )
    row_share = lax.psum_scatter(totals[3], "pcol", scatter_dimension=0, tiled=True)
    reduced_root = lax.psum(row_share[0], "layer")
    root_side = placed[3].astype(jnp.float32) - reduced_root
    root_answer = jnp.dot(
        root_inverse.reshape(super_rows, super_rows),
        root_side,
        precision=lax.Precision.HIGHEST,
        preferred_element_type=jnp.float32,
    ).astype(jnp.bfloat16)
    stacked = jnp.stack(solved + [root_answer]).reshape(4, grid_size, slice_rows, rhs_cols)
    returned = lax.all_to_all(
        lax.all_to_all(stacked, "pcol", split_axis=1, concat_axis=1, tiled=True),
        "prow",
        split_axis=1,
        concat_axis=1,
        tiled=True,
    )
    forest_out = returned[:3].reshape(1, 3 * super_rows, rhs_cols)
    root_out = returned[3].reshape(super_rows, rhs_cols)
    return (forest_out, root_out)


def solution(mesh):
    placed = (
        P("layer", ("prow", "pcol"), None),
        P(("prow", "pcol"), None),
        P("layer", None, "prow", "pcol", None, None, None, None),
        P("layer", None, "prow", "pcol", None, None),
        P("layer", None, "prow", "pcol", None, None),
        P("prow", "pcol", None, None),
    )
    return jax.shard_map(
        shards,
        mesh=mesh,
        in_specs=placed,
        out_specs=(P("layer", ("prow", "pcol"), None), P(("prow", "pcol"), None)),
        check_vma=False,
    )
```

profile of v0, /device:TPU:6, one launch (start us, length us, event | category | flops | bytes accessed | tf_op | source)
XLA Modules:
  0.0 212.7 jit_solution(4917753078483968702)
XLA Ops:
  7.2 0.0 copy-start
  7.2 0.0 copy-start.7
  7.2 1.1 pad_maximum_fusion
  8.4 10.8 %all_to_all.20 = bf16[4,4,32,512]{3,2,0,1:T(8,128)(2,1)} all-to-all(bf16[4,4,32,512]{3,2,0,1:T(8,128)(2,1)S(1)} %copy.14), channel_id=1, replica_groups=mesh['layer'=2,'prow'=4,'pcol'=4] {'prow'}, dimensions={1} | all-to-all | bytes 1048576 | tf_op jit(solution)/shard_map/all_to_all | solution.py:20
  19.2 4.9 %all-to-all-start.1 = ((bf16[4,4,32,512]{3,2,0,1:T(8,128)(2,1)}), bf16[4,4,32,512]{3,2,0,1:T(8,128)(2,1)}, u32[]{:S(2)}, u32[]{:S(2)}) async-start(bf16[4,4,32,512]{3,2,0,1:T(8,128)(2,1)} %all_to_all.20), calls=%async_computation.1 | async-start | bytes 1048576 | tf_op jit(solution)/shard_map/all_to_all | solution.py:19
  24.1 0.0 reduce-scatter.4.cloned.1.call-start
  24.1 0.0 copy-done.7
  24.1 0.1 copy.15
  24.2 2.2 %bitcast_multiply_fusion = bf16[6,4,4,128,128]{4,3,2,1,0:T(8,128)(2,1)S(1)} fusion(bf16[1,6,1,1,4,4,128,128]{7,6,5,4,3,2,1,0:T(8,128)(2,1)} %param.8, bf16[6,4,4]{2,1,0:T(4,128)(2,1)S(1)} %copy.15), kind=kLoop, calls=%fused_computation | loop fusion | flops 1572864 | bytes 6291648 | tf_op jit(solution)/shard_map/mul | solution.py:29
  26.4 12.3 %all-to-all-done.1 = bf16[4,4,32,512]{3,2,0,1:T(8,128)(2,1)} async-done(((bf16[4,4,32,512]{3,2,0,1:T(8,128)(2,1)}), bf16[4,4,32,512]{3,2,0,1:T(8,128)(2,1)}, u32[]{:S(2)}, u32[]{:S(2)}) %all-to-all-start.1) | async-done | bytes 524320 | tf_op jit(solution)/shard_map/all_to_all | solution.py:19
  38.7 1.8 fusion.14
  40.5 1.1 convolution_convert_fusion.3
  41.6 6.9 %all-gather = bf16[512,512]{1,0:T(8,128)(2,1)S(1)} all-gather(bf16[128,512]{1,0:T(8,128)(2,1)S(1)} %bitcast.118), channel_id=2, replica_groups=mesh['layer'=2,'prow'=4,'pcol'=4] {'prow'}, dimensions={0}, use_global_device_ids=true | all-gather | bytes 655360 | tf_op jit(solution)/shard_map/all_gather | solution.py:67
  48.6 0.8 copy-done.1
  49.4 1.4 convolution_bitcast_fusion.5
  50.8 0.0 reduce-scatter.4.cloned.1.call-update
  50.8 0.0 reduce-scatter.6.cloned.1.call-start
  50.9 26.3 %reduce-scatter.4.cloned.1.call-done = f32[1,128,512]{2,1,0:T(8,128)} async-done(((f32[4,128,512]{2,1,0:T(8,128)}), f32[1,128,512]{2,1,0:T(8,128)}) %reduce-scatter.4.cloned.1.call-update) | async-done | bytes 262160 | tf_op jit(solution)/shard_map/reduce_scatter | solution.py:39
  77.2 1.5 convolution_convert_fusion.2
  78.7 6.6 %all-gather.1 = bf16[512,512]{1,0:T(8,128)(2,1)S(1)} all-gather(bf16[128,512]{1,0:T(8,128)(2,1)S(1)} %bitcast.120), channel_id=3, replica_groups=mesh['layer'=2,'prow'=4,'pcol'=4] {'prow'}, dimensions={0}, use_global_device_ids=true | all-gather | bytes 655360 | tf_op jit(solution)/shard_map/all_gather | solution.py:67
  85.3 0.8 copy-done.4
  86.1 0.4 convolution_bitcast_fusion.3
  86.5 0.0 copy-done.2
  86.5 1.4 fusion
  88.0 0.0 reduce-scatter.6.cloned.1.call-update
  88.0 0.0 reduce-scatter.8.cloned.1.call-start
  88.1 2.4 %convolution_bitcast_fusion.1 = f32[4,128,512]{2,1,0:T(8,128)} fusion(bf16[4,128,512,1]{2,1,0,3:T(8,128)(2,1)} %bitcast.116, bf16[6,4,4,128,128]{4,3,2,1,0:T(8,128)(2,1)S(1)} %bitcast_multiply_fusion), kind=kOutput, calls=%fused_computation.2 | convolution fusion | flops 268435456 | bytes 2097152 | tf_op jit(solution)/shard_map/jznv,zvs->jns/dot_general | solution.py:55
  90.5 23.7 %reduce-scatter.6.cloned.1.call-done = f32[1,128,512]{2,1,0:T(8,128)} async-done(((f32[4,128,512]{2,1,0:T(8,128)}), f32[1,128,512]{2,1,0:T(8,128)}) %reduce-scatter.6.cloned.1.call-update) | async-done | bytes 262160 | tf_op jit(solution)/shard_map/reduce_scatter | solution.py:39
  114.2 1.5 convolution_convert_fusion.1
  115.7 0.0 copy-start.6
  115.7 6.6 %all-gather.2 = bf16[512,512]{1,0:T(8,128)(2,1)S(1)} all-gather(bf16[128,512]{1,0:T(8,128)(2,1)S(1)} %bitcast.122), channel_id=4, replica_groups=mesh['layer'=2,'prow'=4,'pcol'=4] {'prow'}, dimensions={0}, use_global_device_ids=true | all-gather | bytes 655360 | tf_op jit(solution)/shard_map/all_gather | solution.py:67
  122.3 0.0 copy-done.6
  122.3 0.4 convolution_bitcast_fusion
  122.8 0.0 copy-done.3
  122.8 0.0 copy-done.5
  122.8 1.4 fusion.2
  124.2 0.0 reduce-scatter.8.cloned.1.call-update
  124.2 0.0 all-reduce.2.cloned.1.call-start
  124.3 26.1 %reduce-scatter.8.cloned.1.call-done = f32[1,128,512]{2,1,0:T(8,128)} async-done(((f32[4,128,512]{2,1,0:T(8,128)}), f32[1,128,512]{2,1,0:T(8,128)}) %reduce-scatter.8.cloned.1.call-update) | async-done | bytes 262160 | tf_op jit(solution)/shard_map/reduce_scatter | solution.py:69
  150.4 0.0 all-reduce.2.cloned.1.call-update
  150.4 23.2 %all-reduce.2.cloned.1.call-done = f32[128,512]{1,0:T(8,128)} async-done(((f32[128,512]{1,0:T(8,128)}), f32[128,512]{1,0:T(8,128)}) %all-reduce.2.cloned.1.call-update) | async-done | bytes 262160 | tf_op jit(solution)/shard_map/psum | solution.py:70
  173.6 0.0 copy-done
  173.6 1.4 convolution_convert_fusion
  175.0 1.0 pad_maximum_fusion.1
  176.0 18.4 %all_to_all.21 = bf16[4,4,32,512]{3,2,0,1:T(8,128)(2,1)S(1)} all-to-all(bf16[4,4,32,512]{3,2,0,1:T(8,128)(2,1)S(1)} %pad_maximum_fusion.1), channel_id=1, replica_groups=mesh['layer'=2,'prow'=4,'pcol'=4] {'pcol'}, dimensions={1} | all-to-all | bytes 1048576 | tf_op jit(solution)/shard_map/all_to_all | solution.py:80
  194.4 10.3 %all_to_all.22 = bf16[4,4,32,512]{3,2,0,1:T(8,128)(2,1)S(1)} all-to-all(bf16[4,4,32,512]{3,2,0,1:T(8,128)(2,1)S(1)} %all_to_all.21), channel_id=1, replica_groups=mesh['layer'=2,'prow'=4,'pcol'=4] {'prow'}, dimensions={1} | all-to-all | bytes 1048576 | tf_op jit(solution)/shard_map/all_to_all | solution.py:79
  204.7 0.8 copy.27
  205.5 0.7 slice.78
  (8 shorter events, 0.1 us)
Async XLA Ops:
  7.2 166.4 %copy-start = (f32[1,1,128,128]{3,2,1,0:T(8,128)S(1)}, f32[1,1,128,128]{3,2,1,0:T(8,128)}, u32[]{:S(2)}) copy-start(f32[1,1,128,128]{3,2,1,0:T(8,128)} %param.11) | copy-start | bytes 196612
  7.2 16.9 %copy-start.7 = (s32[1,6,1,1,4,4]{1,5,4,3,2,0:T(4,128)S(1)}, s32[1,6,1,1,4,4]{1,5,4,3,2,0:T(4,128)}, u32[]{:S(2)}) copy-start(s32[1,6,1,1,4,4]{1,5,4,3,2,0:T(4,128)} %param.9) | copy-start | bytes 1156
  19.2 19.5 %all-to-all-start.1 = ((bf16[4,4,32,512]{3,2,0,1:T(8,128)(2,1)}), bf16[4,4,32,512]{3,2,0,1:T(8,128)(2,1)}, u32[]{:S(2)}, u32[]{:S(2)}) async-start(bf16[4,4,32,512]{3,2,0,1:T(8,128)(2,1)} %all_to_all.20), calls=%async_computation.1 | async-start | bytes 1048576 | tf_op jit(solution)/shard_map/all_to_all | solution.py:19
  24.1 53.1 %reduce-scatter.4.cloned.1.call-start = ((), (), s32[]{:S(2)}) async-start(), calls=%async_computation.7 | async-start | bytes 1310720 | tf_op jit(solution)/shard_map/reduce_scatter | solution.py:39
  48.6 0.8 copy-start.1
  50.8 63.4 %reduce-scatter.6.cloned.1.call-start = ((), (), s32[]{:S(2)}) async-start(), calls=%async_computation.8 | async-start | bytes 1310720 | tf_op jit(solution)/shard_map/reduce_scatter | solution.py:39
  77.2 9.4 %copy-start.2 = (bf16[512,512]{1,0:T(8,128)(2,1)S(1)}, bf16[512,512]{1,0:T(8,128)(2,1)}, u32[]{:S(2)}) copy-start(bf16[512,512]{1,0:T(8,128)(2,1)} %copy-done.1) | copy-start | bytes 1572868
  85.3 0.8 copy-start.4
  88.0 62.4 %reduce-scatter.8.cloned.1.call-start = ((), (), s32[]{:S(2)}) async-start(), calls=%async_computation.9 | async-start | bytes 1310720 | tf_op jit(solution)/shard_map/reduce_scatter | solution.py:69
  114.2 8.6 %copy-start.3 = (bf16[512,512]{1,0:T(8,128)(2,1)S(1)}, bf16[512,512]{1,0:T(8,128)(2,1)}, u32[]{:S(2)}) copy-start(bf16[512,512]{1,0:T(8,128)(2,1)} %copy-done.1) | copy-start | bytes 1572868
  114.2 8.6 %copy-start.5 = (f32[4,128,512]{2,1,0:T(8,128)S(1)}, f32[4,128,512]{2,1,0:T(8,128)}, u32[]{:S(2)}) copy-start(f32[4,128,512]{2,1,0:T(8,128)} %convolution_bitcast_fusion.1) | copy-start | bytes 3145732
  115.7 6.6 %copy-start.6 = (bf16[512,128]{0,1:T(8,128)(2,1)}, bf16[512,128]{0,1:T(8,128)(2,1)S(1)}, u32[]{:S(2)}) copy-start(bf16[512,128]{0,1:T(8,128)(2,1)S(1)} %convolution_convert_fusion.1) | copy-start | bytes 393220
  124.2 49.4 %all-reduce.2.cloned.1.call-start = ((), (), s32[]{:S(2)}) async-start(), calls=%async_computation.10 | async-start | bytes 524288 | tf_op jit(solution)/shard_map/psum | solution.py:70
Sparse Core Ops, SparseCore 0:
  50.9 26.2 reduce-scatter.3
  88.1 26.0 reduce-scatter.5
  124.3 26.0 reduce-scatter.7
  152.6 20.9 all-reduce.1
where the time goes:
time: 217 us; the launch traced here: 213 us
  waiting for transfers between devices  112 us (52%)
  blocking collectives  59.6 us (27%)
  between operations  13.9 us (6%)
  matrix products  13.1 us (6%)
  local copies, waits for them, and re-layouts  5.09 us (2%)
  starting transfers between devices  5 us (2%)
  other arithmetic  4.28 us (2%)
    reduce_scatter x2, waiting for transfers between devices, shards(): lax.psum_scatter(totals[tier_index], 'pcol', scatter_dimension=0, tiled=T...  50 us
    reduce_scatter x1, waiting for transfers between devices, shards(): lax.psum_scatter(totals[3], 'pcol', scatter_dimension=0, tiled=True)  26.1 us
    psum x1, waiting for transfers between devices, shards(): reduced_root = lax.psum(row_share[0], 'layer')  23.2 us
    all_gather x3, blocking collectives, shards(): lax.all_gather(answer[None], 'prow', axis=0, tiled=True)  20.1 us
    all_to_all x1, blocking collectives, shards(): lax.all_to_all(stacked, 'pcol', split_axis=1, concat_axis=1, tiled=True)  18.4 us
    all_to_all x1, waiting for transfers between devices, shards(): lax.all_to_all(lax.all_to_all(joined, 'prow', split_axis=1, concat_axis=1...  12.3 us
    all_to_all x1, blocking collectives, shards(): lax.all_to_all(joined, 'prow', split_axis=1, concat_axis=1, tiled=True)  10.8 us
    all_to_all x1, blocking collectives, shards(): lax.all_to_all(lax.all_to_all(stacked, 'pcol', split_axis=1, concat_axis=...  10.3 us
  transfers between devices with their start and end apart: 5, of which 5 were waited for; matrix products, arithmetic and copies ran while one was open for 2% of the time, Pallas kernels for 0%

commit v1 on v0

v1 whole, which is shorter than its diff:
```python
import functools

import jax
import jax.numpy as jnp
from jax import lax
from jax.experimental import pallas as pl
from jax.experimental.pallas import tpu as pltpu
from jax.sharding import PartitionSpec as P

F32 = jnp.float32
BF16 = jnp.bfloat16
VMEM = pltpu.VMEM
PARAMS = pltpu.CompilerParams(vmem_limit_bytes=32 * 1024 * 1024)
PAIR = {(0, 1): 0, (0, 2): 1, (0, 3): 2, (1, 2): 3, (1, 3): 4, (2, 3): 5}


def whole(count):
    return [pl.BlockSpec(memory_space=VMEM)] * count


def call(kernel, outs, *args, scratch=(), in_specs=None, grid=None):
    extra = {}
    if grid is not None:
        extra["grid"] = grid
    return pl.pallas_call(
        kernel,
        out_shape=[jax.ShapeDtypeStruct(shape, dtype) for shape, dtype in outs],
        in_specs=whole(len(args)) if in_specs is None else in_specs,
        out_specs=whole(len(outs)),
        scratch_shapes=list(scratch),
        compiler_params=PARAMS,
        **extra,
    )(*args)


def dot(left, right):
    return jnp.dot(left, right, preferred_element_type=F32)


def split(value):
    high = value.astype(BF16)
    return high, (value - high.astype(F32)).astype(BF16)


def precise(inverse, value):
    ih, il = split(inverse)
    vh, vl = split(value)
    return dot(
        jnp.concatenate([ih, ih, il], axis=1), jnp.concatenate([vh, vl, vh], axis=0)
    )


def pack_kernel(forest, root, inverse, own, *sends):
    a = lax.axis_index("prow")
    high, low = split(inverse[...])
    half = high.shape[0] // 2
    packed = jnp.concatenate([high[:half], high[half:], low[:half], low[half:]], axis=1)
    own[...] = packed
    for k in range(1, 4):
        first, later = sends[k - 1], sends[k + 2]
        first[:half] = packed
        first[half:] = forest[1, a ^ k]
        later[0] = forest[2, a ^ k]
        later[1] = root[a ^ k]


def mask_kernel(pattern, blocks, out):
    a, b = lax.axis_index("prow"), lax.axis_index("pcol")
    n = pl.program_id(0)
    size = blocks.shape[-1]
    for j in range(4):
        for k in range(4):
            keep = pattern[n, b ^ j, a ^ k]
            block = blocks[0, b ^ j, a ^ k]
            out[0, j, :, k * size : (k + 1) * size] = jnp.where(
                keep != 0, block, jnp.zeros_like(block)
            )


def inject(acc, own, others, slot):
    a, b = lax.axis_index("prow"), lax.axis_index("pcol")
    rows = own.shape[-2]
    acc[...] = jnp.zeros_like(acc)
    place = pl.ds(pl.multiple_of(b * rows, rows), rows)
    for k in range(4):
        value = (own[slot[0], a] if k == 0 else others[k - 1][slot[1]]).astype(F32)
        acc[a ^ b ^ k, place, :] = value


def first_kernel(g0, g1, g2, g3, packed, m1, m2, m3, forest, weights, *rest):
    solved, turned, o0, o1, o2, o3, rows, acc = rest
    a = lax.axis_index("prow")
    part = g0.shape[-2]
    size = 4 * part
    half = size // 2
    for j, piece in enumerate((g0, g1, g2, g3)):
        place = pl.ds(pl.multiple_of((a ^ j) * part, part), part)
        for u in range(4):
            rows[u, place, :] = piece[u]
    for j, message in enumerate((packed, m1, m2, m3)):
        value = message[:half]
        high = jnp.concatenate([value[:, :size], value[:, size : 2 * size]], axis=0)
        low = jnp.concatenate(
            [value[:, 2 * size : 3 * size], value[:, 3 * size :]], axis=0
        )
        side = rows[a ^ j]
        answer = dot(
            jnp.concatenate([high, low], axis=1), jnp.concatenate([side, side], axis=0)
        )
        solved[j * size : (j + 1) * size] = answer.astype(BF16)
    for j in range(4):
        turned[a ^ j] = solved[pl.ds(pl.multiple_of(j * size + a * part, part), part)]
    b = lax.axis_index("pcol")
    acc[...] = jnp.zeros_like(acc)
    place = pl.ds(pl.multiple_of(b * part, part), part)
    for k, message in enumerate((None, m1, m2, m3)):
        value = forest[1, a] if k == 0 else message[half:]
        acc[a ^ b ^ k, place, :] = value.astype(F32)
    for j, out in enumerate((o0, o1, o2, o3)):
        out[...] = (acc[j] - dot(weights[0, j], solved[...])).astype(out.dtype)


def solve_kernel(own, r1, r2, r3, inverse, out):
    value = own[...] + r1[...].astype(F32) + r2[...].astype(F32) + r3[...].astype(F32)
    out[...] = precise(inverse[...], value).astype(out.dtype)


def middle_kernel(s0, s1, s2, s3, weights, acc, *rest):
    solved, turned, o0, o1, o2, o3 = rest
    a = lax.axis_index("prow")
    size = s0.shape[0]
    part = size // 4
    for j, piece in enumerate((s0, s1, s2, s3)):
        solved[j * size : (j + 1) * size] = piece[...]
        turned[a ^ j] = piece[pl.ds(pl.multiple_of(a * part, part), part)]
    for j, out in enumerate((o0, o1, o2, o3)):
        out[...] = (acc[j] - dot(weights[0, j], solved[...])).astype(out.dtype)


def early_kernel(solved, w2, w3, forest, root, c1, c2, c3, acc2, acc3):
    layer = lax.axis_index("layer")
    inject(acc2, forest, (c1, c2, c3), (2, 0))
    inject(acc3, root, (c1, c2, c3), (0, 1))
    first = (layer == 0).astype(F32)
    for j in range(4):
        acc2[j] -= dot(w2[0, j], solved[...])
        acc3[j] = acc3[j] * first - dot(w3[0, j], solved[...])


def later_kernel(solved, weights, acc, out):
    for j in range(4):
        out[j] = acc[j] - dot(weights[0, j], solved[...])


def root_kernel(s0, s1, s2, s3, weights, acc, i0, i1, i2, i3, *rest):
    turned, o0, o1, o2, o3, solved, full = rest
    a, b = lax.axis_index("prow"), lax.axis_index("pcol")
    size = s0.shape[0]
    part = size // 4
    for j, piece in enumerate((s0, s1, s2, s3)):
        solved[j * size : (j + 1) * size] = piece[...]
        turned[a ^ j] = piece[pl.ds(pl.multiple_of(a * part, part), part)]
    for j, inverse in enumerate((i0, i1, i2, i3)):
        full[b ^ j] = precise(inverse[...], acc[j] - dot(weights[0, j], solved[...]))
    for j, out in enumerate((o0, o1, o2, o3)):
        place = pl.ds(pl.multiple_of((b ^ j) * part, part), part)
        out[...] = full[:, place, :].astype(out.dtype)


def total_kernel(own, r1, r2, r3, out):
    value = own[...] + r1[...].astype(F32) + r2[...].astype(F32) + r3[...].astype(F32)
    for layer in range(out.shape[0]):
        out[layer] = value.astype(out.dtype)


def join_kernel(pieces, out):
    out[...] = (pieces[0].astype(F32) + pieces[1].astype(F32)).astype(out.dtype)


def shards(subtree_right_hand, root_rhs, blocks, pattern, forest_inverse, root_inverse):
    layers = lax.axis_size("layer")
    size = blocks.shape[-1]
    part = size // 4
    cols = subtree_right_hand.shape[-1]
    forest = subtree_right_hand.reshape(3, 4, part, cols)
    root = root_rhs.reshape(4, part, cols)
    blocks = blocks.reshape(6, 4, 4, size, size)
    pattern = pattern.reshape(6, 4, 4)
    inverses = forest_inverse.reshape(3, size, size)
    last_inverse = root_inverse.reshape(size, size)
    both = ("prow", "pcol")
    turn = [(i * 4 + j, j * 4 + i) for i in range(4) for j in range(4)]

    def swap(value, axis, k):
        return lax.ppermute(value, axis, [(i, i ^ k) for i in range(4)])

    def gather(value):
        far = swap(value, "prow", 2)
        return value, swap(value, "prow", 1), far, swap(far, "prow", 1)

    def spread(outs):
        return [swap(out, "pcol", k) for k, out in enumerate(outs[1:], 1)]

    def table(pair):
        return pl.BlockSpec((1, 4, size, 4 * size), lambda i: (pair, 0, 0, 0))

    def with_table(kernel, outs, at, pair, *args, scratch=()):
        specs = whole(len(args))
        for index, which in zip(at, pair):
            specs[index] = table(PAIR[which])
        return call(kernel, outs, *args, scratch=scratch, in_specs=specs, grid=(1,))

    piece = ((4, part, cols), BF16)
    partial = [((size, cols), F32)] + [((size, cols), BF16)] * 3
    sums = ((4, size, cols), F32)
    tall = ((4 * size, cols), BF16)

    side = lax.ppermute(forest[0], both, turn)
    packed, *sends = call(
        pack_kernel,
        [((size // 2, cols), BF16)]
        + [((size // 2 + part, cols), BF16)] * 3
        + [((2, part, cols), BF16)] * 3,
        forest,
        root,
        inverses[0],
    )
    early = [swap(send, "prow", k) for k, send in enumerate(sends[:3], 1)]
    weights = pl.pallas_call(
        mask_kernel,
        out_shape=jax.ShapeDtypeStruct((6, 4, size, 4 * size), BF16),
        grid=(6,),
        in_specs=[
            pl.BlockSpec(memory_space=pltpu.SMEM),
            pl.BlockSpec((1, 4, 4, size, size), lambda n: (n, 0, 0, 0, 0)),
        ],
        out_specs=pl.BlockSpec((1, 4, size, 4 * size), lambda n: (n, 0, 0, 0)),
        compiler_params=PARAMS,
    )(pattern, blocks)
    root_inverses = [last_inverse] + [swap(last_inverse, "pcol", k) for k in (1, 2, 3)]

    solved0, turned0, *outs = with_table(
        first_kernel,
        [tall, piece] + partial,
        (9,),
        ((0, 1),),
        *gather(side),
        packed,
        *early,
        forest,
        weights,
        scratch=[VMEM((4, size, cols), BF16), VMEM((4, size, cols), F32)],
    )
    got = spread(outs)
    late = [swap(send, "prow", k) for k, send in enumerate(sends[3:], 1)]
    acc2, acc3 = with_table(
        early_kernel,
        [sums, sums],
        (1, 2),
        ((0, 2), (0, 3)),
        solved0,
        weights,
        weights,
        forest,
        root[None],
        *late,
    )
    (answer,) = call(
        solve_kernel, [((size, cols), BF16)], outs[0], *got, inverses[1]
    )
    given0 = lax.ppermute(turned0, both, turn)
    solved1, turned1, *outs = with_table(
        middle_kernel,
        [tall, piece] + partial,
        (4,),
        ((1, 2),),
        *gather(answer),
        weights,
        acc2,
    )
    got = spread(outs)
    (acc3,) = with_table(later_kernel, [sums], (1,), ((1, 3),), solved1, weights, acc3)
    (answer,) = call(
        solve_kernel, [((size, cols), BF16)], outs[0], *got, inverses[2]
    )
    given1 = lax.ppermute(turned1, both, turn)
    turned2, *outs = with_table(
        root_kernel,
        [piece, ((4, part, cols), F32)] + [piece] * 3,
        (4,),
        ((2, 3),),
        *gather(answer),
        weights,
        acc3,
        *root_inverses,
        scratch=[VMEM((4 * size, cols), BF16), VMEM((4, size, cols), F32)],
    )
    got = spread(outs)
    given2 = lax.ppermute(turned2, both, turn)
    if layers == 2:
        (mine,) = call(
            total_kernel, [((2, 4, part, cols), BF16)], outs[0], *got
        )
        pieces = lax.all_to_all(
            mine.reshape(8, part, cols), ("layer", "prow"), 0, 0, tiled=True
        )
        (root_out,) = call(
            join_kernel, [((4, part, cols), BF16)], pieces.reshape(2, 4, part, cols)
        )
    else:
        (mine,) = call(total_kernel, [((1, 4, part, cols), F32)], outs[0], *got)
        mine = lax.psum(mine[0], "layer")
        root_out = lax.all_to_all(mine, "prow", 0, 0, tiled=True).astype(BF16)
    forest_out = jnp.stack([given0, given1, given2])
    return forest_out.reshape(1, 3 * size, cols), root_out.reshape(size, cols)


def solution(mesh):
    placed = (
        P("layer", ("prow", "pcol"), None),
        P(("prow", "pcol"), None),
        P("layer", None, "prow", "pcol", None, None, None, None),
        P("layer", None, "prow", "pcol", None, None),
        P("layer", None, "prow", "pcol", None, None),
        P("prow", "pcol", None, None),
    )
    return jax.shard_map(
        shards,
        mesh=mesh,
        in_specs=placed,
        out_specs=(P("layer", ("prow", "pcol"), None), P(("prow", "pcol"), None)),
        check_vma=False,
    )
```

time: 217 us -> 124 us (0.57); the launches traced: 213 us -> 122 us
  blocking collectives: 59.6 us -> 0 us
  waiting for transfers between devices: 112 us -> 55 us
  starting transfers between devices: 5 us -> 51.6 us
  matrix products: 13.1 us -> 0 us
  between operations: 13.9 us -> 0.86 us
  Pallas kernels: 0 us -> 7.72 us
  other arithmetic: 4.28 us -> 0.79 us
    reduce_scatter x3 -> x0, waiting for transfers between devices: 76.1 us -> none  [the longest x2 50 us: shards(): lax.psum_scatter(totals[tier_index], 'pcol', scatter_dimension=0, tiled=T...]
    ppermute x0 -> x31, waiting for transfers between devices: none -> 53.9 us  [the longest x27 40.9 us: swap(): return lax.ppermute(value, axis, [(i, i ^ k) for i in range(4)])]
    ppermute x0 -> x31, starting transfers between devices: none -> 40.3 us  [the longest x27 24.6 us: swap(): return lax.ppermute(value, axis, [(i, i ^ k) for i in range(4)])]
    all_to_all x3 -> x0, blocking collectives: 39.5 us -> none  [the longest x1 18.4 us: shards(): lax.all_to_all(stacked, 'pcol', split_axis=1, concat_axis=1, tiled=True)]
    psum x1 -> x0, waiting for transfers between devices: 23.2 us -> none  [shards(): reduced_root = lax.psum(row_share[0], 'layer')]
    all_gather x3 -> x0, blocking collectives: 20.1 us -> none  [shards(): lax.all_gather(answer[None], 'prow', axis=0, tiled=True)]
    dot_general x10 -> x0, matrix products: 13.1 us -> none  [the longest x6 7.59 us: update(): jnp.einsum('jznv,zvs->jns', factor_weights, block_pieces, preferred_eleme...]
    all_to_all x1, waiting for transfers between devices: 12.3 us -> 1.08 us  [shards(): lax.all_to_all(mine.reshape(8, part, cols), ('layer', 'prow'), 0, 0, tile...]
  transfers between devices with their start and end apart: 5 -> 32, of which waited for: 5 -> 16; matrix products, arithmetic and copies ran while one was open for 2% -> 2% of each run, Pallas kernels for 0% -> 3%
where the time goes in v1:
time: 124 us; the launch traced here: 122 us
  waiting for transfers between devices  55 us (44%)
  starting transfers between devices  51.6 us (42%)
  Pallas kernels  7.72 us (6%)
  local copies, waits for them, and re-layouts  6.43 us (5%)
    ppermute x27, waiting for transfers between devices, swap(): return lax.ppermute(value, axis, [(i, i ^ k) for i in range(4)])  40.9 us
    ppermute x27, starting transfers between devices, swap(): return lax.ppermute(value, axis, [(i, i ^ k) for i in range(4)])  24.6 us
    all_to_all x1, starting transfers between devices, shards(): lax.all_to_all(mine.reshape(8, part, cols), ('layer', 'prow'), 0, 0, tile...  11.3 us
    ppermute x1, waiting for transfers between devices, shards(): side = lax.ppermute(forest[0], both, turn)  7.93 us
    pallas_call x10, Pallas kernels, call(): pl.pallas_call(kernel, out_shape=[jax.ShapeDtypeStruct(shape, dtype) for...  6.01 us
    ppermute x1, starting transfers between devices, shards(): side = lax.ppermute(forest[0], both, turn)  4.47 us
    ppermute x1, starting transfers between devices, shards(): given1 = lax.ppermute(turned1, both, turn)  3.99 us
    unnamed x12, local copies, waits for them, and re-layouts  3.8 us
  transfers between devices with their start and end apart: 32, of which 16 were waited for; matrix products, arithmetic and copies ran while one was open for 2% of the time, Pallas kernels for 3%

profile of v1, /device:TPU:6, one launch (start us, length us, event | category | flops | bytes accessed | tf_op | source)
XLA Modules:
  0.0 122.4 jit_solution(7055973091926728023)
XLA Ops:
  0.6 0.9 slice.16
  1.5 4.5 %collective-permute-start = (bf16[4,32,512]{2,1,0:T(8,128)(2,1)S(1)}, bf16[4,32,512]{2,1,0:T(8,128)(2,1)S(1)}, u32[]{:S(2)}, u32[]{:S(2)}) collective-permute-start(bf16[4,32,512]{2,1,0:T(8,128)(2,1)S(1)} %bitcast.33), channel_id=1, source_target_pairs={{0,0},{1,4},{2,8},{3,12},{4,1},{5,5},{6,9},{7,13},{8,2},{9,6},{10,... | collective-permute-start | bytes 393224 | tf_op jit(solution)/shard_map/ppermute | solution.py:218
  6.0 7.9 %collective-permute-done.g0 = bf16[4,32,512]{2,1,0:T(8,128)(2,1)S(1)} collective-permute-done((bf16[4,32,512]{2,1,0:T(8,128)(2,1)S(1)}, bf16[4,32,512]{2,1,0:T(8,128)(2,1)S(1)}, u32[]{:S(2)}, u32[]{:S(2)}) %collective-permute-start) | collective-permute-done | bytes 131104 | tf_op jit(solution)/shard_map/ppermute | solution.py:218
  14.0 5.0 %collective-permute-done.2.g2 = bf16[4,32,512]{2,1,0:T(8,128)(2,1)S(1)} collective-permute-done((bf16[4,32,512]{2,1,0:T(8,128)(2,1)S(1)}, bf16[4,32,512]{2,1,0:T(8,128)(2,1)S(1)}, u32[]{:S(2)}, u32[]{:S(2)}) %collective-permute-start.2) | collective-permute-done | bytes 131104 | tf_op jit(solution)/shard_map/ppermute | solution.py:195
  18.9 0.9 slice_bitcast_fusion
  19.9 1.0 copy-done
  20.9 0.9 copy-done.3
  21.8 0.6 collective-permute-start.4
  22.4 1.4 %collective-permute-start.6 = (bf16[96,512]{1,0:T(8,128)(2,1)S(1)}, bf16[96,512]{1,0:T(8,128)(2,1)S(1)}, u32[]{:S(2)}, u32[]{:S(2)}) collective-permute-start(bf16[96,512]{1,0:T(8,128)(2,1)S(1)} %get-tuple-element.31), channel_id=1, source_target_pairs={{0,12},{4,8},{8,4},{12,0},{1,13},{5,9},{9,5},{13,1},{2,14},{6,10},... | collective-permute-start | bytes 294920 | tf_op jit(solution)/shard_map/ppermute | solution.py:195
  23.8 0.8 copy.8.pattern
  24.6 1.9 %copy-done.2 = bf16[1,6,1,1,4,4,128,128]{7,6,5,4,3,2,1,0:T(8,128)(2,1)S(1)} copy-done((bf16[1,6,1,1,4,4,128,128]{7,6,5,4,3,2,1,0:T(8,128)(2,1)S(1)}, bf16[1,6,1,1,4,4,128,128]{7,6,5,4,3,2,1,0:T(8,128)(2,1)}, u32[]{:S(2)}) %copy-start.2) | copy-done | bytes 3145752
  26.5 1.7 %shard_map.78.weights.w2.w3 = bf16[6,4,128,512]{3,2,1,0:T(8,128)(2,1)S(1)} custom-call(s32[6,4,4]{2,1,0:T(4,128)S(1)} %copy.8.pattern, bf16[6,4,4,128,128]{4,3,2,1,0:T(8,128)(2,1)S(1)} %bitcast.23), custom_call_target="tpu_custom_call" | custom-call | tf_op jit(solution)/shard_map/pallas_call | solution.py:229
  28.4 0.8 shard_map.79
  29.2 2.3 %collective-permute-start.10 = (bf16[128,512]{1,0:T(8,128)(2,1)S(1)}, bf16[128,512]{1,0:T(8,128)(2,1)S(1)}, u32[]{:S(2)}, u32[]{:S(2)}) collective-permute-start(bf16[128,512]{1,0:T(8,128)(2,1)S(1)} %get-tuple-element.36), channel_id=1, source_target_pairs={{0,3},{1,2},{2,1},{3,0},{4,7},{5,6},{6,5},{7,4},{8,11},{9,10},{10,... | collective-permute-start | bytes 393224 | tf_op jit(solution)/shard_map/ppermute | solution.py:195
  31.5 2.2 %collective-permute-start.9 = (bf16[128,512]{1,0:T(8,128)(2,1)S(1)}, bf16[128,512]{1,0:T(8,128)(2,1)S(1)}, u32[]{:S(2)}, u32[]{:S(2)}) collective-permute-start(bf16[128,512]{1,0:T(8,128)(2,1)S(1)} %get-tuple-element.35), channel_id=1, source_target_pairs={{0,2},{1,3},{2,0},{3,1},{4,6},{5,7},{6,4},{7,5},{8,10},{9,11},{10,... | collective-permute-start | bytes 393224 | tf_op jit(solution)/shard_map/ppermute | solution.py:195
  33.7 3.8 %collective-permute-done.10.r3 = bf16[128,512]{1,0:T(8,128)(2,1)S(1)} collective-permute-done((bf16[128,512]{1,0:T(8,128)(2,1)S(1)}, bf16[128,512]{1,0:T(8,128)(2,1)S(1)}, u32[]{:S(2)}, u32[]{:S(2)}) %collective-permute-start.10) | collective-permute-done | bytes 131104 | tf_op jit(solution)/shard_map/ppermute | solution.py:195
  37.5 4.4 %collective-permute-done.8.r1 = bf16[128,512]{1,0:T(8,128)(2,1)S(1)} collective-permute-done((bf16[128,512]{1,0:T(8,128)(2,1)S(1)}, bf16[128,512]{1,0:T(8,128)(2,1)S(1)}, u32[]{:S(2)}, u32[]{:S(2)}) %collective-permute-start.8) | collective-permute-done | bytes 131104 | tf_op jit(solution)/shard_map/ppermute | solution.py:195
  41.9 1.6 %collective-permute-done.9.r2 = bf16[128,512]{1,0:T(8,128)(2,1)S(1)} collective-permute-done((bf16[128,512]{1,0:T(8,128)(2,1)S(1)}, bf16[128,512]{1,0:T(8,128)(2,1)S(1)}, u32[]{:S(2)}, u32[]{:S(2)}) %collective-permute-start.9) | collective-permute-done | bytes 131104 | tf_op jit(solution)/shard_map/ppermute | solution.py:195
  43.8 0.6 collective-permute-start.12
  44.4 4.7 %collective-permute-done.12.s2 = bf16[128,512]{1,0:T(8,128)(2,1)S(1)} collective-permute-done((bf16[128,512]{1,0:T(8,128)(2,1)S(1)}, bf16[128,512]{1,0:T(8,128)(2,1)S(1)}, u32[]{:S(2)}, u32[]{:S(2)}) %collective-permute-start.12) | collective-permute-done | bytes 131104 | tf_op jit(solution)/shard_map/ppermute | solution.py:195
  49.9 1.0 collective-permute-start.16
  50.9 3.4 %collective-permute-done.15.c2 = bf16[2,32,512]{2,1,0:T(8,128)(2,1)S(1)} collective-permute-done((bf16[2,32,512]{2,1,0:T(8,128)(2,1)S(1)}, bf16[2,32,512]{2,1,0:T(8,128)(2,1)S(1)}, u32[]{:S(2)}, u32[]{:S(2)}) %collective-permute-start.15) | collective-permute-done | bytes 65568 | tf_op jit(solution)/shard_map/ppermute | solution.py:195
  54.3 0.8 shard_map.81
  55.7 3.2 %collective-permute-start.19 = (bf16[128,512]{1,0:T(8,128)(2,1)S(1)}, bf16[128,512]{1,0:T(8,128)(2,1)S(1)}, u32[]{:S(2)}, u32[]{:S(2)}) collective-permute-start(bf16[128,512]{1,0:T(8,128)(2,1)S(1)} %get-tuple-element.45), channel_id=1, source_target_pairs={{0,2},{1,3},{2,0},{3,1},{4,6},{5,7},{6,4},{7,5},{8,10},{9,11},{10,... | collective-permute-start | bytes 393224 | tf_op jit(solution)/shard_map/ppermute | solution.py:195
  58.9 1.2 collective-permute-start.20
  60.1 3.8 %collective-permute-done.18.r1 = bf16[128,512]{1,0:T(8,128)(2,1)S(1)} collective-permute-done((bf16[128,512]{1,0:T(8,128)(2,1)S(1)}, bf16[128,512]{1,0:T(8,128)(2,1)S(1)}, u32[]{:S(2)}, u32[]{:S(2)}) %collective-permute-start.18) | collective-permute-done | bytes 131104 | tf_op jit(solution)/shard_map/ppermute | solution.py:195
  63.9 5.0 %collective-permute-done.19.r2 = bf16[128,512]{1,0:T(8,128)(2,1)S(1)} collective-permute-done((bf16[128,512]{1,0:T(8,128)(2,1)S(1)}, bf16[128,512]{1,0:T(8,128)(2,1)S(1)}, u32[]{:S(2)}, u32[]{:S(2)}) %collective-permute-start.19) | collective-permute-done | bytes 131104 | tf_op jit(solution)/shard_map/ppermute | solution.py:195
  69.2 1.5 %collective-permute-start.22 = (bf16[128,512]{1,0:T(8,128)(2,1)S(1)}, bf16[128,512]{1,0:T(8,128)(2,1)S(1)}, u32[]{:S(2)}, u32[]{:S(2)}) collective-permute-start(bf16[128,512]{1,0:T(8,128)(2,1)S(1)} %shard_map.83.s0), channel_id=1, source_target_pairs={{0,8},{4,12},{8,0},{12,4},{1,9},{5,13},{9,1},{13,5},{2,10},{6,14},... | collective-permute-start | bytes 393224 | tf_op jit(solution)/shard_map/ppermute | solution.py:195
  70.7 3.5 %collective-permute-done.22.s2 = bf16[128,512]{1,0:T(8,128)(2,1)S(1)} collective-permute-done((bf16[128,512]{1,0:T(8,128)(2,1)S(1)}, bf16[128,512]{1,0:T(8,128)(2,1)S(1)}, u32[]{:S(2)}, u32[]{:S(2)}) %collective-permute-start.22) | collective-permute-done | bytes 131104 | tf_op jit(solution)/shard_map/ppermute | solution.py:195
  74.2 2.8 %collective-permute-start.24 = (f32[128,128]{1,0:T(8,128)S(1)}, f32[128,128]{1,0:T(8,128)S(1)}, u32[]{:S(2)}, u32[]{:S(2)}) collective-permute-start(f32[128,128]{1,0:T(8,128)S(1)} %bitcast.27), channel_id=1, source_target_pairs={{0,1},{1,0},{2,3},{3,2},{4,5},{5,4},{6,7},{7,6},{8,9},{9,8},{10,11... | collective-permute-start | bytes 196616 | tf_op jit(solution)/shard_map/ppermute | solution.py:195
  77.0 0.7 collective-permute-start.25
  77.7 1.7 %collective-permute-start.26 = (f32[128,128]{1,0:T(8,128)S(1)}, f32[128,128]{1,0:T(8,128)S(1)}, u32[]{:S(2)}, u32[]{:S(2)}) collective-permute-start(f32[128,128]{1,0:T(8,128)S(1)} %bitcast.29), channel_id=1, source_target_pairs={{0,3},{1,2},{2,1},{3,0},{4,7},{5,6},{6,5},{7,4},{8,11},{9,10},{10,... | collective-permute-start | bytes 196616 | tf_op jit(solution)/shard_map/ppermute | solution.py:195
  79.9 5.6 %collective-permute-done.25.i2 = f32[128,128]{1,0:T(8,128)S(1)} collective-permute-done((f32[128,128]{1,0:T(8,128)S(1)}, f32[128,128]{1,0:T(8,128)S(1)}, u32[]{:S(2)}, u32[]{:S(2)}) %collective-permute-start.25) | collective-permute-done | bytes 65568 | tf_op jit(solution)/shard_map/ppermute | solution.py:195
  85.5 1.4 %shard_map.85 = (bf16[4,32,512]{2,1,0:T(8,128)(2,1)S(1)}, f32[4,32,512]{2,1,0:T(8,128)S(1)}, bf16[4,32,512]{2,1,0:T(8,128)(2,1)S(1)}, bf16[4,32,512]{2,1,0:T(8,128)(2,1)S(1)}, bf16[4,32,512]{2,1,0:T(8,128)(2,1)S(1)}) custom-call(bf16[128,512]{1,0:T(8,128)(2,1)S(1)} %shard_map.83.s0, bf16[128,512]{1,0:T(8,128)(2,1)S(1)} %collective-permute-done.21.s1, ...), custom_call_target="tpu_custom_call" | custom-call | tf_op jit(solution)/shard_map/pallas_call | solution.py:25
  86.9 1.4 %collective-permute-start.28 = (bf16[4,32,512]{2,1,0:T(8,128)(2,1)S(1)}, bf16[4,32,512]{2,1,0:T(8,128)(2,1)S(1)}, u32[]{:S(2)}, u32[]{:S(2)}) collective-permute-start(bf16[4,32,512]{2,1,0:T(8,128)(2,1)S(1)} %get-tuple-element.51), channel_id=1, source_target_pairs={{0,1},{1,0},{2,3},{3,2},{4,5},{5,4},{6,7},{7,6},{8,9},{9,8},{10,11... | collective-permute-start | bytes 393224 | tf_op jit(solution)/shard_map/ppermute | solution.py:195
  88.4 1.1 collective-permute-start.29
  89.5 1.9 %collective-permute-start.30 = (bf16[4,32,512]{2,1,0:T(8,128)(2,1)S(1)}, bf16[4,32,512]{2,1,0:T(8,128)(2,1)S(1)}, u32[]{:S(2)}, u32[]{:S(2)}) collective-permute-start(bf16[4,32,512]{2,1,0:T(8,128)(2,1)S(1)} %get-tuple-element.53), channel_id=1, source_target_pairs={{0,3},{1,2},{2,1},{3,0},{4,7},{5,6},{6,5},{7,4},{8,11},{9,10},{10,... | collective-permute-start | bytes 393224 | tf_op jit(solution)/shard_map/ppermute | solution.py:195
  91.4 3.6 %collective-permute-start.7 = (bf16[4,32,512]{2,1,0:T(8,128)(2,1)S(1)}, bf16[4,32,512]{2,1,0:T(8,128)(2,1)S(1)}, u32[]{:S(2)}, u32[]{:S(2)}) collective-permute-start(bf16[4,32,512]{2,1,0:T(8,128)(2,1)S(1)} %get-tuple-element.32), channel_id=1, source_target_pairs={{0,0},{1,4},{2,8},{3,12},{4,1},{5,5},{6,9},{7,13},{8,2},{9,6},{10,... | collective-permute-start | bytes 393224 | tf_op jit(solution)/shard_map/ppermute | solution.py:271
  95.0 4.0 %collective-permute-start.17 = (bf16[4,32,512]{2,1,0:T(8,128)(2,1)S(1)}, bf16[4,32,512]{2,1,0:T(8,128)(2,1)S(1)}, u32[]{:S(2)}, u32[]{:S(2)}) collective-permute-start(bf16[4,32,512]{2,1,0:T(8,128)(2,1)S(1)} %get-tuple-element.42), channel_id=1, source_target_pairs={{0,0},{1,4},{2,8},{3,12},{4,1},{5,5},{6,9},{7,13},{8,2},{9,6},{10,... | collective-permute-start | bytes 393224 | tf_op jit(solution)/shard_map/ppermute | solution.py:286
  99.0 3.7 %collective-permute-start.27 = (bf16[4,32,512]{2,1,0:T(8,128)(2,1)S(1)}, bf16[4,32,512]{2,1,0:T(8,128)(2,1)S(1)}, u32[]{:S(2)}, u32[]{:S(2)}) collective-permute-start(bf16[4,32,512]{2,1,0:T(8,128)(2,1)S(1)} %get-tuple-element.49), channel_id=1, source_target_pairs={{0,0},{1,4},{2,8},{3,12},{4,1},{5,5},{6,9},{7,13},{8,2},{9,6},{10,... | collective-permute-start | bytes 393224 | tf_op jit(solution)/shard_map/ppermute | solution.py:299
  102.7 0.8 shard_map.86
  103.5 11.3 %all-to-all-start = ((bf16[8,32,512]{2,1,0:T(8,128)(2,1)}), bf16[8,32,512]{2,1,0:T(8,128)(2,1)S(1)}, u32[]{:S(2)}, u32[]{:S(2)}) async-start(bf16[8,32,512]{2,1,0:T(8,128)(2,1)} %bitcast.14), calls=%async_computation | async-start | bytes 524288 | tf_op jit(solution)/shard_map/all_to_all | solution.py:304
  114.7 1.0 collective-permute-done.7
  115.7 2.7 %collective-permute-done.17 = bf16[4,32,512]{2,1,0:T(8,128)(2,1)S(1)} collective-permute-done((bf16[4,32,512]{2,1,0:T(8,128)(2,1)S(1)}, bf16[4,32,512]{2,1,0:T(8,128)(2,1)S(1)}, u32[]{:S(2)}, u32[]{:S(2)}) %collective-permute-start.17) | collective-permute-done | bytes 131104 | tf_op jit(solution)/shard_map/ppermute | solution.py:286
  118.5 1.4 %collective-permute-done.27 = bf16[4,32,512]{2,1,0:T(8,128)(2,1)S(1)} collective-permute-done((bf16[4,32,512]{2,1,0:T(8,128)(2,1)S(1)}, bf16[4,32,512]{2,1,0:T(8,128)(2,1)S(1)}, u32[]{:S(2)}, u32[]{:S(2)}) %collective-permute-start.27) | collective-permute-done | bytes 131104 | tf_op jit(solution)/shard_map/ppermute | solution.py:299
  119.9 0.8 pad_maximum_fusion
  120.6 1.1 all-to-all-done
  121.7 0.7 shard_map.87
  (43 shorter events, 2.6 us)
Async XLA Ops:
  1.5 12.4 %collective-permute-start = (bf16[4,32,512]{2,1,0:T(8,128)(2,1)S(1)}, bf16[4,32,512]{2,1,0:T(8,128)(2,1)S(1)}, u32[]{:S(2)}, u32[]{:S(2)}) collective-permute-start(bf16[4,32,512]{2,1,0:T(8,128)(2,1)S(1)} %bitcast.33), channel_id=1, source_target_pairs={{0,0},{1,4},{2,8},{3,12},{4,1},{5,5},{6,9},{7,13},{8,2},{9,6},{10,... | collective-permute-start | bytes 393224 | tf_op jit(solution)/shard_map/ppermute | solution.py:218
  14.0 5.0 %collective-permute-start.2 = (bf16[4,32,512]{2,1,0:T(8,128)(2,1)S(1)}, bf16[4,32,512]{2,1,0:T(8,128)(2,1)S(1)}, u32[]{:S(2)}, u32[]{:S(2)}) collective-permute-start(bf16[4,32,512]{2,1,0:T(8,128)(2,1)S(1)} %collective-permute-done.g0), channel_id=1, source_target_pairs={{0,8},{4,12},{8,0},{12,4},{1,9},{5,13},{9,1},{13,5},{2,10},{6,14},... | collective-permute-start | bytes 393224 | tf_op jit(solution)/shard_map/ppermute | solution.py:195
  14.0 14.4 %collective-permute-start.1 = (bf16[4,32,512]{2,1,0:T(8,128)(2,1)S(1)}, bf16[4,32,512]{2,1,0:T(8,128)(2,1)S(1)}, u32[]{:S(2)}, u32[]{:S(2)}) collective-permute-start(bf16[4,32,512]{2,1,0:T(8,128)(2,1)S(1)} %collective-permute-done.g0), channel_id=1, source_target_pairs={{0,4},{4,0},{8,12},{12,8},{1,5},{5,1},{9,13},{13,9},{2,6},{6,2},{1... | collective-permute-start | bytes 393224 | tf_op jit(solution)/shard_map/ppermute | solution.py:195
  18.9 9.5 %collective-permute-start.3 = (bf16[4,32,512]{2,1,0:T(8,128)(2,1)S(1)}, bf16[4,32,512]{2,1,0:T(8,128)(2,1)S(1)}, u32[]{:S(2)}, u32[]{:S(2)}) collective-permute-start(bf16[4,32,512]{2,1,0:T(8,128)(2,1)S(1)} %collective-permute-done.2.g2), channel_id=1, source_target_pairs={{0,4},{4,0},{8,12},{12,8},{1,5},{5,1},{9,13},{13,9},{2,6},{6,2},{1... | collective-permute-start | bytes 393224 | tf_op jit(solution)/shard_map/ppermute | solution.py:195
  19.9 1.0 copy-start
  20.9 0.9 copy-start.3
  21.8 6.4 %collective-permute-start.4 = (bf16[96,512]{1,0:T(8,128)(2,1)S(1)}, bf16[96,512]{1,0:T(8,128)(2,1)S(1)}, u32[]{:S(2)}, u32[]{:S(2)}) collective-permute-start(bf16[96,512]{1,0:T(8,128)(2,1)S(1)} %get-tuple-element.29), channel_id=1, source_target_pairs={{0,4},{4,0},{8,12},{12,8},{1,5},{5,1},{9,13},{13,9},{2,6},{6,2},{1... | collective-permute-start | bytes 294920 | tf_op jit(solution)/shard_map/ppermute | solution.py:195
  22.4 5.9 %collective-permute-start.5 = (bf16[96,512]{1,0:T(8,128)(2,1)S(1)}, bf16[96,512]{1,0:T(8,128)(2,1)S(1)}, u32[]{:S(2)}, u32[]{:S(2)}) collective-permute-start(bf16[96,512]{1,0:T(8,128)(2,1)S(1)} %get-tuple-element.30), channel_id=1, source_target_pairs={{0,8},{4,12},{8,0},{12,4},{1,9},{5,13},{9,1},{13,5},{2,10},{6,14},... | collective-permute-start | bytes 294920 | tf_op jit(solution)/shard_map/ppermute | solution.py:195
  22.4 6.0 %collective-permute-start.6 = (bf16[96,512]{1,0:T(8,128)(2,1)S(1)}, bf16[96,512]{1,0:T(8,128)(2,1)S(1)}, u32[]{:S(2)}, u32[]{:S(2)}) collective-permute-start(bf16[96,512]{1,0:T(8,128)(2,1)S(1)} %get-tuple-element.31), channel_id=1, source_target_pairs={{0,12},{4,8},{8,4},{12,0},{1,13},{5,9},{9,5},{13,1},{2,14},{6,10},... | collective-permute-start | bytes 294920 | tf_op jit(solution)/shard_map/ppermute | solution.py:195
  24.6 1.9 %copy-start.2 = (bf16[1,6,1,1,4,4,128,128]{7,6,5,4,3,2,1,0:T(8,128)(2,1)S(1)}, bf16[1,6,1,1,4,4,128,128]{7,6,5,4,3,2,1,0:T(8,128)(2,1)}, u32[]{:S(2)}) copy-start(bf16[1,6,1,1,4,4,128,128]{7,6,5,4,3,2,1,0:T(8,128)(2,1)} %param.8) | copy-start | bytes 9437188
  26.5 1.9 %copy-start.1 = (bf16[1,384,512]{2,1,0:T(8,128)(2,1)S(1)}, bf16[1,384,512]{2,1,0:T(8,128)(2,1)}, u32[]{:S(2)}) copy-start(bf16[1,384,512]{2,1,0:T(8,128)(2,1)} %param.6) | copy-start | bytes 1179652
  28.2 26.1 %copy-start.4 = (bf16[128,512]{1,0:T(8,128)(2,1)S(1)}, bf16[128,512]{1,0:T(8,128)(2,1)}, u32[]{:S(2)}) copy-start(bf16[128,512]{1,0:T(8,128)(2,1)} %param.7) | copy-start | bytes 393220
  29.2 8.3 %collective-permute-start.10 = (bf16[128,512]{1,0:T(8,128)(2,1)S(1)}, bf16[128,512]{1,0:T(8,128)(2,1)S(1)}, u32[]{:S(2)}, u32[]{:S(2)}) collective-permute-start(bf16[128,512]{1,0:T(8,128)(2,1)S(1)} %get-tuple-element.36), channel_id=1, source_target_pairs={{0,3},{1,2},{2,1},{3,0},{4,7},{5,6},{6,5},{7,4},{8,11},{9,10},{10,... | collective-permute-start | bytes 393224 | tf_op jit(solution)/shard_map/ppermute | solution.py:195
  31.5 10.4 %collective-permute-start.8 = (bf16[128,512]{1,0:T(8,128)(2,1)S(1)}, bf16[128,512]{1,0:T(8,128)(2,1)S(1)}, u32[]{:S(2)}, u32[]{:S(2)}) collective-permute-start(bf16[128,512]{1,0:T(8,128)(2,1)S(1)} %get-tuple-element.34), channel_id=1, source_target_pairs={{0,1},{1,0},{2,3},{3,2},{4,5},{5,4},{6,7},{7,6},{8,9},{9,8},{10,11... | collective-permute-start | bytes 393224 | tf_op jit(solution)/shard_map/ppermute | solution.py:195
  31.5 11.9 %collective-permute-start.9 = (bf16[128,512]{1,0:T(8,128)(2,1)S(1)}, bf16[128,512]{1,0:T(8,128)(2,1)S(1)}, u32[]{:S(2)}, u32[]{:S(2)}) collective-permute-start(bf16[128,512]{1,0:T(8,128)(2,1)S(1)} %get-tuple-element.35), channel_id=1, source_target_pairs={{0,2},{1,3},{2,0},{3,1},{4,6},{5,7},{6,4},{7,5},{8,10},{9,11},{10,... | collective-permute-start | bytes 393224 | tf_op jit(solution)/shard_map/ppermute | solution.py:195
  43.8 5.3 %collective-permute-start.12 = (bf16[128,512]{1,0:T(8,128)(2,1)S(1)}, bf16[128,512]{1,0:T(8,128)(2,1)S(1)}, u32[]{:S(2)}, u32[]{:S(2)}) collective-permute-start(bf16[128,512]{1,0:T(8,128)(2,1)S(1)} %shard_map.80.s0), channel_id=1, source_target_pairs={{0,8},{4,12},{8,0},{12,4},{1,9},{5,13},{9,1},{13,5},{2,10},{6,14},... | collective-permute-start | bytes 393224 | tf_op jit(solution)/shard_map/ppermute | solution.py:195
  44.4 10.8 %collective-permute-start.11 = (bf16[128,512]{1,0:T(8,128)(2,1)S(1)}, bf16[128,512]{1,0:T(8,128)(2,1)S(1)}, u32[]{:S(2)}, u32[]{:S(2)}) collective-permute-start(bf16[128,512]{1,0:T(8,128)(2,1)S(1)} %shard_map.80.s0), channel_id=1, source_target_pairs={{0,4},{4,0},{8,12},{12,8},{1,5},{5,1},{9,13},{13,9},{2,6},{6,2},{1... | collective-permute-start | bytes 393224 | tf_op jit(solution)/shard_map/ppermute | solution.py:195
  49.1 6.1 %collective-permute-start.13 = (bf16[128,512]{1,0:T(8,128)(2,1)S(1)}, bf16[128,512]{1,0:T(8,128)(2,1)S(1)}, u32[]{:S(2)}, u32[]{:S(2)}) collective-permute-start(bf16[128,512]{1,0:T(8,128)(2,1)S(1)} %collective-permute-done.12.s2), channel_id=1, source_target_pairs={{0,4},{4,0},{8,12},{12,8},{1,5},{5,1},{9,13},{13,9},{2,6},{6,2},{1... | collective-permute-start | bytes 393224 | tf_op jit(solution)/shard_map/ppermute | solution.py:195
  49.1 1.9 %collective-permute-start.14 = (bf16[2,32,512]{2,1,0:T(8,128)(2,1)S(1)}, bf16[2,32,512]{2,1,0:T(8,128)(2,1)S(1)}, u32[]{:S(2)}, u32[]{:S(2)}) collective-permute-start(bf16[2,32,512]{2,1,0:T(8,128)(2,1)S(1)} %get-tuple-element.38), channel_id=1, source_target_pairs={{0,4},{4,0},{8,12},{12,8},{1,5},{5,1},{9,13},{13,9},{2,6},{6,2},{1... | collective-permute-start | bytes 196616 | tf_op jit(solution)/shard_map/ppermute | solution.py:195
  49.6 4.7 %collective-permute-start.15 = (bf16[2,32,512]{2,1,0:T(8,128)(2,1)S(1)}, bf16[2,32,512]{2,1,0:T(8,128)(2,1)S(1)}, u32[]{:S(2)}, u32[]{:S(2)}) collective-permute-start(bf16[2,32,512]{2,1,0:T(8,128)(2,1)S(1)} %get-tuple-element.39), channel_id=1, source_target_pairs={{0,8},{4,12},{8,0},{12,4},{1,9},{5,13},{9,1},{13,5},{2,10},{6,14},... | collective-permute-start | bytes 196616 | tf_op jit(solution)/shard_map/ppermute | solution.py:195
  49.9 4.4 %collective-permute-start.16 = (bf16[2,32,512]{2,1,0:T(8,128)(2,1)S(1)}, bf16[2,32,512]{2,1,0:T(8,128)(2,1)S(1)}, u32[]{:S(2)}, u32[]{:S(2)}) collective-permute-start(bf16[2,32,512]{2,1,0:T(8,128)(2,1)S(1)} %get-tuple-element.40), channel_id=1, source_target_pairs={{0,12},{4,8},{8,4},{12,0},{1,13},{5,9},{9,5},{13,1},{2,14},{6,10},... | collective-permute-start | bytes 196616 | tf_op jit(solution)/shard_map/ppermute | solution.py:195
  55.2 19.0 %copy-start.5 = (f32[1,1,128,128]{3,2,1,0:T(8,128)S(1)}, f32[1,1,128,128]{3,2,1,0:T(8,128)}, u32[]{:S(2)}) copy-start(f32[1,1,128,128]{3,2,1,0:T(8,128)} %param.11) | copy-start | bytes 196612
  55.7 8.2 %collective-permute-start.18 = (bf16[128,512]{1,0:T(8,128)(2,1)S(1)}, bf16[128,512]{1,0:T(8,128)(2,1)S(1)}, u32[]{:S(2)}, u32[]{:S(2)}) collective-permute-start(bf16[128,512]{1,0:T(8,128)(2,1)S(1)} %get-tuple-element.44), channel_id=1, source_target_pairs={{0,1},{1,0},{2,3},{3,2},{4,5},{5,4},{6,7},{7,6},{8,9},{9,8},{10,11... | collective-permute-start | bytes 393224 | tf_op jit(solution)/shard_map/ppermute | solution.py:195
  55.7 13.1 %collective-permute-start.19 = (bf16[128,512]{1,0:T(8,128)(2,1)S(1)}, bf16[128,512]{1,0:T(8,128)(2,1)S(1)}, u32[]{:S(2)}, u32[]{:S(2)}) collective-permute-start(bf16[128,512]{1,0:T(8,128)(2,1)S(1)} %get-tuple-element.45), channel_id=1, source_target_pairs={{0,2},{1,3},{2,0},{3,1},{4,6},{5,7},{6,4},{7,5},{8,10},{9,11},{10,... | collective-permute-start | bytes 393224 | tf_op jit(solution)/shard_map/ppermute | solution.py:195
  58.9 10.0 %collective-permute-start.20 = (bf16[128,512]{1,0:T(8,128)(2,1)S(1)}, bf16[128,512]{1,0:T(8,128)(2,1)S(1)}, u32[]{:S(2)}, u32[]{:S(2)}) collective-permute-start(bf16[128,512]{1,0:T(8,128)(2,1)S(1)} %get-tuple-element.46), channel_id=1, source_target_pairs={{0,3},{1,2},{2,1},{3,0},{4,7},{5,6},{6,5},{7,4},{8,11},{9,10},{10,... | collective-permute-start | bytes 393224 | tf_op jit(solution)/shard_map/ppermute | solution.py:195
  69.2 5.0 %collective-permute-start.22 = (bf16[128,512]{1,0:T(8,128)(2,1)S(1)}, bf16[128,512]{1,0:T(8,128)(2,1)S(1)}, u32[]{:S(2)}, u32[]{:S(2)}) collective-permute-start(bf16[128,512]{1,0:T(8,128)(2,1)S(1)} %shard_map.83.s0), channel_id=1, source_target_pairs={{0,8},{4,12},{8,0},{12,4},{1,9},{5,13},{9,1},{13,5},{2,10},{6,14},... | collective-permute-start | bytes 393224 | tf_op jit(solution)/shard_map/ppermute | solution.py:195
  70.7 14.8 %collective-permute-start.21 = (bf16[128,512]{1,0:T(8,128)(2,1)S(1)}, bf16[128,512]{1,0:T(8,128)(2,1)S(1)}, u32[]{:S(2)}, u32[]{:S(2)}) collective-permute-start(bf16[128,512]{1,0:T(8,128)(2,1)S(1)} %shard_map.83.s0), channel_id=1, source_target_pairs={{0,4},{4,0},{8,12},{12,8},{1,5},{5,1},{9,13},{13,9},{2,6},{6,2},{1... | collective-permute-start | bytes 393224 | tf_op jit(solution)/shard_map/ppermute | solution.py:195
  74.2 11.3 %collective-permute-start.23 = (bf16[128,512]{1,0:T(8,128)(2,1)S(1)}, bf16[128,512]{1,0:T(8,128)(2,1)S(1)}, u32[]{:S(2)}, u32[]{:S(2)}) collective-permute-start(bf16[128,512]{1,0:T(8,128)(2,1)S(1)} %collective-permute-done.22.s2), channel_id=1, source_target_pairs={{0,4},{4,0},{8,12},{12,8},{1,5},{5,1},{9,13},{13,9},{2,6},{6,2},{1... | collective-permute-start | bytes 393224 | tf_op jit(solution)/shard_map/ppermute | solution.py:195
  74.2 5.7 %collective-permute-start.24 = (f32[128,128]{1,0:T(8,128)S(1)}, f32[128,128]{1,0:T(8,128)S(1)}, u32[]{:S(2)}, u32[]{:S(2)}) collective-permute-start(f32[128,128]{1,0:T(8,128)S(1)} %bitcast.27), channel_id=1, source_target_pairs={{0,1},{1,0},{2,3},{3,2},{4,5},{5,4},{6,7},{7,6},{8,9},{9,8},{10,11... | collective-permute-start | bytes 196616 | tf_op jit(solution)/shard_map/ppermute | solution.py:195
  77.0 8.5 %collective-permute-start.25 = (f32[128,128]{1,0:T(8,128)S(1)}, f32[128,128]{1,0:T(8,128)S(1)}, u32[]{:S(2)}, u32[]{:S(2)}) collective-permute-start(f32[128,128]{1,0:T(8,128)S(1)} %bitcast.28), channel_id=1, source_target_pairs={{0,2},{1,3},{2,0},{3,1},{4,6},{5,7},{6,4},{7,5},{8,10},{9,11},{10,... | collective-permute-start | bytes 196616 | tf_op jit(solution)/shard_map/ppermute | solution.py:195
  77.7 7.8 %collective-permute-start.26 = (f32[128,128]{1,0:T(8,128)S(1)}, f32[128,128]{1,0:T(8,128)S(1)}, u32[]{:S(2)}, u32[]{:S(2)}) collective-permute-start(f32[128,128]{1,0:T(8,128)S(1)} %bitcast.29), channel_id=1, source_target_pairs={{0,3},{1,2},{2,1},{3,0},{4,7},{5,6},{6,5},{7,4},{8,11},{9,10},{10,... | collective-permute-start | bytes 196616 | tf_op jit(solution)/shard_map/ppermute | solution.py:195
  86.9 12.1 %collective-permute-start.28 = (bf16[4,32,512]{2,1,0:T(8,128)(2,1)S(1)}, bf16[4,32,512]{2,1,0:T(8,128)(2,1)S(1)}, u32[]{:S(2)}, u32[]{:S(2)}) collective-permute-start(bf16[4,32,512]{2,1,0:T(8,128)(2,1)S(1)} %get-tuple-element.51), channel_id=1, source_target_pairs={{0,1},{1,0},{2,3},{3,2},{4,5},{5,4},{6,7},{7,6},{8,9},{9,8},{10,11... | collective-permute-start | bytes 393224 | tf_op jit(solution)/shard_map/ppermute | solution.py:195
  88.4 14.3 %collective-permute-start.29 = (bf16[4,32,512]{2,1,0:T(8,128)(2,1)S(1)}, bf16[4,32,512]{2,1,0:T(8,128)(2,1)S(1)}, u32[]{:S(2)}, u32[]{:S(2)}) collective-permute-start(bf16[4,32,512]{2,1,0:T(8,128)(2,1)S(1)} %get-tuple-element.52), channel_id=1, source_target_pairs={{0,2},{1,3},{2,0},{3,1},{4,6},{5,7},{6,4},{7,5},{8,10},{9,11},{10,... | collective-permute-start | bytes 393224 | tf_op jit(solution)/shard_map/ppermute | solution.py:195
  89.5 13.2 %collective-permute-start.30 = (bf16[4,32,512]{2,1,0:T(8,128)(2,1)S(1)}, bf16[4,32,512]{2,1,0:T(8,128)(2,1)S(1)}, u32[]{:S(2)}, u32[]{:S(2)}) collective-permute-start(bf16[4,32,512]{2,1,0:T(8,128)(2,1)S(1)} %get-tuple-element.53), channel_id=1, source_target_pairs={{0,3},{1,2},{2,1},{3,0},{4,7},{5,6},{6,5},{7,4},{8,11},{9,10},{10,... | collective-permute-start | bytes 393224 | tf_op jit(solution)/shard_map/ppermute | solution.py:195
  91.4 24.4 %collective-permute-start.7 = (bf16[4,32,512]{2,1,0:T(8,128)(2,1)S(1)}, bf16[4,32,512]{2,1,0:T(8,128)(2,1)S(1)}, u32[]{:S(2)}, u32[]{:S(2)}) collective-permute-start(bf16[4,32,512]{2,1,0:T(8,128)(2,1)S(1)} %get-tuple-element.32), channel_id=1, source_target_pairs={{0,0},{1,4},{2,8},{3,12},{4,1},{5,5},{6,9},{7,13},{8,2},{9,6},{10,... | collective-permute-start | bytes 393224 | tf_op jit(solution)/shard_map/ppermute | solution.py:271
  95.0 23.4 %collective-permute-start.17 = (bf16[4,32,512]{2,1,0:T(8,128)(2,1)S(1)}, bf16[4,32,512]{2,1,0:T(8,128)(2,1)S(1)}, u32[]{:S(2)}, u32[]{:S(2)}) collective-permute-start(bf16[4,32,512]{2,1,0:T(8,128)(2,1)S(1)} %get-tuple-element.42), channel_id=1, source_target_pairs={{0,0},{1,4},{2,8},{3,12},{4,1},{5,5},{6,9},{7,13},{8,2},{9,6},{10,... | collective-permute-start | bytes 393224 | tf_op jit(solution)/shard_map/ppermute | solution.py:286
  99.0 20.8 %collective-permute-start.27 = (bf16[4,32,512]{2,1,0:T(8,128)(2,1)S(1)}, bf16[4,32,512]{2,1,0:T(8,128)(2,1)S(1)}, u32[]{:S(2)}, u32[]{:S(2)}) collective-permute-start(bf16[4,32,512]{2,1,0:T(8,128)(2,1)S(1)} %get-tuple-element.49), channel_id=1, source_target_pairs={{0,0},{1,4},{2,8},{3,12},{4,1},{5,5},{6,9},{7,13},{8,2},{9,6},{10,... | collective-permute-start | bytes 393224 | tf_op jit(solution)/shard_map/ppermute | solution.py:299
  103.5 18.3 %all-to-all-start = ((bf16[8,32,512]{2,1,0:T(8,128)(2,1)}), bf16[8,32,512]{2,1,0:T(8,128)(2,1)S(1)}, u32[]{:S(2)}, u32[]{:S(2)}) async-start(bf16[8,32,512]{2,1,0:T(8,128)(2,1)} %bitcast.14), calls=%async_computation | async-start | bytes 524288 | tf_op jit(solution)/shard_map/all_to_all | solution.py:304

commit v2 on v0

v2 whole, which is shorter than its diff:
```python
import functools

import jax
import jax.numpy as jnp
from jax import lax
from jax.experimental import pallas as pl
from jax.experimental.pallas import tpu as pltpu
from jax.sharding import PartitionSpec as P

F32 = jnp.float32
BF16 = jnp.bfloat16
VMEM = pltpu.VMEM
MIB = 1024 * 1024
PAIR = {(0, 1): 0, (0, 2): 1, (0, 3): 2, (1, 2): 3, (1, 3): 4, (2, 3): 5}


def whole(count):
    return [pl.BlockSpec(memory_space=VMEM)] * count


def call(kernel, outs, *args, scratch=(), in_specs=None, grid=None, limit=32):
    extra = {}
    if grid is not None:
        extra["grid"] = grid
    return pl.pallas_call(
        kernel,
        out_shape=[jax.ShapeDtypeStruct(shape, dtype) for shape, dtype in outs],
        in_specs=whole(len(args)) if in_specs is None else in_specs,
        out_specs=whole(len(outs)),
        scratch_shapes=list(scratch),
        compiler_params=pltpu.CompilerParams(vmem_limit_bytes=limit * MIB),
        **extra,
    )(*args)


def dot(left, right):
    return jnp.dot(left, right, preferred_element_type=F32)


def split(value):
    high = value.astype(BF16)
    return high, (value - high.astype(F32)).astype(BF16)


def precise(inverse, value):
    ih, il = split(inverse)
    vh, vl = split(value)
    return dot(
        jnp.concatenate([ih, ih, il], axis=1), jnp.concatenate([vh, vl, vh], axis=0)
    )


def crossed(index):
    return 2 * (index % 2) + index // 2


def pack_kernel(forest, root, first, last, side, *rest):
    own, near, far, *late, halved = rest[:8]
    held, top, inverse, final, sems = rest[8:]
    a = lax.axis_index("prow")
    half = inverse.shape[0] // 2
    chunks, cols = side.shape[0], side.shape[-1]
    moves = [
        pltpu.make_async_copy(forest, held, sems.at[0]),
        pltpu.make_async_copy(root, top, sems.at[1]),
        pltpu.make_async_copy(first.at[0], inverse, sems.at[2]),
        pltpu.make_async_copy(
            last.at[pl.ds(lax.axis_index("layer") % 2 * half, half)], final, sems.at[3]
        ),
    ]
    for move in moves:
        move.start()
    moves[0].wait()
    for h in range(chunks):
        side[h] = held[0, :, :, h * cols : (h + 1) * cols]
    moves[2].wait()
    high, low = split(inverse[...])
    packed = jnp.concatenate([high[:half], high[half:], low[:half], low[half:]], axis=1)
    part = held.shape[2]
    for out, slots in ((own, (0,)), (near, (1,)), (far, (2, 3))):
        out[:half] = packed
        for i, k in enumerate(slots):
            out[half + i * part : half + (i + 1) * part] = held[1, a ^ k]
    moves[1].wait()
    for k, out in enumerate(late):
        out[0] = held[2, a ^ k]
        out[1] = top[a ^ k]
    moves[3].wait()
    high, low = split(final[...])
    quarter = half // 2
    halved[...] = jnp.concatenate(
        [high[:quarter], high[quarter:], low[:quarter], low[quarter:]], axis=1
    )


def masked_pair(n, pattern, blocks, out):
    a, b = lax.axis_index("prow"), lax.axis_index("pcol")
    size = blocks.shape[-1]
    for j in range(4):
        for k in range(4):
            block = blocks[b ^ j, a ^ k]
            out[j, :, k * size : (k + 1) * size] = jnp.where(
                pattern[n, b ^ j, a ^ k] != 0, block, jnp.zeros_like(block)
            )


def mask_kernel(pattern, blocks, out, held, sems):
    pairs = out.shape[0]
    moves = [
        pltpu.make_async_copy(blocks.at[n], held.at[n], sems.at[n])
        for n in range(pairs)
    ]
    for move in moves:
        move.start()
    for n, move in enumerate(moves):
        move.wait()
        masked_pair(n, pattern, held.at[n], out.at[n])


def send_sums(acc, weights, solved, outs):
    for j, out in enumerate(outs):
        value = acc(j) - dot(weights[0, j], solved[...])
        out[: value.shape[0]] = value.astype(out.dtype)


def first_kernel(h, g0, g1, g2, g3, m0, m1, m2, m3, halved, weights, *rest):
    solved, *outs, rows, acc = rest
    a, b = lax.axis_index("prow"), lax.axis_index("pcol")
    part, cols = g0.shape[-2:]
    size = 4 * part
    half = size // 2
    for j, piece in enumerate((g0, g1, g2, g3)):
        place = pl.ds(pl.multiple_of((a ^ j) * part, part), part)
        for u in range(4):
            rows[u, place, :] = piece[u]
    acc[...] = jnp.zeros_like(acc)
    place = pl.ds(pl.multiple_of(b * part, part), part)
    for j, message in enumerate((m0, m1, m2, m3)):
        value = message[:half]
        high = jnp.concatenate([value[:, :size], value[:, size : 2 * size]], axis=0)
        low = jnp.concatenate(
            [value[:, 2 * size : 3 * size], value[:, 3 * size : 4 * size]], axis=0
        )
        right = rows[a ^ j]
        answer = dot(
            jnp.concatenate([high, low], axis=1),
            jnp.concatenate([right, right], axis=0),
        )
        solved[j * size : (j + 1) * size] = answer.astype(BF16)
        value = message[message.shape[0] - part :, h * cols : (h + 1) * cols]
        if j == 2:
            value = message[half : half + part, h * cols : (h + 1) * cols]
        acc[a ^ b ^ j, place, :] = value.astype(F32)
    send_sums(lambda j: acc[j], weights, solved, outs)
    if h == 0:
        for out in outs[1:]:
            out[size:] = halved[...]


def solve_kernel(own, r1, r2, r3, inverse, out):
    value = own[...]
    for other in (r1, r2, r3):
        value += other[: value.shape[0]].astype(F32)
    out[...] = precise(inverse[...], value).astype(out.dtype)


def middle_kernel(h, s0, s1, s2, s3, weights, acc, solved, *outs):
    size, cols = s0.shape
    for j, piece in enumerate((s0, s1, s2, s3)):
        solved[j * size : (j + 1) * size] = piece[...]
    here = slice(h * cols, (h + 1) * cols)
    send_sums(lambda j: acc[j, :, here], weights, solved, outs)


def turn_rows(solved, here, turned):
    a = lax.axis_index("prow")
    part = turned.shape[1]
    for j in range(4):
        start = 4 * part * j + crossed(a) * part
        place = pl.ds(pl.multiple_of(start, part), part)
        turned[a ^ j, :, here] = solved[place]


def early_kernel(chunks, *refs):
    solved, (w2, w3, c0, c1, c2, c3) = refs[:chunks], refs[chunks : chunks + 6]
    acc2, acc3, turned = refs[chunks + 6 :]
    a, b = lax.axis_index("prow"), lax.axis_index("pcol")
    part = c0.shape[1]
    cols = solved[0].shape[1]
    place = pl.ds(pl.multiple_of(b * part, part), part)
    top = (lax.axis_index("layer") == 0).astype(F32)
    acc2[...] = jnp.zeros_like(acc2)
    acc3[...] = jnp.zeros_like(acc3)
    for k, piece in enumerate((c0, c1, c2, c3)):
        acc2[a ^ b ^ k, place, :] = piece[0].astype(F32)
        acc3[a ^ b ^ k, place, :] = piece[1].astype(F32) * top
    for h in range(chunks):
        here = slice(h * cols, (h + 1) * cols)
        turn_rows(solved[h], here, turned)
        for j in range(4):
            acc2[j, :, here] -= dot(w2[0, j], solved[h][...])
            acc3[j, :, here] -= dot(w3[0, j], solved[h][...])


def later_kernel(chunks, *refs):
    solved, (weights, acc, out, turned) = refs[:chunks], refs[chunks:]
    cols = solved[0].shape[1]
    for h in range(chunks):
        here = slice(h * cols, (h + 1) * cols)
        turn_rows(solved[h], here, turned)
        for j in range(4):
            out[j, :, here] = acc[j, :, here] - dot(weights[0, j], solved[h][...])


def root_kernel(h, s0, s1, s2, s3, weights, acc, mine, theirs, *rest):
    turned, *outs, solved, full = rest
    b = lax.axis_index("pcol")
    size, cols = s0.shape
    part = size // 4
    for j, piece in enumerate((s0, s1, s2, s3)):
        solved[j * size : (j + 1) * size] = piece[...]
    turn_rows(solved, slice(None), turned)
    here = slice(h * cols, (h + 1) * cols)
    upper = lax.axis_index("layer") % 2 == 0
    for j in range(4):
        one, two = mine[j], theirs[j]
        inverse = jnp.concatenate(
            [jnp.where(upper, one, two), jnp.where(upper, two, one)], axis=0
        )
        value = acc[j, :, here] - dot(weights[0, j], solved[...])
        full[b ^ j] = precise(inverse, value)
    for j, out in enumerate(outs):
        place = pl.ds(pl.multiple_of((b ^ j) * part, part), part)
        out[...] = full[:, place, :].astype(out.dtype)


def halves_kernel(own, r1, r2, r3, out):
    quarter = own.shape[0]
    size = out.shape[-1]
    for j, ref in enumerate((own, r1, r2, r3)):
        value = ref[ref.shape[0] - quarter :].astype(F32)
        for i in range(2):
            high = value[:, i * size : (i + 1) * size]
            low = value[:, (2 + i) * size : (3 + i) * size]
            out[j, i * quarter : (i + 1) * quarter] = high + low


def turned_kernel(first, second, *rest):
    *third, out = rest
    out[0] = first[...]
    out[1] = second[...]
    cols = third[0].shape[-1]
    for h, piece in enumerate(third):
        out[2, :, :, h * cols : (h + 1) * cols] = piece[...]


def total_kernel(chunks, *refs):
    parts, out = refs[:-1], refs[-1]
    cols = parts[0].shape[-1]
    for h in range(chunks):
        own, *others = parts[4 * h : 4 * h + 4]
        value = own[...]
        for other in others:
            value += other[...].astype(F32)
        for layer in range(out.shape[0]):
            out[layer, :, :, h * cols : (h + 1) * cols] = value.astype(out.dtype)


def join_kernel(pieces, out):
    out[...] = (pieces[0].astype(F32) + pieces[1].astype(F32)).astype(out.dtype)


CHUNKS = 1
LARGE = 60


def shards(subtree_right_hand, root_rhs, blocks, pattern, forest_inverse, root_inverse):
    layers = lax.axis_size("layer")
    size = blocks.shape[-1]
    part, half = size // 4, size // 2
    width = subtree_right_hand.shape[-1]
    cols = width // CHUNKS
    forest = subtree_right_hand.reshape(3, 4, part, width)
    root = root_rhs.reshape(4, part, width)
    blocks = blocks.reshape(6, 4, 4, size, size)
    pattern = pattern.reshape(6, 4, 4)
    inverses = forest_inverse.reshape(3, size, size)
    last_inverse = root_inverse.reshape(size, size)
    both = ("prow", "pcol")
    turn = [(i * 4 + j, j * 4 + i) for i in range(4) for j in range(4)]
    back = [(crossed(i) * 4 + j, j * 4 + i) for i in range(4) for j in range(4)]
    hbm = pl.BlockSpec(memory_space=pltpu.HBM)
    dma = pltpu.SemaphoreType.DMA

    def after(*values):
        return lax.optimization_barrier(values)

    def swap(value, axis, k):
        return lax.ppermute(value, axis, [(i, i ^ k) for i in range(4)])

    def gather(value):
        far = swap(value, "prow", 2)
        return value, swap(value, "prow", 1), far, swap(far, "prow", 1)

    def spread(outs):
        return [swap(out, "pcol", k) for k, out in enumerate(outs[1:], 1)]

    def with_table(kernel, outs, at, pair, *args, scratch=()):
        specs = whole(len(args))
        for index, which in zip(at, pair):
            place = PAIR[which]
            specs[index] = pl.BlockSpec(
                (1, 4, size, 4 * size), lambda i, place=place: (place, 0, 0, 0)
            )
        return call(kernel, outs, *args, scratch=scratch, in_specs=specs, grid=(1,))

    piece = ((4, part, width), BF16)
    partial = [((size, cols), F32)] + [((size, cols), BF16)] * 3
    sums = ((4, size, width), F32)
    tall = ((4 * size, cols), BF16)
    every = range(CHUNKS)
    run = functools.partial

    side, *sends = call(
        pack_kernel,
        [((CHUNKS, 4, part, cols), BF16)]
        + [((half + i * part, width), BF16) for i in (1, 1, 2)]
        + [((2, part, width), BF16)] * 4
        + [((half // 2, width), BF16)],
        forest,
        root,
        inverses,
        last_inverse,
        in_specs=[hbm] * 4,
        limit=LARGE,
        scratch=[
            VMEM((3, 4, part, width), BF16),
            VMEM((4, part, width), BF16),
            VMEM((size, size), F32),
            VMEM((half, size), F32),
            dma((4,)),
        ],
    )
    side = lax.ppermute(side, both, turn)
    far = swap(sends[2], "prow", 2)
    (weights,) = call(
        mask_kernel,
        [((6, 4, size, 4 * size), BF16)],
        pattern,
        blocks,
        in_specs=[pl.BlockSpec(memory_space=pltpu.SMEM), hbm],
        scratch=[VMEM(blocks.shape, BF16), dma((6,))],
    )
    side, far, weights = after(side, far, weights)
    early = [sends[0], swap(sends[1], "prow", 1), far, swap(far, "prow", 1)]

    sides = [gather(side[h]) for h in every]
    longer = [partial[0]] + [((size + half // 2, cols), BF16)] * 3
    solved0, outs, got = {}, {}, {}
    for h in every:
        solved0[h], *outs[h] = with_table(
            run(first_kernel, h),
            [tall] + (longer if h == 0 else partial),
            (9,),
            ((0, 1),),
            *sides[h],
            *early,
            sends[7],
            weights,
            scratch=[VMEM((4, size, cols), BF16), VMEM((4, size, cols), F32)],
        )
        got[h] = spread(outs[h])
    late = after(*sends[4:7], got[0][0])[:3]
    late = [sends[3]] + [swap(late[k - 1], "prow", k) for k in (1, 2, 3)]
    *got[0], late[1], late[2], late[3] = after(*got[0], *late[1:])
    acc2, acc3, turned0 = with_table(
        run(early_kernel, CHUNKS),
        [sums, sums, piece],
        (CHUNKS, CHUNKS + 1),
        ((0, 2), (0, 3)),
        *solved0.values(),
        weights,
        weights,
        *late,
    )
    answers = {}
    for h in every:
        (answers[h],) = call(
            solve_kernel, [((size, cols), BF16)], outs[h][0], *got[h], inverses[1]
        )
    (mine,) = call(halves_kernel, [((4, half, size), F32)], sends[7], *got[0])
    solved1 = {}
    for h in every:
        solved1[h], *outs[h] = with_table(
            run(middle_kernel, h),
            [tall] + partial,
            (4,),
            ((1, 2),),
            *gather(answers[h]),
            weights,
            acc2,
        )
        got[h] = spread(outs[h])
    stacked = after(mine, got[0][0])[0]
    pairs = [(i, i ^ 1) for i in range(layers)]
    theirs = lax.ppermute(stacked, "layer", pairs)
    *got[0], theirs = after(*got[0], theirs)
    acc3, turned1 = with_table(
        run(later_kernel, CHUNKS),
        [sums, piece],
        (CHUNKS,),
        ((1, 3),),
        *solved1.values(),
        weights,
        acc3,
    )
    for h in every:
        (answers[h],) = call(
            solve_kernel, [((size, cols), BF16)], outs[h][0], *got[h], inverses[2]
        )
    turned2 = {}
    for h in every:
        turned2[h], *outs[h] = with_table(
            run(root_kernel, h),
            [((4, part, cols), BF16), ((4, part, cols), F32)]
            + [((4, part, cols), BF16)] * 3,
            (4,),
            ((2, 3),),
            *gather(answers[h]),
            weights,
            acc3,
            mine,
            theirs,
            scratch=[VMEM((4 * size, cols), BF16), VMEM((4, size, cols), F32)],
        )
        got[h] = spread(outs[h])
    (turned,) = call(
        turned_kernel,
        [((3, 4, part, width), BF16)],
        turned0,
        turned1,
        *turned2.values(),
    )
    turned = after(turned, *got[CHUNKS - 1])[0]
    forest_out = lax.ppermute(turned, both, back)
    parts = []
    for h in every:
        parts += [outs[h][0], *got[h]]
    copies = 2 if layers == 2 else 1
    (total,) = call(
        run(total_kernel, CHUNKS),
        [((copies, 4, part, width), BF16 if copies == 2 else F32)],
        *parts,
    )
    if copies == 2:
        total = total.reshape(8, part, width)
        pieces = lax.all_to_all(total, ("layer", "prow"), 0, 0, tiled=True)
        pieces = pieces.reshape(2, 4, part, width)
        (root_out,) = call(join_kernel, [piece], pieces)
    else:
        total = lax.psum(total[0], "layer")
        root_out = lax.all_to_all(total, "prow", 0, 0, tiled=True).astype(BF16)
    return forest_out.reshape(1, 3 * size, width), root_out.reshape(size, width)


def solution(mesh):
    placed = (
        P("layer", ("prow", "pcol"), None),
        P(("prow", "pcol"), None),
        P("layer", None, "prow", "pcol", None, None, None, None),
        P("layer", None, "prow", "pcol", None, None),
        P("layer", None, "prow", "pcol", None, None),
        P("prow", "pcol", None, None),
    )
    return jax.shard_map(
        shards,
        mesh=mesh,
        in_specs=placed,
        out_specs=(P("layer", ("prow", "pcol"), None), P(("prow", "pcol"), None)),
        check_vma=False,
    )
```

time: 217 us -> 106 us (0.49); the launches traced: 213 us -> 105 us
  waiting for transfers between devices: 112 us -> 50 us
  blocking collectives: 59.6 us -> 13.6 us
  starting transfers between devices: 5 us -> 28.2 us
  matrix products: 13.1 us -> 0 us
  between operations: 13.9 us -> 0.88 us
  Pallas kernels: 0 us -> 9.02 us
  other arithmetic: 4.28 us -> 0 us
    reduce_scatter x3 -> x0, waiting for transfers between devices: 76.1 us -> none  [the longest x2 50 us: shards(): lax.psum_scatter(totals[tier_index], 'pcol', scatter_dimension=0, tiled=T...]
    ppermute x0 -> x27, waiting for transfers between devices: none -> 50 us  [the longest x24 46.4 us: swap(): return lax.ppermute(value, axis, [(i, i ^ k) for i in range(4)])]
    ppermute x0 -> x27, starting transfers between devices: none -> 28.2 us  [the longest x24 19.2 us: swap(): return lax.ppermute(value, axis, [(i, i ^ k) for i in range(4)])]
    all_to_all x3 -> x1, blocking collectives: 39.5 us -> 13.6 us  [shards(): pieces = lax.all_to_all(total, ('layer', 'prow'), 0, 0, tiled=True)]
    psum x1 -> x0, waiting for transfers between devices: 23.2 us -> none  [shards(): reduced_root = lax.psum(row_share[0], 'layer')]
    all_gather x3 -> x0, blocking collectives: 20.1 us -> none  [shards(): lax.all_gather(answer[None], 'prow', axis=0, tiled=True)]
    dot_general x10 -> x0, matrix products: 13.1 us -> none  [the longest x6 7.59 us: update(): jnp.einsum('jznv,zvs->jns', factor_weights, block_pieces, preferred_eleme...]
    all_to_all x1 -> x0, waiting for transfers between devices: 12.3 us -> none  [shards(): lax.all_to_all(lax.all_to_all(joined, 'prow', split_axis=1, concat_axis=1...]
  transfers between devices with their start and end apart: 5 -> 27, of which waited for: 5 -> 14; matrix products, arithmetic and copies ran while one was open for 2% -> 1% of each run, Pallas kernels for 0% -> 4%
where the time goes in v2:
time: 106 us; the launch traced here: 105 us
  waiting for transfers between devices  50 us (47%)
  starting transfers between devices  28.2 us (27%)
  blocking collectives  13.6 us (13%)
  Pallas kernels  9.02 us (9%)
  local copies, waits for them, and re-layouts  3.48 us (3%)
    ppermute x24, waiting for transfers between devices, swap(): return lax.ppermute(value, axis, [(i, i ^ k) for i in range(4)])  46.4 us
    ppermute x24, starting transfers between devices, swap(): return lax.ppermute(value, axis, [(i, i ^ k) for i in range(4)])  19.2 us
    all_to_all x1, blocking collectives, shards(): pieces = lax.all_to_all(total, ('layer', 'prow'), 0, 0, tiled=True)  13.6 us
    pallas_call x13, Pallas kernels, call(): pl.pallas_call(kernel, out_shape=[jax.ShapeDtypeStruct(shape, dtype) for...  9.02 us
    ppermute x1, starting transfers between devices, shards(): side = lax.ppermute(side, both, turn)  4.47 us
    ppermute x1, starting transfers between devices, shards(): forest_out = lax.ppermute(turned, both, back)  4.06 us
    ppermute x1, waiting for transfers between devices, shards(): side = lax.ppermute(side, both, turn)  3.57 us
    unnamed x19, local copies, waits for them, and re-layouts  2.67 us
  transfers between devices with their start and end apart: 27, of which 14 were waited for; matrix products, arithmetic and copies ran while one was open for 1% of the time, Pallas kernels for 4%

profile of v2, /device:TPU:6, one launch (start us, length us, event | category | flops | bytes accessed | tf_op | source)
XLA Modules:
  0.0 105.2 jit_solution(13973178227246619677)
XLA Ops:
  0.6 2.0 %shard_map.77 = (bf16[1,4,32,512]{3,2,1,0:T(8,128)(2,1)}, bf16[96,512]{1,0:T(8,128)(2,1)}, bf16[96,512]{1,0:T(8,128)(2,1)}, bf16[128,512]{1,0:T(8,128)(2,1)}, bf...) custom-call(bf16[3,4,32,512]{3,2,1,0:T(8,128)(2,1)} %bitcast.22, ...), custom_call_target="tpu_custom_call" | custom-call | tf_op jit(solution)/shard_map/pallas_call | solution.py:25
  2.6 4.5 %collective-permute-start = (bf16[1,4,32,512]{3,2,1,0:T(8,128)(2,1)}, bf16[1,4,32,512]{3,2,1,0:T(8,128)(2,1)S(1)}, u32[]{:S(2)}, u32[]{:S(2)}) collective-permute-start(bf16[1,4,32,512]{3,2,1,0:T(8,128)(2,1)} %get-tuple-element.49), channel_id=1, source_target_pairs={{0,0},{1,4},{2,8},{3,12},{4,1},{5,5},{6,9},{7,13},{8,2},{9,6},{10,... | collective-permute-start | bytes 393224 | tf_op jit(solution)/shard_map/ppermute | solution.py:344
  7.1 0.1 collective-permute-start.1
  7.1 0.8 copy.8.pattern
  8.0 1.9 %copy-done = bf16[1,6,1,1,4,4,128,128]{7,6,5,4,3,2,1,0:T(8,128)(2,1)S(1)} copy-done((bf16[1,6,1,1,4,4,128,128]{7,6,5,4,3,2,1,0:T(8,128)(2,1)S(1)}, bf16[1,6,1,1,4,4,128,128]{7,6,5,4,3,2,1,0:T(8,128)(2,1)}, u32[]{:S(2)}) %copy-start) | copy-done | bytes 3145752
  9.8 1.8 %shard_map.78.weights.refs_1_.refs_2_ = bf16[6,4,128,512]{3,2,1,0:T(8,128)(2,1)S(1)} custom-call(s32[6,4,4]{2,1,0:T(4,128)S(1)} %copy.8.pattern, bf16[6,4,4,128,128]{4,3,2,1,0:T(8,128)(2,1)S(1)} %bitcast.15), custom_call_target="tpu_custom_call" | custom-call | tf_op jit(solution)/shard_map/pallas_call | solution.py:25
  11.7 3.6 %collective-permute-done = bf16[1,4,32,512]{3,2,1,0:T(8,128)(2,1)S(1)} collective-permute-done((bf16[1,4,32,512]{3,2,1,0:T(8,128)(2,1)}, bf16[1,4,32,512]{3,2,1,0:T(8,128)(2,1)S(1)}, u32[]{:S(2)}, u32[]{:S(2)}) %collective-permute-start) | collective-permute-done | bytes 131104 | tf_op jit(solution)/shard_map/ppermute | solution.py:344
  15.3 1.0 collective-permute-done.1.m2
  16.2 0.1 collective-permute-start.2
  16.3 0.4 collective-permute-start.6
  16.7 5.0 %collective-permute-done.3.g2 = bf16[4,32,512]{2,1,0:T(8,128)(2,1)S(1)} collective-permute-done((bf16[4,32,512]{2,1,0:T(8,128)(2,1)S(1)}, bf16[4,32,512]{2,1,0:T(8,128)(2,1)S(1)}, u32[]{:S(2)}, u32[]{:S(2)}) %collective-permute-start.3) | collective-permute-done | bytes 131104 | tf_op jit(solution)/shard_map/ppermute | solution.py:299
  21.7 0.5 collective-permute-start.5
  22.2 1.0 collective-permute-done.5.m1
  23.2 0.8 shard_map.79
  24.1 0.1 collective-permute-start.7
  24.2 0.4 collective-permute-start.8
  24.6 4.0 %collective-permute-start.9 = (bf16[160,512]{1,0:T(8,128)(2,1)S(1)}, bf16[160,512]{1,0:T(8,128)(2,1)S(1)}, u32[]{:S(2)}, u32[]{:S(2)}) collective-permute-start(bf16[160,512]{1,0:T(8,128)(2,1)S(1)} %get-tuple-element.61), channel_id=1, source_target_pairs={{0,3},{1,2},{2,1},{3,0},{4,7},{5,6},{6,5},{7,4},{8,11},{9,10},{10,... | collective-permute-start | bytes 491528 | tf_op jit(solution)/shard_map/ppermute | solution.py:299
  28.5 3.2 %collective-permute-done.7.r1 = bf16[160,512]{1,0:T(8,128)(2,1)S(1)} collective-permute-done((bf16[160,512]{1,0:T(8,128)(2,1)S(1)}, bf16[160,512]{1,0:T(8,128)(2,1)S(1)}, u32[]{:S(2)}, u32[]{:S(2)}) %collective-permute-start.7) | collective-permute-done | bytes 163872 | tf_op jit(solution)/shard_map/ppermute | solution.py:299
  31.8 1.7 %collective-permute-start.11 = (bf16[2,32,512]{2,1,0:T(8,128)(2,1)S(1)}, bf16[2,32,512]{2,1,0:T(8,128)(2,1)S(1)}, u32[]{:S(2)}, u32[]{:S(2)}) collective-permute-start(bf16[2,32,512]{2,1,0:T(8,128)(2,1)S(1)} %copy-done.7), channel_id=1, source_target_pairs={{0,8},{4,12},{8,0},{12,4},{1,9},{5,13},{9,1},{13,5},{2,10},{6,14},... | collective-permute-start | bytes 196616 | tf_op jit(solution)/shard_map/ppermute | solution.py:299
  33.5 0.1 collective-permute-start.12
  33.6 5.6 %collective-permute-done.8.r2 = bf16[160,512]{1,0:T(8,128)(2,1)S(1)} collective-permute-done((bf16[160,512]{1,0:T(8,128)(2,1)S(1)}, bf16[160,512]{1,0:T(8,128)(2,1)S(1)}, u32[]{:S(2)}, u32[]{:S(2)}) %collective-permute-start.8) | collective-permute-done | bytes 163872 | tf_op jit(solution)/shard_map/ppermute | solution.py:299
  39.2 0.3 shard_map.81.s0
  39.5 0.4 collective-permute-start.14
  39.9 4.7 %collective-permute-done.14.s2 = bf16[128,512]{1,0:T(8,128)(2,1)S(1)} collective-permute-done((bf16[128,512]{1,0:T(8,128)(2,1)S(1)}, bf16[128,512]{1,0:T(8,128)(2,1)S(1)}, u32[]{:S(2)}, u32[]{:S(2)}) %collective-permute-start.14) | collective-permute-done | bytes 131104 | tf_op jit(solution)/shard_map/ppermute | solution.py:299
  44.6 0.8 shard_map.80
  45.4 0.5 collective-permute-done.15.s3
  45.9 0.5 shard_map.82
  46.4 3.6 %collective-permute-start.16 = (bf16[128,512]{1,0:T(8,128)(2,1)S(1)}, bf16[128,512]{1,0:T(8,128)(2,1)S(1)}, u32[]{:S(2)}, u32[]{:S(2)}) collective-permute-start(bf16[128,512]{1,0:T(8,128)(2,1)S(1)} %get-tuple-element.81), channel_id=1, source_target_pairs={{0,1},{1,0},{2,3},{3,2},{4,5},{5,4},{6,7},{7,6},{8,9},{9,8},{10,11... | collective-permute-start | bytes 393224 | tf_op jit(solution)/shard_map/ppermute | solution.py:299
  49.9 0.1 collective-permute-start.17
  50.0 2.4 %collective-permute-start.18 = (bf16[128,512]{1,0:T(8,128)(2,1)S(1)}, bf16[128,512]{1,0:T(8,128)(2,1)S(1)}, u32[]{:S(2)}, u32[]{:S(2)}) collective-permute-start(bf16[128,512]{1,0:T(8,128)(2,1)S(1)} %get-tuple-element.83), channel_id=1, source_target_pairs={{0,3},{1,2},{2,1},{3,0},{4,7},{5,6},{6,5},{7,4},{8,11},{9,10},{10,... | collective-permute-start | bytes 393224 | tf_op jit(solution)/shard_map/ppermute | solution.py:299
  52.4 2.4 %collective-permute-done.16.r1 = bf16[128,512]{1,0:T(8,128)(2,1)S(1)} collective-permute-done((bf16[128,512]{1,0:T(8,128)(2,1)S(1)}, bf16[128,512]{1,0:T(8,128)(2,1)S(1)}, u32[]{:S(2)}, u32[]{:S(2)}) %collective-permute-start.16) | collective-permute-done | bytes 131104 | tf_op jit(solution)/shard_map/ppermute | solution.py:299
  54.8 0.5 collective-permute-start.19
  55.3 7.4 %collective-permute-done.17.r2 = bf16[128,512]{1,0:T(8,128)(2,1)S(1)} collective-permute-done((bf16[128,512]{1,0:T(8,128)(2,1)S(1)}, bf16[128,512]{1,0:T(8,128)(2,1)S(1)}, u32[]{:S(2)}, u32[]{:S(2)}) %collective-permute-start.17) | collective-permute-done | bytes 131104 | tf_op jit(solution)/shard_map/ppermute | solution.py:299
  62.7 0.3 shard_map.85.s0
  63.0 0.5 collective-permute-start.21
  63.4 4.6 %collective-permute-done.21.s2 = bf16[128,512]{1,0:T(8,128)(2,1)S(1)} collective-permute-done((bf16[128,512]{1,0:T(8,128)(2,1)S(1)}, bf16[128,512]{1,0:T(8,128)(2,1)S(1)}, u32[]{:S(2)}, u32[]{:S(2)}) %collective-permute-start.21) | collective-permute-done | bytes 131104 | tf_op jit(solution)/shard_map/ppermute | solution.py:299
  68.0 0.4 shard_map.83
  68.5 0.9 collective-permute-done.22.s3
  69.4 1.4 %shard_map.86 = (bf16[4,32,512]{2,1,0:T(8,128)(2,1)S(1)}, f32[4,32,512]{2,1,0:T(8,128)S(1)}, bf16[4,32,512]{2,1,0:T(8,128)(2,1)S(1)}, bf16[4,32,512]{2,1,0:T(8,128)(2,1)S(1)}, bf16[4,32,512]{2,1,0:T(8,128)(2,1)S(1)}) custom-call(bf16[128,512]{1,0:T(8,128)(2,1)S(1)} %shard_map.85.s0, bf16[128,512]{1,0:T(8,128)(2,1)S(1)} %collective-permute-done.20.s1, ...), custom_call_target="tpu_custom_call" | custom-call | tf_op jit(solution)/shard_map/pallas_call | solution.py:25
  70.8 2.5 %collective-permute-start.23 = (bf16[4,32,512]{2,1,0:T(8,128)(2,1)S(1)}, bf16[4,32,512]{2,1,0:T(8,128)(2,1)S(1)}, u32[]{:S(2)}, u32[]{:S(2)}) collective-permute-start(bf16[4,32,512]{2,1,0:T(8,128)(2,1)S(1)} %get-tuple-element.91), channel_id=1, source_target_pairs={{0,1},{1,0},{2,3},{3,2},{4,5},{5,4},{6,7},{7,6},{8,9},{9,8},{10,11... | collective-permute-start | bytes 393224 | tf_op jit(solution)/shard_map/ppermute | solution.py:299
  73.3 2.4 %collective-permute-start.25 = (bf16[4,32,512]{2,1,0:T(8,128)(2,1)S(1)}, bf16[4,32,512]{2,1,0:T(8,128)(2,1)S(1)}, u32[]{:S(2)}, u32[]{:S(2)}) collective-permute-start(bf16[4,32,512]{2,1,0:T(8,128)(2,1)S(1)} %get-tuple-element.93), channel_id=1, source_target_pairs={{0,3},{1,2},{2,1},{3,0},{4,7},{5,6},{6,5},{7,4},{8,11},{9,10},{10,... | collective-permute-start | bytes 393224 | tf_op jit(solution)/shard_map/ppermute | solution.py:299
  75.8 2.6 %collective-permute-done.23.refs_1_ = bf16[4,32,512]{2,1,0:T(8,128)(2,1)S(1)} collective-permute-done((bf16[4,32,512]{2,1,0:T(8,128)(2,1)S(1)}, bf16[4,32,512]{2,1,0:T(8,128)(2,1)S(1)}, u32[]{:S(2)}, u32[]{:S(2)}) %collective-permute-start.23) | collective-permute-done | bytes 131104 | tf_op jit(solution)/shard_map/ppermute | solution.py:299
  78.4 7.7 %collective-permute-done.24.refs_2_ = bf16[4,32,512]{2,1,0:T(8,128)(2,1)S(1)} collective-permute-done((bf16[4,32,512]{2,1,0:T(8,128)(2,1)S(1)}, bf16[4,32,512]{2,1,0:T(8,128)(2,1)S(1)}, u32[]{:S(2)}, u32[]{:S(2)}) %collective-permute-start.24) | collective-permute-done | bytes 131104 | tf_op jit(solution)/shard_map/ppermute | solution.py:299
  86.0 4.1 %collective-permute-start.26 = (bf16[3,4,32,512]{3,2,1,0:T(8,128)(2,1)S(1)}, bf16[3,4,32,512]{3,2,1,0:T(8,128)(2,1)S(1)}, u32[]{:S(2)}, u32[]{:S(2)}) collective-permute-start(bf16[3,4,32,512]{3,2,1,0:T(8,128)(2,1)S(1)} %shard_map.87), channel_id=1, source_target_pairs={{0,0},{1,4},{2,8},{3,12},{8,1},{9,5},{10,9},{11,13},{4,2},{5,6},{6... | collective-permute-start | bytes 1179656 | tf_op jit(solution)/shard_map/ppermute | solution.py:445
  90.1 0.1 shard_map.88
  90.2 13.6 %all_to_all.5 = bf16[8,32,512]{2,1,0:T(8,128)(2,1)S(1)} all-to-all(bf16[8,32,512]{2,1,0:T(8,128)(2,1)S(1)} %bitcast.16), channel_id=1, replica_groups=mesh['layer'=2,'prow'=4,'pcol'=4] {'layer','prow'}, dimensions={0} | all-to-all | bytes 524288 | tf_op jit(solution)/shard_map/all_to_all | solution.py:457
  103.8 0.7 shard_map.89
  104.5 0.7 copy.10
  (41 shorter events, 0.2 us)
Async XLA Ops:
  2.6 12.7 %collective-permute-start = (bf16[1,4,32,512]{3,2,1,0:T(8,128)(2,1)}, bf16[1,4,32,512]{3,2,1,0:T(8,128)(2,1)S(1)}, u32[]{:S(2)}, u32[]{:S(2)}) collective-permute-start(bf16[1,4,32,512]{3,2,1,0:T(8,128)(2,1)} %get-tuple-element.49), channel_id=1, source_target_pairs={{0,0},{1,4},{2,8},{3,12},{4,1},{5,5},{6,9},{7,13},{8,2},{9,6},{10,... | collective-permute-start | bytes 393224 | tf_op jit(solution)/shard_map/ppermute | solution.py:344
  7.1 9.1 %collective-permute-start.1 = (bf16[128,512]{1,0:T(8,128)(2,1)}, bf16[128,512]{1,0:T(8,128)(2,1)S(1)}, u32[]{:S(2)}, u32[]{:S(2)}) collective-permute-start(bf16[128,512]{1,0:T(8,128)(2,1)} %get-tuple-element.50), channel_id=1, source_target_pairs={{0,8},{4,12},{8,0},{12,4},{1,9},{5,13},{9,1},{13,5},{2,10},{6,14},... | collective-permute-start | bytes 393224 | tf_op jit(solution)/shard_map/ppermute | solution.py:299
  8.0 1.9 %copy-start = (bf16[1,6,1,1,4,4,128,128]{7,6,5,4,3,2,1,0:T(8,128)(2,1)S(1)}, bf16[1,6,1,1,4,4,128,128]{7,6,5,4,3,2,1,0:T(8,128)(2,1)}, u32[]{:S(2)}) copy-start(bf16[1,6,1,1,4,4,128,128]{7,6,5,4,3,2,1,0:T(8,128)(2,1)} %param.8) | copy-start | bytes 9437188
  9.8 11.9 %copy-start.5 = (bf16[96,512]{1,0:T(8,128)(2,1)S(1)}, bf16[96,512]{1,0:T(8,128)(2,1)}, u32[]{:S(2)}) copy-start(bf16[96,512]{1,0:T(8,128)(2,1)} %get-tuple-element.53) | copy-start | bytes 294916
  9.8 13.4 %copy-start.1 = (bf16[32,512]{1,0:T(8,128)(2,1)S(1)}, bf16[32,512]{1,0:T(8,128)(2,1)}, u32[]{:S(2)}) copy-start(bf16[32,512]{1,0:T(8,128)(2,1)} %get-tuple-element.55.halved.own) | copy-start | bytes 98308
  9.8 13.4 %copy-start.2 = (bf16[96,512]{1,0:T(8,128)(2,1)S(1)}, bf16[96,512]{1,0:T(8,128)(2,1)}, u32[]{:S(2)}) copy-start(bf16[96,512]{1,0:T(8,128)(2,1)} %get-tuple-element.52.m0) | copy-start | bytes 294916
  11.6 20.1 %copy-start.8 = (bf16[2,32,512]{2,1,0:T(8,128)(2,1)S(1)}, bf16[2,32,512]{2,1,0:T(8,128)(2,1)}, u32[]{:S(2)}) copy-start(bf16[2,32,512]{2,1,0:T(8,128)(2,1)} %get-tuple-element.65) | copy-start | bytes 196612
  11.6 20.1 %copy-start.7 = (bf16[2,32,512]{2,1,0:T(8,128)(2,1)S(1)}, bf16[2,32,512]{2,1,0:T(8,128)(2,1)}, u32[]{:S(2)}) copy-start(bf16[2,32,512]{2,1,0:T(8,128)(2,1)} %get-tuple-element.66) | copy-start | bytes 196612
  11.7 21.8 %copy-start.6 = (bf16[2,32,512]{2,1,0:T(8,128)(2,1)S(1)}, bf16[2,32,512]{2,1,0:T(8,128)(2,1)}, u32[]{:S(2)}) copy-start(bf16[2,32,512]{2,1,0:T(8,128)(2,1)} %get-tuple-element.67) | copy-start | bytes 196612
  11.7 22.0 %copy-start.4 = (f32[1,3,1,1,128,128]{5,4,3,2,1,0:T(8,128)S(1)}, f32[1,3,1,1,128,128]{5,4,3,2,1,0:T(8,128)}, u32[]{:S(2)}) copy-start(f32[1,3,1,1,128,128]{5,4,3,2,1,0:T(8,128)} %param.10) | copy-start | bytes 589828
  11.7 32.9 %copy-start.3 = (bf16[2,32,512]{2,1,0:T(8,128)(2,1)S(1)}, bf16[2,32,512]{2,1,0:T(8,128)(2,1)}, u32[]{:S(2)}) copy-start(bf16[2,32,512]{2,1,0:T(8,128)(2,1)} %get-tuple-element.58.refs_3_) | copy-start | bytes 196612
  16.2 5.5 %collective-permute-start.3 = (bf16[4,32,512]{2,1,0:T(8,128)(2,1)S(1)}, bf16[4,32,512]{2,1,0:T(8,128)(2,1)S(1)}, u32[]{:S(2)}, u32[]{:S(2)}) collective-permute-start(bf16[4,32,512]{2,1,0:T(8,128)(2,1)S(1)} %bitcast.18), channel_id=1, source_target_pairs={{0,8},{4,12},{8,0},{12,4},{1,9},{5,13},{9,1},{13,5},{2,10},{6,14},... | collective-permute-start | bytes 393224 | tf_op jit(solution)/shard_map/ppermute | solution.py:299
  16.2 7.0 %collective-permute-start.2 = (bf16[4,32,512]{2,1,0:T(8,128)(2,1)S(1)}, bf16[4,32,512]{2,1,0:T(8,128)(2,1)S(1)}, u32[]{:S(2)}, u32[]{:S(2)}) collective-permute-start(bf16[4,32,512]{2,1,0:T(8,128)(2,1)S(1)} %bitcast.19), channel_id=1, source_target_pairs={{0,4},{4,0},{8,12},{12,8},{1,5},{5,1},{9,13},{13,9},{2,6},{6,2},{1... | collective-permute-start | bytes 393224 | tf_op jit(solution)/shard_map/ppermute | solution.py:299
  16.3 6.9 %collective-permute-start.6 = (bf16[128,512]{1,0:T(8,128)(2,1)S(1)}, bf16[128,512]{1,0:T(8,128)(2,1)S(1)}, u32[]{:S(2)}, u32[]{:S(2)}) collective-permute-start(bf16[128,512]{1,0:T(8,128)(2,1)S(1)} %collective-permute-done.1.m2), channel_id=1, source_target_pairs={{0,4},{4,0},{8,12},{12,8},{1,5},{5,1},{9,13},{13,9},{2,6},{6,2},{1... | collective-permute-start | bytes 393224 | tf_op jit(solution)/shard_map/ppermute | solution.py:299
  21.7 1.5 %collective-permute-start.4 = (bf16[4,32,512]{2,1,0:T(8,128)(2,1)S(1)}, bf16[4,32,512]{2,1,0:T(8,128)(2,1)S(1)}, u32[]{:S(2)}, u32[]{:S(2)}) collective-permute-start(bf16[4,32,512]{2,1,0:T(8,128)(2,1)S(1)} %collective-permute-done.3.g2), channel_id=1, source_target_pairs={{0,4},{4,0},{8,12},{12,8},{1,5},{5,1},{9,13},{13,9},{2,6},{6,2},{1... | collective-permute-start | bytes 393224 | tf_op jit(solution)/shard_map/ppermute | solution.py:299
  21.7 1.5 %collective-permute-start.5 = (bf16[96,512]{1,0:T(8,128)(2,1)S(1)}, bf16[96,512]{1,0:T(8,128)(2,1)S(1)}, u32[]{:S(2)}, u32[]{:S(2)}) collective-permute-start(bf16[96,512]{1,0:T(8,128)(2,1)S(1)} %copy-done.5), channel_id=1, source_target_pairs={{0,4},{4,0},{8,12},{12,8},{1,5},{5,1},{9,13},{13,9},{2,6},{6,2},{1... | collective-permute-start | bytes 294920 | tf_op jit(solution)/shard_map/ppermute | solution.py:299
  24.1 7.7 %collective-permute-start.7 = (bf16[160,512]{1,0:T(8,128)(2,1)S(1)}, bf16[160,512]{1,0:T(8,128)(2,1)S(1)}, u32[]{:S(2)}, u32[]{:S(2)}) collective-permute-start(bf16[160,512]{1,0:T(8,128)(2,1)S(1)} %get-tuple-element.59), channel_id=1, source_target_pairs={{0,1},{1,0},{2,3},{3,2},{4,5},{5,4},{6,7},{7,6},{8,9},{9,8},{10,11... | collective-permute-start | bytes 491528 | tf_op jit(solution)/shard_map/ppermute | solution.py:299
  24.2 15.1 %collective-permute-start.8 = (bf16[160,512]{1,0:T(8,128)(2,1)S(1)}, bf16[160,512]{1,0:T(8,128)(2,1)S(1)}, u32[]{:S(2)}, u32[]{:S(2)}) collective-permute-start(bf16[160,512]{1,0:T(8,128)(2,1)S(1)} %get-tuple-element.60), channel_id=1, source_target_pairs={{0,2},{1,3},{2,0},{3,1},{4,6},{5,7},{6,4},{7,5},{8,10},{9,11},{10,... | collective-permute-start | bytes 491528 | tf_op jit(solution)/shard_map/ppermute | solution.py:299
  24.6 14.7 %collective-permute-start.9 = (bf16[160,512]{1,0:T(8,128)(2,1)S(1)}, bf16[160,512]{1,0:T(8,128)(2,1)S(1)}, u32[]{:S(2)}, u32[]{:S(2)}) collective-permute-start(bf16[160,512]{1,0:T(8,128)(2,1)S(1)} %get-tuple-element.61), channel_id=1, source_target_pairs={{0,3},{1,2},{2,1},{3,0},{4,7},{5,6},{6,5},{7,4},{8,11},{9,10},{10,... | collective-permute-start | bytes 491528 | tf_op jit(solution)/shard_map/ppermute | solution.py:299
  31.8 7.5 %collective-permute-start.10 = (bf16[2,32,512]{2,1,0:T(8,128)(2,1)S(1)}, bf16[2,32,512]{2,1,0:T(8,128)(2,1)S(1)}, u32[]{:S(2)}, u32[]{:S(2)}) collective-permute-start(bf16[2,32,512]{2,1,0:T(8,128)(2,1)S(1)} %copy-done.8), channel_id=1, source_target_pairs={{0,4},{4,0},{8,12},{12,8},{1,5},{5,1},{9,13},{13,9},{2,6},{6,2},{1... | collective-permute-start | bytes 196616 | tf_op jit(solution)/shard_map/ppermute | solution.py:299
  31.8 7.5 %collective-permute-start.11 = (bf16[2,32,512]{2,1,0:T(8,128)(2,1)S(1)}, bf16[2,32,512]{2,1,0:T(8,128)(2,1)S(1)}, u32[]{:S(2)}, u32[]{:S(2)}) collective-permute-start(bf16[2,32,512]{2,1,0:T(8,128)(2,1)S(1)} %copy-done.7), channel_id=1, source_target_pairs={{0,8},{4,12},{8,0},{12,4},{1,9},{5,13},{9,1},{13,5},{2,10},{6,14},... | collective-permute-start | bytes 196616 | tf_op jit(solution)/shard_map/ppermute | solution.py:299
  33.5 5.7 %collective-permute-start.12 = (bf16[2,32,512]{2,1,0:T(8,128)(2,1)S(1)}, bf16[2,32,512]{2,1,0:T(8,128)(2,1)S(1)}, u32[]{:S(2)}, u32[]{:S(2)}) collective-permute-start(bf16[2,32,512]{2,1,0:T(8,128)(2,1)S(1)} %copy-done.6), channel_id=1, source_target_pairs={{0,12},{4,8},{8,4},{12,0},{1,13},{5,9},{9,5},{13,1},{2,14},{6,10},... | collective-permute-start | bytes 196616 | tf_op jit(solution)/shard_map/ppermute | solution.py:299
  39.5 5.0 %collective-permute-start.14 = (bf16[128,512]{1,0:T(8,128)(2,1)S(1)}, bf16[128,512]{1,0:T(8,128)(2,1)S(1)}, u32[]{:S(2)}, u32[]{:S(2)}) collective-permute-start(bf16[128,512]{1,0:T(8,128)(2,1)S(1)} %shard_map.81.s0), channel_id=1, source_target_pairs={{0,8},{4,12},{8,0},{12,4},{1,9},{5,13},{9,1},{13,5},{2,10},{6,14},... | collective-permute-start | bytes 393224 | tf_op jit(solution)/shard_map/ppermute | solution.py:299
  39.9 5.5 %collective-permute-start.13 = (bf16[128,512]{1,0:T(8,128)(2,1)S(1)}, bf16[128,512]{1,0:T(8,128)(2,1)S(1)}, u32[]{:S(2)}, u32[]{:S(2)}) collective-permute-start(bf16[128,512]{1,0:T(8,128)(2,1)S(1)} %shard_map.81.s0), channel_id=1, source_target_pairs={{0,4},{4,0},{8,12},{12,8},{1,5},{5,1},{9,13},{13,9},{2,6},{6,2},{1... | collective-permute-start | bytes 393224 | tf_op jit(solution)/shard_map/ppermute | solution.py:299
  44.6 1.3 %collective-permute-start.15 = (bf16[128,512]{1,0:T(8,128)(2,1)S(1)}, bf16[128,512]{1,0:T(8,128)(2,1)S(1)}, u32[]{:S(2)}, u32[]{:S(2)}) collective-permute-start(bf16[128,512]{1,0:T(8,128)(2,1)S(1)} %collective-permute-done.14.s2), channel_id=1, source_target_pairs={{0,4},{4,0},{8,12},{12,8},{1,5},{5,1},{9,13},{13,9},{2,6},{6,2},{1... | collective-permute-start | bytes 393224 | tf_op jit(solution)/shard_map/ppermute | solution.py:299
  46.4 8.4 %collective-permute-start.16 = (bf16[128,512]{1,0:T(8,128)(2,1)S(1)}, bf16[128,512]{1,0:T(8,128)(2,1)S(1)}, u32[]{:S(2)}, u32[]{:S(2)}) collective-permute-start(bf16[128,512]{1,0:T(8,128)(2,1)S(1)} %get-tuple-element.81), channel_id=1, source_target_pairs={{0,1},{1,0},{2,3},{3,2},{4,5},{5,4},{6,7},{7,6},{8,9},{9,8},{10,11... | collective-permute-start | bytes 393224 | tf_op jit(solution)/shard_map/ppermute | solution.py:299
  49.9 12.7 %collective-permute-start.17 = (bf16[128,512]{1,0:T(8,128)(2,1)S(1)}, bf16[128,512]{1,0:T(8,128)(2,1)S(1)}, u32[]{:S(2)}, u32[]{:S(2)}) collective-permute-start(bf16[128,512]{1,0:T(8,128)(2,1)S(1)} %get-tuple-element.82), channel_id=1, source_target_pairs={{0,2},{1,3},{2,0},{3,1},{4,6},{5,7},{6,4},{7,5},{8,10},{9,11},{10,... | collective-permute-start | bytes 393224 | tf_op jit(solution)/shard_map/ppermute | solution.py:299
  50.0 12.7 %collective-permute-start.18 = (bf16[128,512]{1,0:T(8,128)(2,1)S(1)}, bf16[128,512]{1,0:T(8,128)(2,1)S(1)}, u32[]{:S(2)}, u32[]{:S(2)}) collective-permute-start(bf16[128,512]{1,0:T(8,128)(2,1)S(1)} %get-tuple-element.83), channel_id=1, source_target_pairs={{0,3},{1,2},{2,1},{3,0},{4,7},{5,6},{6,5},{7,4},{8,11},{9,10},{10,... | collective-permute-start | bytes 393224 | tf_op jit(solution)/shard_map/ppermute | solution.py:299
  54.8 7.9 %collective-permute-start.19 = (f32[4,64,128]{2,1,0:T(8,128)S(1)}, f32[4,64,128]{2,1,0:T(8,128)S(1)}, u32[]{:S(2)}, u32[]{:S(2)}) collective-permute-start(f32[4,64,128]{2,1,0:T(8,128)S(1)} %shard_map.84.mine), channel_id=1, source_target_pairs={{0,16},{16,0},{1,17},{17,1},{2,18},{18,2},{3,19},{19,3},{4,20},{20... | collective-permute-start | bytes 393224 | tf_op jit(solution)/shard_map/ppermute | solution.py:406
  63.0 5.0 %collective-permute-start.21 = (bf16[128,512]{1,0:T(8,128)(2,1)S(1)}, bf16[128,512]{1,0:T(8,128)(2,1)S(1)}, u32[]{:S(2)}, u32[]{:S(2)}) collective-permute-start(bf16[128,512]{1,0:T(8,128)(2,1)S(1)} %shard_map.85.s0), channel_id=1, source_target_pairs={{0,8},{4,12},{8,0},{12,4},{1,9},{5,13},{9,1},{13,5},{2,10},{6,14},... | collective-permute-start | bytes 393224 | tf_op jit(solution)/shard_map/ppermute | solution.py:299
  63.4 5.0 %collective-permute-start.20 = (bf16[128,512]{1,0:T(8,128)(2,1)S(1)}, bf16[128,512]{1,0:T(8,128)(2,1)S(1)}, u32[]{:S(2)}, u32[]{:S(2)}) collective-permute-start(bf16[128,512]{1,0:T(8,128)(2,1)S(1)} %shard_map.85.s0), channel_id=1, source_target_pairs={{0,4},{4,0},{8,12},{12,8},{1,5},{5,1},{9,13},{13,9},{2,6},{6,2},{1... | collective-permute-start | bytes 393224 | tf_op jit(solution)/shard_map/ppermute | solution.py:299
  68.0 1.3 %collective-permute-start.22 = (bf16[128,512]{1,0:T(8,128)(2,1)S(1)}, bf16[128,512]{1,0:T(8,128)(2,1)S(1)}, u32[]{:S(2)}, u32[]{:S(2)}) collective-permute-start(bf16[128,512]{1,0:T(8,128)(2,1)S(1)} %collective-permute-done.21.s2), channel_id=1, source_target_pairs={{0,4},{4,0},{8,12},{12,8},{1,5},{5,1},{9,13},{13,9},{2,6},{6,2},{1... | collective-permute-start | bytes 393224 | tf_op jit(solution)/shard_map/ppermute | solution.py:299
  70.8 7.6 %collective-permute-start.23 = (bf16[4,32,512]{2,1,0:T(8,128)(2,1)S(1)}, bf16[4,32,512]{2,1,0:T(8,128)(2,1)S(1)}, u32[]{:S(2)}, u32[]{:S(2)}) collective-permute-start(bf16[4,32,512]{2,1,0:T(8,128)(2,1)S(1)} %get-tuple-element.91), channel_id=1, source_target_pairs={{0,1},{1,0},{2,3},{3,2},{4,5},{5,4},{6,7},{7,6},{8,9},{9,8},{10,11... | collective-permute-start | bytes 393224 | tf_op jit(solution)/shard_map/ppermute | solution.py:299
  73.3 12.7 %collective-permute-start.24 = (bf16[4,32,512]{2,1,0:T(8,128)(2,1)S(1)}, bf16[4,32,512]{2,1,0:T(8,128)(2,1)S(1)}, u32[]{:S(2)}, u32[]{:S(2)}) collective-permute-start(bf16[4,32,512]{2,1,0:T(8,128)(2,1)S(1)} %get-tuple-element.92), channel_id=1, source_target_pairs={{0,2},{1,3},{2,0},{3,1},{4,6},{5,7},{6,4},{7,5},{8,10},{9,11},{10,... | collective-permute-start | bytes 393224 | tf_op jit(solution)/shard_map/ppermute | solution.py:299
  73.3 12.7 %collective-permute-start.25 = (bf16[4,32,512]{2,1,0:T(8,128)(2,1)S(1)}, bf16[4,32,512]{2,1,0:T(8,128)(2,1)S(1)}, u32[]{:S(2)}, u32[]{:S(2)}) collective-permute-start(bf16[4,32,512]{2,1,0:T(8,128)(2,1)S(1)} %get-tuple-element.93), channel_id=1, source_target_pairs={{0,3},{1,2},{2,1},{3,0},{4,7},{5,6},{6,5},{7,4},{8,11},{9,10},{10,... | collective-permute-start | bytes 393224 | tf_op jit(solution)/shard_map/ppermute | solution.py:299
  86.0 18.4 %collective-permute-start.26 = (bf16[3,4,32,512]{3,2,1,0:T(8,128)(2,1)S(1)}, bf16[3,4,32,512]{3,2,1,0:T(8,128)(2,1)S(1)}, u32[]{:S(2)}, u32[]{:S(2)}) collective-permute-start(bf16[3,4,32,512]{3,2,1,0:T(8,128)(2,1)S(1)} %shard_map.87), channel_id=1, source_target_pairs={{0,0},{1,4},{2,8},{3,12},{8,1},{9,5},{10,9},{11,13},{4,2},{5,6},{6... | collective-permute-start | bytes 1179656 | tf_op jit(solution)/shard_map/ppermute | solution.py:445

commit v3 on v0

v3 whole, which is shorter than its diff:
```python
import functools

import jax
import jax.numpy as jnp
from jax import lax
from jax.experimental import pallas as pl
from jax.experimental.pallas import tpu as pltpu
from jax.sharding import PartitionSpec as P

F32 = jnp.float32
BF16 = jnp.bfloat16
VMEM = pltpu.VMEM
MIB = 1024 * 1024
LARGE = 60
CHUNKS = 2


def whole(count):
    return [pl.BlockSpec(memory_space=VMEM)] * count


def cost(micros):
    return pl.CostEstimate(
        flops=0, bytes_accessed=int(micros * 3.69e6), transcendentals=0
    )


def call(kernel, outs, *args, scratch=(), in_specs=None, limit=32, time=0.1):
    return pl.pallas_call(
        kernel,
        out_shape=[jax.ShapeDtypeStruct(shape, dtype) for shape, dtype in outs],
        in_specs=whole(len(args)) if in_specs is None else in_specs,
        out_specs=whole(len(outs)),
        scratch_shapes=list(scratch),
        compiler_params=pltpu.CompilerParams(vmem_limit_bytes=limit * MIB),
        cost_estimate=cost(time),
    )(*args)


def dot(left, right):
    return jnp.dot(left, right, preferred_element_type=F32)


def split(value):
    high = value.astype(BF16)
    return high, (value - high.astype(F32)).astype(BF16)


def precise(inverse, value):
    ih, il = inverse
    vh, vl = split(value)
    return dot(
        jnp.concatenate([ih, ih, il], axis=1), jnp.concatenate([vh, vl, vh], axis=0)
    )


def packed(inverse):
    high, low = split(inverse)
    half = high.shape[0] // 2
    return jnp.concatenate([high[:half], high[half:], low[:half], low[half:]], axis=1)


def unpacked(value):
    size = value.shape[1] // 4
    parts = [value[:, i * size : (i + 1) * size] for i in range(4)]
    return (
        jnp.concatenate(parts[:2], axis=0),
        jnp.concatenate(parts[2:], axis=0),
    )


def here():
    a, b = lax.axis_index("prow"), lax.axis_index("pcol")
    return a, b, a % 2


def at(start, length):
    return pl.ds(pl.multiple_of(start * length, length), length)


def crossed(index):
    return 2 * (index % 2) + index // 2


def pack_kernel(forest, root, inverses, last, side, own, near, far, *rest):
    held, top, inverse, final, sems = rest
    a, b, _ = here()
    part, wide = held.shape[2], side.shape[-1]
    half = final.shape[0] // 2
    moves = [
        pltpu.make_async_copy(source, out, sems.at[i])
        for i, (source, out) in enumerate(
            (
                (forest, held),
                (inverses, inverse),
                (root, top),
                (last, final),
            )
        )
    ]
    for move in moves:
        move.start()

    def piece(rows, k):
        there = a ^ k
        base, columns = there - there % 2, at(there % 2, wide)
        return jnp.concatenate(
            [rows[base, :, columns], rows[base + 1, :, columns]], axis=1
        )

    moves[0].wait()
    for i in range(2):
        side[i] = held[0, :, :, at((b % 2) ^ i, wide)]
    for i in range(1, 4):
        moves[i].wait()
    for out, slots in ((own, (0,)), (near, (1,)), (far, (2, 3))):
        out[:half] = packed(inverse[0])
        start = half
        for k in slots:
            for rows in (held.at[1], held.at[2], top):
                out[start : start + part] = piece(rows, k)
                start += part
    for value in (inverse[1], inverse[2], final[...]):
        for out in (own, near):
            out[start - 3 * part : start - 3 * part + half] = packed(value)
        start += half


def masked_rows(n, pattern, block, out, index):
    b, base = lax.axis_index("pcol"), index - index % 2
    size = block.shape[-1]
    for j in range(4):
        for k in range(4):
            value = block[b ^ j, base ^ k]
            out[j, :, k * size : (k + 1) * size] = jnp.where(
                pattern[n, b ^ j, base ^ k] != 0, value, jnp.zeros_like(value)
            )


def mask_kernel(first, flip, pattern, blocks, out, held, sems):
    a, _, _ = here()
    moves = [
        pltpu.make_async_copy(blocks.at[first + n], held.at[n], sems.at[n])
        for n in range(out.shape[0])
    ]
    for move in moves:
        move.start()
    for n, move in enumerate(moves):
        move.wait()
        masked_rows(first + n, pattern, held.at[n], out.at[n], a ^ flip)


def products(weights, solved):
    four, size, depth = weights.shape
    value = dot(weights[...].reshape(four * size, depth), solved[...])
    return value.reshape(four, size, solved.shape[1])


def send_sums(acc, own, other, solved, o0, o2, message):
    _, _, c = here()
    rows, size = o0.shape[0], own.shape[1]
    for weights, r in ((own, c), (other, 1 - c)):
        value = acc[r] - products(weights, solved)
        o0[at(r, size)] = value[0]
        o2[at(r, size)] = value[2]
        message[at(r, size)] = value[3].astype(message.dtype)
        message[at(2 + r, size)] = value[1].astype(message.dtype)


def place_rows(acc, given, h):
    _, b, _ = here()
    part, cols = given.shape[2], acc.shape[-1]
    acc[...] = jnp.zeros_like(acc)
    value = given[:, :, :, h * cols : (h + 1) * cols]
    acc[:, :, at(b, part)] = value.astype(F32)


def first_kernel(g0, g1, g2, g3, m0, m1, m2, m3, own, other, *rest):
    *solved, given, o0, o2, message, rows, acc = rest
    a, b, c = here()
    part, cols = g0.shape[-2], o0.shape[-1]
    size = 4 * part
    half = size // 2
    for m, piece in enumerate((g0, g1, g2, g3)):
        for u in range(4):
            rows[u, at(a ^ m, part)] = piece[m % 2, u]
    for m, packet in enumerate((m0, m1, m2, m3)):
        high, low = unpacked(packet[:half])
        right = rows[a ^ m]
        answer = dot(
            jnp.concatenate([high, low], axis=1),
            jnp.concatenate([right, right], axis=0),
        ).astype(BF16)
        for h, out in enumerate(solved):
            out[at(m ^ c, size)] = answer[:, h * cols : (h + 1) * cols]
        start = half + (3 * part if m == 3 else 0)
        wide = given.shape[-1]
        for level in range(3):
            for r in range(2):
                value = packet[start : start + part, r * wide : (r + 1) * wide]
                given[level, r, a ^ b ^ m] = value
            start += part
    place_rows(acc, given.at[0], 0)
    send_sums(acc, own.at[0], other.at[0], solved[0], o0, o2, message)


def second_kernel(h, solved, given, own, other, o0, o2, message, acc):
    place_rows(acc, given.at[0], h)
    send_sums(acc, own.at[0], other.at[0], solved, o0, o2, message)


def add_kernel(kept, came, out):
    out[...] = (kept[...] + came[: kept.shape[0]].astype(F32)).astype(out.dtype)


def summed(terms):
    rows = terms[-1].shape[0]
    total = terms[0][...].astype(F32)
    for term in terms[1:]:
        total += term[term.shape[0] - rows :].astype(F32)
    return total


def sum_kernel(*refs):
    refs[-1][...] = summed(refs[:-1]).astype(refs[-1].dtype)


def solve_kernel(level, *refs):
    *terms, own, near, out, value = refs
    _, _, c = here()
    value[...] = summed(terms)
    size = value.shape[0] // 2
    half = size // 2
    start = near.shape[0] - (4 - level) * half
    for message, r in ((own, c), (near, 1 - c)):
        inverse = unpacked(message[start : start + half])
        out[at(r, size)] = precise(inverse, value[at(r, size)]).astype(out.dtype)


def middle_kernel(own_at, other_at, s, far, own, other, acc, solved, *outs):
    rows = s.shape[0]
    solved[:rows] = s[...]
    solved[rows:] = far[...]
    send_sums(acc, own.at[own_at], other.at[other_at], solved, *outs)


def turn_rows(solved, mine, theirs):
    a, _, c = here()
    part = mine.shape[1]
    for out, index in ((mine, crossed(a)), (theirs, crossed(a ^ 1))):
        for k in range(4):
            out[(a - c) ^ k] = solved[at(4 * k + index, part)]


def rows_kernel(solved, mine, theirs):
    turn_rows(solved, mine, theirs)


def early_kernel(h, solved, given, own, other, *outs):
    acc2, acc3, mine, theirs = outs
    _, _, c = here()
    turn_rows(solved, mine, theirs)
    top = (lax.axis_index("layer") == 0).astype(F32)
    place_rows(acc2, given.at[1], h)
    place_rows(acc3, given.at[2], h)
    acc3[...] *= top
    for r, weights, first in ((c, own, 1), (1 - c, other, 0)):
        acc2[r] -= products(weights.at[first], solved)
        acc3[r] -= products(weights.at[first + 1], solved)


def later_kernel(solved, own, other, acc, out, mine, theirs):
    _, _, c = here()
    turn_rows(solved, mine, theirs)
    out[c] = acc[c] - products(own.at[4], solved)
    out[1 - c] = acc[1 - c] - products(other.at[3], solved)


def turn_kernel(*refs):
    *parts, mine, theirs = refs
    cols = parts[0].shape[-1]
    for index in range(0, len(parts), 2):
        level, h = divmod(index // 2, CHUNKS)
        columns = slice(h * cols, (h + 1) * cols)
        mine[level, :, :, columns] = parts[index][...]
        theirs[level, :, :, columns] = parts[index + 1][...]


def last_kernel(*refs):
    *parts, mine, theirs = refs
    a, _, c = here()
    rows, cols = parts[0].shape
    part = mine.shape[2]
    for index, piece in enumerate(parts):
        h, group = divmod(index, 2)
        columns = slice(h * cols, (h + 1) * cols)
        for out, place in ((mine, crossed(a)), (theirs, crossed(a ^ 1))):
            for r in range(2):
                value = piece[at(4 * r + place, part)]
                out[0, (a - c) ^ (2 * group + r), :, columns] = value


def swap_kernel(mine, came, out):
    _, _, c = here()
    cols = came.shape[-1]
    for level in range(out.shape[0]):
        out[level, :, :, at(c, cols)] = mine[level]
        out[level, :, :, at(1 - c, cols)] = came[level]


def output_kernel(first, second, forest, root):
    forest[...] = first[...]
    root[...] = second[...]


def shards(subtree_right_hand, root_rhs, blocks, pattern, forest_inverse, root_inverse):
    layers = lax.axis_size("layer")
    size = blocks.shape[-1]
    part, half = size // 4, size // 2
    width = subtree_right_hand.shape[-1]
    forest = subtree_right_hand.reshape(3, 4, part, width)
    root = root_rhs.reshape(4, part, width)
    blocks = blocks.reshape(6, 4, 4, size, size)
    pattern = pattern.reshape(6, 4, 4)
    inverses = forest_inverse.reshape(3, size, size)
    last_inverse = root_inverse.reshape(size, size)
    both = ("prow", "pcol")
    turn = [(i * 4 + j, j * 4 + i) for i in range(4) for j in range(4)]
    back = [
        [(i * 4 + j, j * 4 + crossed(i ^ k)) for i in range(4) for j in range(4)]
        for k in range(2)
    ]
    hbm = pl.BlockSpec(memory_space=pltpu.HBM)
    dma = pltpu.SemaphoreType.DMA
    run = functools.partial

    def after(*values):
        return lax.optimization_barrier(values)

    def swap(value, axis, k):
        return lax.ppermute(value, axis, [(i, i ^ k) for i in range(4)])

    tokens = []

    def step(how, kernel, outs, *args, in_specs=None, **options):
        count = len(args)
        specs = whole(count) if in_specs is None else list(in_specs)
        chained = bool(tokens)

        def body(*refs):
            ins, refs = refs[:count], refs[count + chained :]
            made, token, held = refs[: len(outs)], refs[len(outs)], refs[len(outs) + 1 :]
            token[...] = jnp.zeros_like(token)
            kernel(*ins, *made, *held)

        *results, token = how(
            body,
            [*outs, ((8, 128), F32)],
            *args,
            *tokens,
            in_specs=specs + whole(chained),
            **options,
        )
        tokens[:] = [token]
        return results

    rows = 2 * size
    wide = width // 2
    cols = wide // CHUNKS
    every = range(CHUNKS)
    block, kept = ((rows, cols), BF16), ((rows, cols), F32)
    sums = ((2, 4, size, cols), F32)
    tall = ((4 * size, cols), BF16)
    turned = ((4, part, cols), BF16)

    side, own, near, far = call(
        pack_kernel,
        [
            ((2, 4, part, wide), BF16),
            ((4 * half + 3 * part, width), BF16),
            ((4 * half + 3 * part, width), BF16),
            ((half + 6 * part, width), BF16),
        ],
        forest,
        root,
        inverses,
        last_inverse,
        in_specs=[hbm] * 4,
        time=2,
        scratch=[
            VMEM((3, 4, part, width), BF16),
            VMEM((4, part, width), BF16),
            VMEM((3, size, size), F32),
            VMEM((size, size), F32),
            dma((4,)),
        ],
        limit=LARGE,
    )
    side = lax.ppermute(side, both, turn)
    far = swap(far, "prow", 2)
    near = swap(near, "prow", 1)
    blocks_other, pattern_other = swap(blocks, "prow", 1), swap(pattern, "prow", 1)
    smem = pl.BlockSpec(memory_space=pltpu.SMEM)

    def masked(first, count, flip):
        (out,) = step(
            call,
            run(mask_kernel, first, flip),
            [((count, 4, size, 4 * size), BF16)],
            pattern_other if flip else pattern,
            blocks_other if flip else blocks,
            in_specs=[smem, hbm],
            scratch=[VMEM((count, 4, 4, size, size), BF16), dma((count,))],
            time=0.3 * count,
        )
        return out

    weights = masked(0, 6, 0)
    side, far, weights = after(side, far, weights)
    fourth = swap(far, "prow", 1)

    def send(outs):
        return swap(outs[2], "pcol", 1)

    def add(outs, came):
        (passed,) = step(call, add_kernel, [block], outs[1], came)
        return outs[0], came, swap(passed, "pcol", 2)

    def solve(level, *terms):
        (answer,) = step(
            call,
            run(solve_kernel, level),
            [block],
            *terms,
            own,
            near,
            scratch=[VMEM(*kept)],
            time=0.3,
        )
        return answer, swap(answer, "prow", 2)

    def join(mine, theirs):
        shape = (mine.shape[0], 4, part, width)
        return step(call, swap_kernel, [(shape, BF16)], mine, theirs)[0]

    message = ((2 * rows, cols), BF16)
    cross = swap(side, "prow", 2)
    sides = (side, swap(side, "prow", 1), cross, swap(cross, "prow", 1))
    first_other = masked(0, 1, 1)
    solved, outs, came, terms, pieces, acc2, acc3 = ({} for _ in range(7))
    turns = [{}, {}, {}]

    def early(h):
        acc2[h], acc3[h], *turns[0][h] = step(
            call,
            run(early_kernel, h),
            [sums, sums, turned, turned],
            solved[h],
            given,
            weights,
            others,
            time=0.7,
        )

    def later(h):
        acc3[h], *turns[1][h] = step(
            call,
            later_kernel,
            [sums, turned, turned],
            solved[h],
            weights,
            others,
            acc3[h],
            time=0.4,
        )

    def middle(h, pair, acc):
        solved[h], *outs[h] = step(
            call,
            run(middle_kernel, pair, pair - 1),
            [tall, kept, kept, message],
            *pieces[h],
            weights,
            others,
            acc[h],
            time=0.4,
        )
        came[h] = send(outs[h])

    *values, given, o0, o2, first_message = step(
        call,
        first_kernel,
        [tall] * CHUNKS + [((3, 2, 4, part, wide), BF16), kept, kept, message],
        *sides,
        own,
        near,
        far,
        fourth,
        weights,
        first_other,
        scratch=[VMEM((4, size, wide), BF16), VMEM((2, 4, size, cols), F32)],
        time=1.5,
    )
    for h in every:
        solved[h] = values[h]
        if h > 0:
            o0, o2, first_message = step(
                call,
                run(second_kernel, h),
                [kept, kept, message],
                solved[h],
                given,
                weights,
                first_other,
                scratch=[VMEM((2, 4, size, cols), F32)],
                time=0.4,
            )
        outs[h] = o0, o2, first_message
        came[h] = send(outs[h])
    others = masked(1, 5, 1)
    for h in every:
        terms[h] = add(outs[h], came[h])
        early(h)
    for h in every:
        pieces[h] = solve(1, *terms[h])
    for h in every:
        middle(h, 3, acc2)
    for h in every:
        terms[h] = add(outs[h], came[h])
        later(h)
    for h in every:
        pieces[h] = solve(2, *terms[h])
    for h in every:
        middle(h, 5, acc3)
    for h in every:
        turns[2][h] = step(call, rows_kernel, [turned, turned], solved[h])
    parts = [value for level in turns for h in every for value in level[h]]
    mine, theirs = step(call, turn_kernel, [((3, 4, part, wide), BF16)] * 2, *parts)
    theirs = swap(theirs, "prow", 1)
    for h in every:
        terms[h] = add(outs[h], came[h])
        if h == 0:
            pass
    for h in every:
        if h == 1:
            forest_rows = join(mine, theirs)
        (total,) = step(call, sum_kernel, [block if layers == 2 else kept], *terms[h])
        if layers == 2:
            terms[h] = total, lax.ppermute(total, "layer", [(0, 1), (1, 0)])
        else:
            terms[h] = (lax.psum(total, "layer"),)
    forest_out = lax.ppermute(forest_rows, both, back[0])
    for h in every:
        pieces[h] = solve(3, *terms[h])
    lasts = [piece for h in every for piece in pieces[h]]
    mine, theirs = step(call, last_kernel, [((1, 4, part, wide), BF16)] * 2, *lasts)
    root_rows = join(mine, swap(theirs, "prow", 1))
    root_out = lax.ppermute(root_rows, both, back[0])
    forest_out, root_out = step(
        call,
        output_kernel,
        [((3, 4, part, width), BF16), ((1, 4, part, width), BF16)],
        forest_out,
        root_out,
    )
    return forest_out.reshape(1, 3 * size, width), root_out.reshape(size, width)


def solution(mesh):
    placed = (
        P("layer", ("prow", "pcol"), None),
        P(("prow", "pcol"), None),
        P("layer", None, "prow", "pcol", None, None, None, None),
        P("layer", None, "prow", "pcol", None, None),
        P("layer", None, "prow", "pcol", None, None),
        P("prow", "pcol", None, None),
    )
    return jax.shard_map(
        shards,
        mesh=mesh,
        in_specs=placed,
        out_specs=(P("layer", ("prow", "pcol"), None), P(("prow", "pcol"), None)),
        check_vma=False,
    )
```

time: 217 us -> 102 us (0.47); the launches traced: 213 us -> 102 us
  blocking collectives: 59.6 us -> 0 us
  waiting for transfers between devices: 112 us -> 53.7 us
  starting transfers between devices: 5 us -> 29.2 us
  Pallas kernels: 0 us -> 15.5 us
  matrix products: 13.1 us -> 0 us
  between operations: 13.9 us -> 0.98 us
  other arithmetic: 4.28 us -> 0 us
  local copies, waits for them, and re-layouts: 5.09 us -> 2.69 us
    reduce_scatter x3 -> x0, waiting for transfers between devices: 76.1 us -> none  [the longest x2 50 us: shards(): lax.psum_scatter(totals[tier_index], 'pcol', scatter_dimension=0, tiled=T...]
    ppermute x0 -> x33, waiting for transfers between devices: none -> 53.7 us  [the longest x28 40.1 us: swap(): return lax.ppermute(value, axis, [(i, i ^ k) for i in range(4)])]
    all_to_all x3 -> x0, blocking collectives: 39.5 us -> none  [the longest x1 18.4 us: shards(): lax.all_to_all(stacked, 'pcol', split_axis=1, concat_axis=1, tiled=True)]
    ppermute x0 -> x33, starting transfers between devices: none -> 29.2 us  [the longest x28 17.6 us: swap(): return lax.ppermute(value, axis, [(i, i ^ k) for i in range(4)])]
    psum x1 -> x0, waiting for transfers between devices: 23.2 us -> none  [shards(): reduced_root = lax.psum(row_share[0], 'layer')]
    all_gather x3 -> x0, blocking collectives: 20.1 us -> none  [shards(): lax.all_gather(answer[None], 'prow', axis=0, tiled=True)]
    pallas_call x0 -> x35, Pallas kernels: none -> 15.5 us  [call(): pl.pallas_call(kernel, out_shape=[jax.ShapeDtypeStruct(shape, dtype) for...]
    dot_general x10 -> x0, matrix products: 13.1 us -> none  [the longest x6 7.59 us: update(): jnp.einsum('jznv,zvs->jns', factor_weights, block_pieces, preferred_eleme...]
  transfers between devices with their start and end apart: 5 -> 33, of which waited for: 5 -> 26; matrix products, arithmetic and copies ran while one was open for 2% -> 1% of each run, Pallas kernels for 0% -> 13%
where the time goes in v3:
time: 102 us
  waiting for transfers between devices  53.7 us (53%)
  starting transfers between devices  29.2 us (29%)
  Pallas kernels  15.5 us (15%)
  local copies, waits for them, and re-layouts  2.69 us (3%)
    ppermute x28, waiting for transfers between devices, swap(): return lax.ppermute(value, axis, [(i, i ^ k) for i in range(4)])  40.1 us
    ppermute x28, starting transfers between devices, swap(): return lax.ppermute(value, axis, [(i, i ^ k) for i in range(4)])  17.6 us
    pallas_call x35, Pallas kernels, call(): pl.pallas_call(kernel, out_shape=[jax.ShapeDtypeStruct(shape, dtype) for...  15.5 us
    ppermute x1, waiting for transfers between devices, shards(): root_out = lax.ppermute(root_rows, both, back[0])  8.14 us
    ppermute x1, starting transfers between devices, shards(): side = lax.ppermute(side, both, turn)  5.41 us
    ppermute x2, waiting for transfers between devices, shards(): terms[h] = (total, lax.ppermute(total, 'layer', [(0, 1), (1, 0)]))  3.92 us
    ppermute x1, starting transfers between devices, shards(): forest_out = lax.ppermute(forest_rows, both, back[0])  2.3 us
  transfers between devices with their start and end apart: 33, of which 26 were waited for; matrix products, arithmetic and copies ran while one was open for 1% of the time, Pallas kernels for 13%

profile of v3, /device:TPU:6, one launch (start us, length us, event | category | flops | bytes accessed | tf_op | source)
XLA Modules:
  0.0 102.1 jit_solution(5084889443059979379)
XLA Ops:
  0.7 2.1 %shard_map.77 = (bf16[2,4,32,256]{3,2,1,0:T(8,128)(2,1)}, bf16[352,512]{1,0:T(8,128)(2,1)}, bf16[352,512]{1,0:T(8,128)(2,1)}, bf16[256,512]{1,0:T(8,128)(2,1)}) custom-call(bf16[3,4,32,512]{3,2,1,0:T(8,128)(2,1)} %bitcast.10, bf16[4,32,512]{2,1,0:T(8,128)(2,1)} %bitcast.12, f32[3,128,128]{2,1,0:T(8,128)} %bitcast.11, f32[128,128]{1,0:T(8,128)} %bitcast.13), custom_call_target="tpu_custom_call" | custom-call | bytes 7380000 | tf_op jit(solution)/shard_map/pallas_call | solution.py:29
  2.9 0.6 collective-permute-start.1
  3.5 5.4 %collective-permute-start = (bf16[2,4,32,256]{3,2,1,0:T(8,128)(2,1)}, bf16[2,4,32,256]{3,2,1,0:T(8,128)(2,1)}, u32[]{:S(2)}, u32[]{:S(2)}) collective-permute-start(bf16[2,4,32,256]{3,2,1,0:T(8,128)(2,1)} %get-tuple-element.110), channel_id=1, source_target_pairs={{0,0},{1,4},{2,8},{3,12},{4,1},{5,5},{6,9},{7,13},{8,2},{9,6},{10,... | collective-permute-start | bytes 393224 | tf_op jit(solution)/shard_map/ppermute | solution.py:399
  8.9 1.2 %collective-permute-start.5 = (bf16[352,512]{1,0:T(8,128)(2,1)}, bf16[352,512]{1,0:T(8,128)(2,1)S(1)}, u32[]{:S(2)}, u32[]{:S(2)}) collective-permute-start(bf16[352,512]{1,0:T(8,128)(2,1)} %get-tuple-element.115), channel_id=1, source_target_pairs={{0,4},{4,0},{8,12},{12,8},{1,5},{5,1},{9,13},{13,9},{2,6},{6,2},{1... | collective-permute-start | bytes 1081352 | tf_op jit(solution)/shard_map/ppermute | solution.py:341
  10.1 0.8 copy.8.refs_0_
  10.9 1.9 %copy-done.1 = bf16[1,6,1,1,4,4,128,128]{7,6,5,4,3,2,1,0:T(8,128)(2,1)S(1)} copy-done((bf16[1,6,1,1,4,4,128,128]{7,6,5,4,3,2,1,0:T(8,128)(2,1)S(1)}, bf16[1,6,1,1,4,4,128,128]{7,6,5,4,3,2,1,0:T(8,128)(2,1)}, u32[]{:S(2)}) %copy-start.1) | copy-done | bytes 3145752
  12.8 1.8 %shard_map.78 = (bf16[6,4,128,512]{3,2,1,0:T(8,128)(2,1)S(1)}, f32[8,128]{1,0:T(8,128)S(1)}) custom-call(s32[6,4,4]{2,1,0:T(4,128)S(1)} %copy.8.refs_0_, bf16[6,4,4,128,128]{4,3,2,1,0:T(8,128)(2,1)S(1)} %bitcast.9), custom_call_target="tpu_custom_call" | custom-call | bytes 6641999 | tf_op jit(solution)/shard_map/pallas_call | solution.py:29
  14.6 1.6 %collective-permute-done.refs_0_ = bf16[2,4,32,256]{3,2,1,0:T(8,128)(2,1)} collective-permute-done((bf16[2,4,32,256]{3,2,1,0:T(8,128)(2,1)}, bf16[2,4,32,256]{3,2,1,0:T(8,128)(2,1)}, u32[]{:S(2)}, u32[]{:S(2)}) %collective-permute-start) | collective-permute-done | bytes 131104 | tf_op jit(solution)/shard_map/ppermute | solution.py:399
  16.7 1.0 %collective-permute-done.7.refs_0_ = s32[6,4,4]{2,1,0:T(4,128)S(1)} collective-permute-done((s32[6,4,4]{2,1,0:T(4,128)S(1)}, s32[6,4,4]{2,1,0:T(4,128)S(1)}, u32[]{:S(2)}, u32[]{:S(2)}) %collective-permute-start.7) | collective-permute-done | bytes 416 | tf_op jit(solution)/shard_map/ppermute | solution.py:341
  17.9 3.5 %collective-permute-done.3.refs_2_ = bf16[2,4,32,256]{3,2,1,0:T(8,128)(2,1)S(1)} collective-permute-done((bf16[2,4,32,256]{3,2,1,0:T(8,128)(2,1)}, bf16[2,4,32,256]{3,2,1,0:T(8,128)(2,1)S(1)}, u32[]{:S(2)}, u32[]{:S(2)}) %collective-permute-start.3) | collective-permute-done | bytes 131104 | tf_op jit(solution)/shard_map/ppermute | solution.py:341
  21.4 0.9 shard_map.79
  22.7 1.7 %shard_map.80 = (bf16[512,128]{1,0:T(8,128)(2,1)S(1)}, bf16[512,128]{1,0:T(8,128)(2,1)S(1)}, bf16[3,2,4,32,256]{4,3,2,1,0:T(8,128)(2,1)S(1)}, f32[256,128]{1,0:T...) custom-call(bf16[2,4,32,256]{3,2,1,0:T(8,128)(2,1)} %collective-permute-done.refs_0_, ...), custom_call_target="tpu_custom_call" | custom-call | bytes 5535000 | tf_op jit(solution)/shard_map/pallas_call | solution.py:29
  24.5 0.7 collective-permute-start.9
  25.6 1.5 %collective-permute-start.10 = (bf16[512,128]{1,0:T(8,128)(2,1)S(1)}, bf16[512,128]{1,0:T(8,128)(2,1)S(1)}, u32[]{:S(2)}, u32[]{:S(2)}) collective-permute-start(bf16[512,128]{1,0:T(8,128)(2,1)S(1)} %get-tuple-element.134), channel_id=1, source_target_pairs={{0,1},{1,0},{2,3},{3,2},{4,5},{5,4},{6,7},{7,6},{8,9},{9,8},{10,11... | collective-permute-start | bytes 393224 | tf_op jit(solution)/shard_map/ppermute | solution.py:341
  27.1 1.6 %shard_map.82 = (bf16[5,4,128,512]{3,2,1,0:T(8,128)(2,1)S(1)}, f32[8,128]{1,0:T(8,128)S(1)}) custom-call(s32[6,4,4]{2,1,0:T(4,128)S(1)} %collective-permute-done.7.refs_0_, bf16[6,4,4,128,128]{4,3,2,1,0:T(8,128)(2,1)S(1)} %collective-permute-done.8.refs_1_, f32[8,128]{1,0:T(8,128)S(1)} %get-tuple-element.125.refs_2_), custom_call_target="tpu_custom_call" | custom-call | bytes 5535000 | tf_op jit(solution)/shard_map/pallas_call | solution.py:29
  28.7 2.2 %collective-permute-done.9.refs_1_ = bf16[512,128]{1,0:T(8,128)(2,1)S(1)} collective-permute-done((bf16[512,128]{1,0:T(8,128)(2,1)S(1)}, bf16[512,128]{1,0:T(8,128)(2,1)S(1)}, u32[]{:S(2)}, u32[]{:S(2)}) %collective-permute-start.9) | collective-permute-done | bytes 131104 | tf_op jit(solution)/shard_map/ppermute | solution.py:341
  31.2 0.8 shard_map.84
  32.0 0.8 collective-permute-done.10.refs_1_
  32.9 1.9 %collective-permute-start.13 = (bf16[256,128]{1,0:T(8,128)(2,1)S(1)}, bf16[256,128]{1,0:T(8,128)(2,1)S(1)}, u32[]{:S(2)}, u32[]{:S(2)}) collective-permute-start(bf16[256,128]{1,0:T(8,128)(2,1)S(1)} %get-tuple-element.145), channel_id=1, source_target_pairs={{0,2},{1,3},{2,0},{3,1},{4,6},{5,7},{6,4},{7,5},{8,10},{9,11},{10,... | collective-permute-start | bytes 196616 | tf_op jit(solution)/shard_map/ppermute | solution.py:341
  34.8 0.8 shard_map.86
  35.6 3.2 %collective-permute-done.11.refs_2_ = bf16[256,128]{1,0:T(8,128)(2,1)S(1)} collective-permute-done((bf16[256,128]{1,0:T(8,128)(2,1)S(1)}, bf16[256,128]{1,0:T(8,128)(2,1)S(1)}, u32[]{:S(2)}, u32[]{:S(2)}) %collective-permute-start.11) | collective-permute-done | bytes 65568 | tf_op jit(solution)/shard_map/ppermute | solution.py:341
  39.9 1.5 %collective-permute-start.15 = (bf16[256,128]{1,0:T(8,128)(2,1)S(1)}, bf16[256,128]{1,0:T(8,128)(2,1)S(1)}, u32[]{:S(2)}, u32[]{:S(2)}) collective-permute-start(bf16[256,128]{1,0:T(8,128)(2,1)S(1)} %get-tuple-element.152.refs_0_), channel_id=1, source_target_pairs={{0,8},{4,12},{8,0},{12,4},{1,9},{5,13},{9,1},{13,5},{2,10},{6,14},... | collective-permute-start | bytes 196616 | tf_op jit(solution)/shard_map/ppermute | solution.py:341
  41.4 2.1 %collective-permute-done.12.refs_1_ = bf16[256,128]{1,0:T(8,128)(2,1)S(1)} collective-permute-done((bf16[256,128]{1,0:T(8,128)(2,1)S(1)}, bf16[256,128]{1,0:T(8,128)(2,1)S(1)}, u32[]{:S(2)}, u32[]{:S(2)}) %collective-permute-start.12) | collective-permute-done | bytes 65568 | tf_op jit(solution)/shard_map/ppermute | solution.py:341
  44.7 1.9 %collective-permute-start.16 = (bf16[512,128]{1,0:T(8,128)(2,1)S(1)}, bf16[512,128]{1,0:T(8,128)(2,1)S(1)}, u32[]{:S(2)}, u32[]{:S(2)}) collective-permute-start(bf16[512,128]{1,0:T(8,128)(2,1)S(1)} %get-tuple-element.162), channel_id=1, source_target_pairs={{0,1},{1,0},{2,3},{3,2},{4,5},{5,4},{6,7},{7,6},{8,9},{9,8},{10,11... | collective-permute-start | bytes 393224 | tf_op jit(solution)/shard_map/ppermute | solution.py:341
  46.6 3.2 %collective-permute-done.14.refs_1_ = bf16[512,128]{1,0:T(8,128)(2,1)S(1)} collective-permute-done((bf16[512,128]{1,0:T(8,128)(2,1)S(1)}, bf16[512,128]{1,0:T(8,128)(2,1)S(1)}, u32[]{:S(2)}, u32[]{:S(2)}) %collective-permute-start.14) | collective-permute-done | bytes 131104 | tf_op jit(solution)/shard_map/ppermute | solution.py:341
  50.3 0.9 collective-permute-done.16.refs_1_
  51.2 2.1 %collective-permute-start.19 = (bf16[256,128]{1,0:T(8,128)(2,1)S(1)}, bf16[256,128]{1,0:T(8,128)(2,1)S(1)}, u32[]{:S(2)}, u32[]{:S(2)}) collective-permute-start(bf16[256,128]{1,0:T(8,128)(2,1)S(1)} %get-tuple-element.173), channel_id=1, source_target_pairs={{0,2},{1,3},{2,0},{3,1},{4,6},{5,7},{6,4},{7,5},{8,10},{9,11},{10,... | collective-permute-start | bytes 196616 | tf_op jit(solution)/shard_map/ppermute | solution.py:341
  53.8 1.7 %collective-permute-done.17.refs_2_ = bf16[256,128]{1,0:T(8,128)(2,1)S(1)} collective-permute-done((bf16[256,128]{1,0:T(8,128)(2,1)S(1)}, bf16[256,128]{1,0:T(8,128)(2,1)S(1)}, u32[]{:S(2)}, u32[]{:S(2)}) %collective-permute-start.17) | collective-permute-done | bytes 65568 | tf_op jit(solution)/shard_map/ppermute | solution.py:341
  56.0 1.2 %collective-permute-done.19.refs_2_ = bf16[256,128]{1,0:T(8,128)(2,1)S(1)} collective-permute-done((bf16[256,128]{1,0:T(8,128)(2,1)S(1)}, bf16[256,128]{1,0:T(8,128)(2,1)S(1)}, u32[]{:S(2)}, u32[]{:S(2)}) %collective-permute-start.19) | collective-permute-done | bytes 65568 | tf_op jit(solution)/shard_map/ppermute | solution.py:341
  57.5 0.6 collective-permute-start.20
  58.1 1.9 %collective-permute-done.18.refs_1_ = bf16[256,128]{1,0:T(8,128)(2,1)S(1)} collective-permute-done((bf16[256,128]{1,0:T(8,128)(2,1)S(1)}, bf16[256,128]{1,0:T(8,128)(2,1)S(1)}, u32[]{:S(2)}, u32[]{:S(2)}) %collective-permute-start.18) | collective-permute-done | bytes 65568 | tf_op jit(solution)/shard_map/ppermute | solution.py:341
  60.6 1.3 %collective-permute-done.20.refs_1_ = bf16[256,128]{1,0:T(8,128)(2,1)S(1)} collective-permute-done((bf16[256,128]{1,0:T(8,128)(2,1)S(1)}, bf16[256,128]{1,0:T(8,128)(2,1)S(1)}, u32[]{:S(2)}, u32[]{:S(2)}) %collective-permute-start.20) | collective-permute-done | bytes 65568 | tf_op jit(solution)/shard_map/ppermute | solution.py:341
  62.5 0.8 collective-permute-start.24
  63.3 2.2 %collective-permute-done.22.refs_1_ = bf16[512,128]{1,0:T(8,128)(2,1)S(1)} collective-permute-done((bf16[512,128]{1,0:T(8,128)(2,1)S(1)}, bf16[512,128]{1,0:T(8,128)(2,1)S(1)}, u32[]{:S(2)}, u32[]{:S(2)}) %collective-permute-start.22) | collective-permute-done | bytes 131104 | tf_op jit(solution)/shard_map/ppermute | solution.py:341
  65.6 3.5 %collective-permute-done.24.refs_1_ = bf16[512,128]{1,0:T(8,128)(2,1)S(1)} collective-permute-done((bf16[512,128]{1,0:T(8,128)(2,1)S(1)}, bf16[512,128]{1,0:T(8,128)(2,1)S(1)}, u32[]{:S(2)}, u32[]{:S(2)}) %collective-permute-start.24) | collective-permute-done | bytes 131104 | tf_op jit(solution)/shard_map/ppermute | solution.py:341
  69.1 1.8 %collective-permute-start.27 = (bf16[256,128]{1,0:T(8,128)(2,1)S(1)}, bf16[256,128]{1,0:T(8,128)(2,1)S(1)}, u32[]{:S(2)}, u32[]{:S(2)}) collective-permute-start(bf16[256,128]{1,0:T(8,128)(2,1)S(1)} %get-tuple-element.203), channel_id=1, source_target_pairs={{0,2},{1,3},{2,0},{3,1},{4,6},{5,7},{6,4},{7,5},{8,10},{9,11},{10,... | collective-permute-start | bytes 196616 | tf_op jit(solution)/shard_map/ppermute | solution.py:341
  70.9 0.9 collective-permute-done.23.refs_2_
  71.9 2.3 %collective-permute-start.25 = (bf16[3,4,32,512]{3,2,1,0:T(8,128)(2,1)S(1)}, bf16[3,4,32,512]{3,2,1,0:T(8,128)(2,1)S(1)}, u32[]{:S(2)}, u32[]{:S(2)}) collective-permute-start(bf16[3,4,32,512]{3,2,1,0:T(8,128)(2,1)S(1)} %get-tuple-element.200), channel_id=1, source_target_pairs={{0,0},{1,4},{2,8},{3,12},{4,2},{5,6},{6,10},{7,14},{8,1},{9,5},{10... | collective-permute-start | bytes 1179656 | tf_op jit(solution)/shard_map/ppermute | solution.py:552
  75.1 1.4 %collective-permute-start.29 = (bf16[256,128]{1,0:T(8,128)(2,1)S(1)}, bf16[256,128]{1,0:T(8,128)(2,1)S(1)}, u32[]{:S(2)}, u32[]{:S(2)}) collective-permute-start(bf16[256,128]{1,0:T(8,128)(2,1)S(1)} %get-tuple-element.207.refs_0_), channel_id=1, source_target_pairs={{0,16},{16,0},{1,17},{17,1},{2,18},{18,2},{3,19},{19,3},{4,20},{20... | collective-permute-start | bytes 196616 | tf_op jit(solution)/shard_map/ppermute | solution.py:549
  76.4 2.8 %collective-permute-done.26.refs_1_ = bf16[256,128]{1,0:T(8,128)(2,1)S(1)} collective-permute-done((bf16[256,128]{1,0:T(8,128)(2,1)S(1)}, bf16[256,128]{1,0:T(8,128)(2,1)S(1)}, u32[]{:S(2)}, u32[]{:S(2)}) %collective-permute-start.26) | collective-permute-done | bytes 65568 | tf_op jit(solution)/shard_map/ppermute | solution.py:549
  79.6 1.1 %collective-permute-done.29.refs_1_ = bf16[256,128]{1,0:T(8,128)(2,1)S(1)} collective-permute-done((bf16[256,128]{1,0:T(8,128)(2,1)S(1)}, bf16[256,128]{1,0:T(8,128)(2,1)S(1)}, u32[]{:S(2)}, u32[]{:S(2)}) %collective-permute-start.29) | collective-permute-done | bytes 65568 | tf_op jit(solution)/shard_map/ppermute | solution.py:549
  80.9 1.0 collective-permute-start.30
  81.9 6.6 %collective-permute-done.28.refs_1_ = bf16[256,128]{1,0:T(8,128)(2,1)S(1)} collective-permute-done((bf16[256,128]{1,0:T(8,128)(2,1)S(1)}, bf16[256,128]{1,0:T(8,128)(2,1)S(1)}, u32[]{:S(2)}, u32[]{:S(2)}) %collective-permute-start.28) | collective-permute-done | bytes 65568 | tf_op jit(solution)/shard_map/ppermute | solution.py:341
  88.5 1.3 %collective-permute-done.30.refs_3_ = bf16[256,128]{1,0:T(8,128)(2,1)S(1)} collective-permute-done((bf16[256,128]{1,0:T(8,128)(2,1)S(1)}, bf16[256,128]{1,0:T(8,128)(2,1)S(1)}, u32[]{:S(2)}, u32[]{:S(2)}) %collective-permute-start.30) | collective-permute-done | bytes 65568 | tf_op jit(solution)/shard_map/ppermute | solution.py:341
  89.9 1.2 %collective-permute-done.31.refs_1_ = bf16[1,4,32,256]{3,2,1,0:T(8,128)(2,1)S(1)} collective-permute-done((bf16[1,4,32,256]{3,2,1,0:T(8,128)(2,1)S(1)}, bf16[1,4,32,256]{3,2,1,0:T(8,128)(2,1)S(1)}, u32[]{:S(2)}, u32[]{:S(2)}) %collective-permute-start.31) | collective-permute-done | bytes 65568 | tf_op jit(solution)/shard_map/ppermute | solution.py:341
  91.2 1.9 %collective-permute-start.32 = (bf16[1,4,32,512]{3,2,1,0:T(8,128)(2,1)S(1)}, bf16[1,4,32,512]{3,2,1,0:T(8,128)(2,1)S(1)}, u32[]{:S(2)}, u32[]{:S(2)}) collective-permute-start(bf16[1,4,32,512]{3,2,1,0:T(8,128)(2,1)S(1)} %get-tuple-element.214), channel_id=1, source_target_pairs={{0,0},{1,4},{2,8},{3,12},{4,2},{5,6},{6,10},{7,14},{8,1},{9,5},{10... | collective-permute-start | bytes 393224 | tf_op jit(solution)/shard_map/ppermute | solution.py:558
  93.1 8.1 %collective-permute-done.32.refs_1_ = bf16[1,4,32,512]{3,2,1,0:T(8,128)(2,1)S(1)} collective-permute-done((bf16[1,4,32,512]{3,2,1,0:T(8,128)(2,1)S(1)}, bf16[1,4,32,512]{3,2,1,0:T(8,128)(2,1)S(1)}, u32[]{:S(2)}, u32[]{:S(2)}) %collective-permute-start.32) | collective-permute-done | bytes 131104 | tf_op jit(solution)/shard_map/ppermute | solution.py:558
  101.3 0.8 shard_map.111
  (58 shorter events, 8.8 us)
Async XLA Ops:
  0.6 20.7 %collective-permute-start.8 = (bf16[6,4,4,128,128]{4,3,2,1,0:T(8,128)(2,1)}, bf16[6,4,4,128,128]{4,3,2,1,0:T(8,128)(2,1)S(1)}, u32[]{:S(2)}, u32[]{:S(2)}) collective-permute-start(bf16[6,4,4,128,128]{4,3,2,1,0:T(8,128)(2,1)} %bitcast.8), channel_id=1, source_target_pairs={{0,4},{4,0},{8,12},{12,8},{1,5},{5,1},{9,13},{13,9},{2,6},{6,2},{1... | collective-permute-start | bytes 9437192 | tf_op jit(solution)/shard_map/ppermute | solution.py:341
  2.9 13.3 %collective-permute-start.1 = (bf16[256,512]{1,0:T(8,128)(2,1)}, bf16[256,512]{1,0:T(8,128)(2,1)}, u32[]{:S(2)}, u32[]{:S(2)}) collective-permute-start(bf16[256,512]{1,0:T(8,128)(2,1)} %get-tuple-element.111), channel_id=1, source_target_pairs={{0,8},{4,12},{8,0},{12,4},{1,9},{5,13},{9,1},{13,5},{2,10},{6,14},... | collective-permute-start | bytes 786440 | tf_op jit(solution)/shard_map/ppermute | solution.py:341
  3.5 12.7 %collective-permute-start = (bf16[2,4,32,256]{3,2,1,0:T(8,128)(2,1)}, bf16[2,4,32,256]{3,2,1,0:T(8,128)(2,1)}, u32[]{:S(2)}, u32[]{:S(2)}) collective-permute-start(bf16[2,4,32,256]{3,2,1,0:T(8,128)(2,1)} %get-tuple-element.110), channel_id=1, source_target_pairs={{0,0},{1,4},{2,8},{3,12},{4,1},{5,5},{6,9},{7,13},{8,2},{9,6},{10,... | collective-permute-start | bytes 393224 | tf_op jit(solution)/shard_map/ppermute | solution.py:399
  8.9 13.4 %collective-permute-start.5 = (bf16[352,512]{1,0:T(8,128)(2,1)}, bf16[352,512]{1,0:T(8,128)(2,1)S(1)}, u32[]{:S(2)}, u32[]{:S(2)}) collective-permute-start(bf16[352,512]{1,0:T(8,128)(2,1)} %get-tuple-element.115), channel_id=1, source_target_pairs={{0,4},{4,0},{8,12},{12,8},{1,5},{5,1},{9,13},{13,9},{2,6},{6,2},{1... | collective-permute-start | bytes 1081352 | tf_op jit(solution)/shard_map/ppermute | solution.py:341
  10.9 1.9 %copy-start.1 = (bf16[1,6,1,1,4,4,128,128]{7,6,5,4,3,2,1,0:T(8,128)(2,1)S(1)}, bf16[1,6,1,1,4,4,128,128]{7,6,5,4,3,2,1,0:T(8,128)(2,1)}, u32[]{:S(2)}) copy-start(bf16[1,6,1,1,4,4,128,128]{7,6,5,4,3,2,1,0:T(8,128)(2,1)} %param.8) | copy-start | bytes 9437188
  12.8 9.9 %copy-start = (bf16[352,512]{1,0:T(8,128)(2,1)S(1)}, bf16[352,512]{1,0:T(8,128)(2,1)}, u32[]{:S(2)}) copy-start(bf16[352,512]{1,0:T(8,128)(2,1)} %get-tuple-element.114.refs_4_.refs_3_.refs_2_) | copy-start | bytes 1081348
  16.2 5.2 %collective-permute-start.3 = (bf16[2,4,32,256]{3,2,1,0:T(8,128)(2,1)}, bf16[2,4,32,256]{3,2,1,0:T(8,128)(2,1)S(1)}, u32[]{:S(2)}, u32[]{:S(2)}) collective-permute-start(bf16[2,4,32,256]{3,2,1,0:T(8,128)(2,1)} %collective-permute-done.refs_0_), channel_id=1, source_target_pairs={{0,8},{4,12},{8,0},{12,4},{1,9},{5,13},{9,1},{13,5},{2,10},{6,14},... | collective-permute-start | bytes 393224 | tf_op jit(solution)/shard_map/ppermute | solution.py:341
  16.2 6.5 %collective-permute-start.6 = (bf16[256,512]{1,0:T(8,128)(2,1)}, bf16[256,512]{1,0:T(8,128)(2,1)S(1)}, u32[]{:S(2)}, u32[]{:S(2)}) collective-permute-start(bf16[256,512]{1,0:T(8,128)(2,1)} %collective-permute-done.1.refs_6_), channel_id=1, source_target_pairs={{0,4},{4,0},{8,12},{12,8},{1,5},{5,1},{9,13},{13,9},{2,6},{6,2},{1... | collective-permute-start | bytes 786440 | tf_op jit(solution)/shard_map/ppermute | solution.py:341
  16.2 1.5 %collective-permute-start.7 = (s32[6,4,4]{2,1,0:T(4,128)S(1)}, s32[6,4,4]{2,1,0:T(4,128)S(1)}, u32[]{:S(2)}, u32[]{:S(2)}) collective-permute-start(s32[6,4,4]{2,1,0:T(4,128)S(1)} %copy.8.refs_0_), channel_id=1, source_target_pairs={{0,4},{4,0},{8,12},{12,8},{1,5},{5,1},{9,13},{13,9},{2,6},{6,2},{1... | collective-permute-start | bytes 1160 | tf_op jit(solution)/shard_map/ppermute | solution.py:341
  17.7 4.6 %collective-permute-start.2 = (bf16[2,4,32,256]{3,2,1,0:T(8,128)(2,1)}, bf16[2,4,32,256]{3,2,1,0:T(8,128)(2,1)S(1)}, u32[]{:S(2)}, u32[]{:S(2)}) collective-permute-start(bf16[2,4,32,256]{3,2,1,0:T(8,128)(2,1)} %collective-permute-done.refs_0_), channel_id=1, source_target_pairs={{0,4},{4,0},{8,12},{12,8},{1,5},{5,1},{9,13},{13,9},{2,6},{6,2},{1... | collective-permute-start | bytes 393224 | tf_op jit(solution)/shard_map/ppermute | solution.py:341
  21.4 1.3 %collective-permute-start.4 = (bf16[2,4,32,256]{3,2,1,0:T(8,128)(2,1)S(1)}, bf16[2,4,32,256]{3,2,1,0:T(8,128)(2,1)S(1)}, u32[]{:S(2)}, u32[]{:S(2)}) collective-permute-start(bf16[2,4,32,256]{3,2,1,0:T(8,128)(2,1)S(1)} %collective-permute-done.3.refs_2_), channel_id=1, source_target_pairs={{0,4},{4,0},{8,12},{12,8},{1,5},{5,1},{9,13},{13,9},{2,6},{6,2},{1... | collective-permute-start | bytes 393224 | tf_op jit(solution)/shard_map/ppermute | solution.py:341
  24.5 6.4 %collective-permute-start.9 = (bf16[512,128]{1,0:T(8,128)(2,1)S(1)}, bf16[512,128]{1,0:T(8,128)(2,1)S(1)}, u32[]{:S(2)}, u32[]{:S(2)}) collective-permute-start(bf16[512,128]{1,0:T(8,128)(2,1)S(1)} %get-tuple-element.128), channel_id=1, source_target_pairs={{0,1},{1,0},{2,3},{3,2},{4,5},{5,4},{6,7},{7,6},{8,9},{9,8},{10,11... | collective-permute-start | bytes 393224 | tf_op jit(solution)/shard_map/ppermute | solution.py:341
  25.6 7.3 %collective-permute-start.10 = (bf16[512,128]{1,0:T(8,128)(2,1)S(1)}, bf16[512,128]{1,0:T(8,128)(2,1)S(1)}, u32[]{:S(2)}, u32[]{:S(2)}) collective-permute-start(bf16[512,128]{1,0:T(8,128)(2,1)S(1)} %get-tuple-element.134), channel_id=1, source_target_pairs={{0,1},{1,0},{2,3},{3,2},{4,5},{5,4},{6,7},{7,6},{8,9},{9,8},{10,11... | collective-permute-start | bytes 393224 | tf_op jit(solution)/shard_map/ppermute | solution.py:341
  30.9 7.9 %collective-permute-start.11 = (bf16[256,128]{1,0:T(8,128)(2,1)S(1)}, bf16[256,128]{1,0:T(8,128)(2,1)S(1)}, u32[]{:S(2)}, u32[]{:S(2)}) collective-permute-start(bf16[256,128]{1,0:T(8,128)(2,1)S(1)} %get-tuple-element.140), channel_id=1, source_target_pairs={{0,2},{1,3},{2,0},{3,1},{4,6},{5,7},{6,4},{7,5},{8,10},{9,11},{10,... | collective-permute-start | bytes 196616 | tf_op jit(solution)/shard_map/ppermute | solution.py:341
  32.9 6.7 %collective-permute-start.13 = (bf16[256,128]{1,0:T(8,128)(2,1)S(1)}, bf16[256,128]{1,0:T(8,128)(2,1)S(1)}, u32[]{:S(2)}, u32[]{:S(2)}) collective-permute-start(bf16[256,128]{1,0:T(8,128)(2,1)S(1)} %get-tuple-element.145), channel_id=1, source_target_pairs={{0,2},{1,3},{2,0},{3,1},{4,6},{5,7},{6,4},{7,5},{8,10},{9,11},{10,... | collective-permute-start | bytes 196616 | tf_op jit(solution)/shard_map/ppermute | solution.py:341
  39.0 4.5 %collective-permute-start.12 = (bf16[256,128]{1,0:T(8,128)(2,1)S(1)}, bf16[256,128]{1,0:T(8,128)(2,1)S(1)}, u32[]{:S(2)}, u32[]{:S(2)}) collective-permute-start(bf16[256,128]{1,0:T(8,128)(2,1)S(1)} %get-tuple-element.142.refs_0_), channel_id=1, source_target_pairs={{0,8},{4,12},{8,0},{12,4},{1,9},{5,13},{9,1},{13,5},{2,10},{6,14},... | collective-permute-start | bytes 196616 | tf_op jit(solution)/shard_map/ppermute | solution.py:341
  39.9 4.3 %collective-permute-start.15 = (bf16[256,128]{1,0:T(8,128)(2,1)S(1)}, bf16[256,128]{1,0:T(8,128)(2,1)S(1)}, u32[]{:S(2)}, u32[]{:S(2)}) collective-permute-start(bf16[256,128]{1,0:T(8,128)(2,1)S(1)} %get-tuple-element.152.refs_0_), channel_id=1, source_target_pairs={{0,8},{4,12},{8,0},{12,4},{1,9},{5,13},{9,1},{13,5},{2,10},{6,14},... | collective-permute-start | bytes 196616 | tf_op jit(solution)/shard_map/ppermute | solution.py:341
  44.0 5.8 %collective-permute-start.14 = (bf16[512,128]{1,0:T(8,128)(2,1)S(1)}, bf16[512,128]{1,0:T(8,128)(2,1)S(1)}, u32[]{:S(2)}, u32[]{:S(2)}) collective-permute-start(bf16[512,128]{1,0:T(8,128)(2,1)S(1)} %get-tuple-element.151), channel_id=1, source_target_pairs={{0,1},{1,0},{2,3},{3,2},{4,5},{5,4},{6,7},{7,6},{8,9},{9,8},{10,11... | collective-permute-start | bytes 393224 | tf_op jit(solution)/shard_map/ppermute | solution.py:341
  44.7 6.5 %collective-permute-start.16 = (bf16[512,128]{1,0:T(8,128)(2,1)S(1)}, bf16[512,128]{1,0:T(8,128)(2,1)S(1)}, u32[]{:S(2)}, u32[]{:S(2)}) collective-permute-start(bf16[512,128]{1,0:T(8,128)(2,1)S(1)} %get-tuple-element.162), channel_id=1, source_target_pairs={{0,1},{1,0},{2,3},{3,2},{4,5},{5,4},{6,7},{7,6},{8,9},{9,8},{10,11... | collective-permute-start | bytes 393224 | tf_op jit(solution)/shard_map/ppermute | solution.py:341
  49.8 5.7 %collective-permute-start.17 = (bf16[256,128]{1,0:T(8,128)(2,1)S(1)}, bf16[256,128]{1,0:T(8,128)(2,1)S(1)}, u32[]{:S(2)}, u32[]{:S(2)}) collective-permute-start(bf16[256,128]{1,0:T(8,128)(2,1)S(1)} %get-tuple-element.168), channel_id=1, source_target_pairs={{0,2},{1,3},{2,0},{3,1},{4,6},{5,7},{6,4},{7,5},{8,10},{9,11},{10,... | collective-permute-start | bytes 196616 | tf_op jit(solution)/shard_map/ppermute | solution.py:341
  51.2 6.0 %collective-permute-start.19 = (bf16[256,128]{1,0:T(8,128)(2,1)S(1)}, bf16[256,128]{1,0:T(8,128)(2,1)S(1)}, u32[]{:S(2)}, u32[]{:S(2)}) collective-permute-start(bf16[256,128]{1,0:T(8,128)(2,1)S(1)} %get-tuple-element.173), channel_id=1, source_target_pairs={{0,2},{1,3},{2,0},{3,1},{4,6},{5,7},{6,4},{7,5},{8,10},{9,11},{10,... | collective-permute-start | bytes 196616 | tf_op jit(solution)/shard_map/ppermute | solution.py:341
  55.7 4.3 %collective-permute-start.18 = (bf16[256,128]{1,0:T(8,128)(2,1)S(1)}, bf16[256,128]{1,0:T(8,128)(2,1)S(1)}, u32[]{:S(2)}, u32[]{:S(2)}) collective-permute-start(bf16[256,128]{1,0:T(8,128)(2,1)S(1)} %get-tuple-element.170.refs_0_), channel_id=1, source_target_pairs={{0,8},{4,12},{8,0},{12,4},{1,9},{5,13},{9,1},{13,5},{2,10},{6,14},... | collective-permute-start | bytes 196616 | tf_op jit(solution)/shard_map/ppermute | solution.py:341
  57.5 4.3 %collective-permute-start.20 = (bf16[256,128]{1,0:T(8,128)(2,1)S(1)}, bf16[256,128]{1,0:T(8,128)(2,1)S(1)}, u32[]{:S(2)}, u32[]{:S(2)}) collective-permute-start(bf16[256,128]{1,0:T(8,128)(2,1)S(1)} %get-tuple-element.177.refs_0_), channel_id=1, source_target_pairs={{0,8},{4,12},{8,0},{12,4},{1,9},{5,13},{9,1},{13,5},{2,10},{6,14},... | collective-permute-start | bytes 196616 | tf_op jit(solution)/shard_map/ppermute | solution.py:341
  60.5 5.0 %collective-permute-start.22 = (bf16[512,128]{1,0:T(8,128)(2,1)S(1)}, bf16[512,128]{1,0:T(8,128)(2,1)S(1)}, u32[]{:S(2)}, u32[]{:S(2)}) collective-permute-start(bf16[512,128]{1,0:T(8,128)(2,1)S(1)} %get-tuple-element.191), channel_id=1, source_target_pairs={{0,1},{1,0},{2,3},{3,2},{4,5},{5,4},{6,7},{7,6},{8,9},{9,8},{10,11... | collective-permute-start | bytes 393224 | tf_op jit(solution)/shard_map/ppermute | solution.py:341
  62.4 9.4 %collective-permute-start.21 = (bf16[3,4,32,256]{3,2,1,0:T(8,128)(2,1)S(1)}, bf16[3,4,32,256]{3,2,1,0:T(8,128)(2,1)S(1)}, u32[]{:S(2)}, u32[]{:S(2)}) collective-permute-start(bf16[3,4,32,256]{3,2,1,0:T(8,128)(2,1)S(1)} %get-tuple-element.189), channel_id=1, source_target_pairs={{0,4},{4,0},{8,12},{12,8},{1,5},{5,1},{9,13},{13,9},{2,6},{6,2},{1... | collective-permute-start | bytes 589832 | tf_op jit(solution)/shard_map/ppermute | solution.py:341
  62.5 6.6 %collective-permute-start.24 = (bf16[512,128]{1,0:T(8,128)(2,1)S(1)}, bf16[512,128]{1,0:T(8,128)(2,1)S(1)}, u32[]{:S(2)}, u32[]{:S(2)}) collective-permute-start(bf16[512,128]{1,0:T(8,128)(2,1)S(1)} %get-tuple-element.196), channel_id=1, source_target_pairs={{0,1},{1,0},{2,3},{3,2},{4,5},{5,4},{6,7},{7,6},{8,9},{9,8},{10,11... | collective-permute-start | bytes 393224 | tf_op jit(solution)/shard_map/ppermute | solution.py:341
  65.5 6.3 %collective-permute-start.23 = (bf16[256,128]{1,0:T(8,128)(2,1)S(1)}, bf16[256,128]{1,0:T(8,128)(2,1)S(1)}, u32[]{:S(2)}, u32[]{:S(2)}) collective-permute-start(bf16[256,128]{1,0:T(8,128)(2,1)S(1)} %get-tuple-element.194), channel_id=1, source_target_pairs={{0,2},{1,3},{2,0},{3,1},{4,6},{5,7},{6,4},{7,5},{8,10},{9,11},{10,... | collective-permute-start | bytes 196616 | tf_op jit(solution)/shard_map/ppermute | solution.py:341
  69.1 5.9 %collective-permute-start.27 = (bf16[256,128]{1,0:T(8,128)(2,1)S(1)}, bf16[256,128]{1,0:T(8,128)(2,1)S(1)}, u32[]{:S(2)}, u32[]{:S(2)}) collective-permute-start(bf16[256,128]{1,0:T(8,128)(2,1)S(1)} %get-tuple-element.203), channel_id=1, source_target_pairs={{0,2},{1,3},{2,0},{3,1},{4,6},{5,7},{6,4},{7,5},{8,10},{9,11},{10,... | collective-permute-start | bytes 196616 | tf_op jit(solution)/shard_map/ppermute | solution.py:341
  71.9 29.3 %collective-permute-start.25 = (bf16[3,4,32,512]{3,2,1,0:T(8,128)(2,1)S(1)}, bf16[3,4,32,512]{3,2,1,0:T(8,128)(2,1)S(1)}, u32[]{:S(2)}, u32[]{:S(2)}) collective-permute-start(bf16[3,4,32,512]{3,2,1,0:T(8,128)(2,1)S(1)} %get-tuple-element.200), channel_id=1, source_target_pairs={{0,0},{1,4},{2,8},{3,12},{4,2},{5,6},{6,10},{7,14},{8,1},{9,5},{10... | collective-permute-start | bytes 1179656 | tf_op jit(solution)/shard_map/ppermute | solution.py:552
  74.2 5.0 %collective-permute-start.26 = (bf16[256,128]{1,0:T(8,128)(2,1)S(1)}, bf16[256,128]{1,0:T(8,128)(2,1)S(1)}, u32[]{:S(2)}, u32[]{:S(2)}) collective-permute-start(bf16[256,128]{1,0:T(8,128)(2,1)S(1)} %get-tuple-element.201.refs_0_), channel_id=1, source_target_pairs={{0,16},{16,0},{1,17},{17,1},{2,18},{18,2},{3,19},{19,3},{4,20},{20... | collective-permute-start | bytes 196616 | tf_op jit(solution)/shard_map/ppermute | solution.py:549
  75.1 5.6 %collective-permute-start.29 = (bf16[256,128]{1,0:T(8,128)(2,1)S(1)}, bf16[256,128]{1,0:T(8,128)(2,1)S(1)}, u32[]{:S(2)}, u32[]{:S(2)}) collective-permute-start(bf16[256,128]{1,0:T(8,128)(2,1)S(1)} %get-tuple-element.207.refs_0_), channel_id=1, source_target_pairs={{0,16},{16,0},{1,17},{17,1},{2,18},{18,2},{3,19},{19,3},{4,20},{20... | collective-permute-start | bytes 196616 | tf_op jit(solution)/shard_map/ppermute | solution.py:549
  79.5 9.0 %collective-permute-start.28 = (bf16[256,128]{1,0:T(8,128)(2,1)S(1)}, bf16[256,128]{1,0:T(8,128)(2,1)S(1)}, u32[]{:S(2)}, u32[]{:S(2)}) collective-permute-start(bf16[256,128]{1,0:T(8,128)(2,1)S(1)} %get-tuple-element.206.refs_0_), channel_id=1, source_target_pairs={{0,8},{4,12},{8,0},{12,4},{1,9},{5,13},{9,1},{13,5},{2,10},{6,14},... | collective-permute-start | bytes 196616 | tf_op jit(solution)/shard_map/ppermute | solution.py:341
  80.9 8.9 %collective-permute-start.30 = (bf16[256,128]{1,0:T(8,128)(2,1)S(1)}, bf16[256,128]{1,0:T(8,128)(2,1)S(1)}, u32[]{:S(2)}, u32[]{:S(2)}) collective-permute-start(bf16[256,128]{1,0:T(8,128)(2,1)S(1)} %get-tuple-element.209.refs_2_), channel_id=1, source_target_pairs={{0,8},{4,12},{8,0},{12,4},{1,9},{5,13},{9,1},{13,5},{2,10},{6,14},... | collective-permute-start | bytes 196616 | tf_op jit(solution)/shard_map/ppermute | solution.py:341
  89.8 1.3 %collective-permute-start.31 = (bf16[1,4,32,256]{3,2,1,0:T(8,128)(2,1)S(1)}, bf16[1,4,32,256]{3,2,1,0:T(8,128)(2,1)S(1)}, u32[]{:S(2)}, u32[]{:S(2)}) collective-permute-start(bf16[1,4,32,256]{3,2,1,0:T(8,128)(2,1)S(1)} %get-tuple-element.212), channel_id=1, source_target_pairs={{0,4},{4,0},{8,12},{12,8},{1,5},{5,1},{9,13},{13,9},{2,6},{6,2},{1... | collective-permute-start | bytes 196616 | tf_op jit(solution)/shard_map/ppermute | solution.py:341
  91.2 10.1 %collective-permute-start.32 = (bf16[1,4,32,512]{3,2,1,0:T(8,128)(2,1)S(1)}, bf16[1,4,32,512]{3,2,1,0:T(8,128)(2,1)S(1)}, u32[]{:S(2)}, u32[]{:S(2)}) collective-permute-start(bf16[1,4,32,512]{3,2,1,0:T(8,128)(2,1)S(1)} %get-tuple-element.214), channel_id=1, source_target_pairs={{0,0},{1,4},{2,8},{3,12},{4,2},{5,6},{6,10},{7,14},{8,1},{9,5},{10... | collective-permute-start | bytes 393224 | tf_op jit(solution)/shard_map/ppermute | solution.py:558

commit v4 on v3

--- a/solution.py
+++ b/solution.py
@@ -79,7 +79,7 @@
 
 
 def crossed(index):
-    return 2 * (index % 2) + index // 2
+    return (4 - index) % 4
 
 
 def pack_kernel(forest, root, inverses, last, side, own, near, far, *rest):
@@ -520,6 +520,7 @@
     others = masked(1, 5, 1)
     for h in every:
         terms[h] = add(outs[h], came[h])
+    for h in every:
         early(h)
     for h in every:
         pieces[h] = solve(1, *terms[h])
@@ -527,6 +528,7 @@
         middle(h, 3, acc2)
     for h in every:
         terms[h] = add(outs[h], came[h])
+    for h in every:
         later(h)
     for h in every:
         pieces[h] = solve(2, *terms[h])

time: 102 us -> 101 us (level)
  waiting for transfers between devices: 53.7 us -> 52.5 us
    ppermute x28, starting transfers between devices: 17.6 us -> 15.8 us  [swap(): return lax.ppermute(value, axis, [(i, i ^ k) for i in range(4)])]
    ppermute x2, waiting for transfers between devices: 3.92 us -> 2.74 us  [shards(): terms[h] = (total, lax.ppermute(total, 'layer', [(0, 1), (1, 0)]))]
where the time goes in v4:
time: 101 us; the launch traced here: 100 us
  waiting for transfers between devices  52.5 us (52%)
  starting transfers between devices  28.8 us (29%)
  Pallas kernels  15.4 us (15%)
  local copies, waits for them, and re-layouts  2.69 us (3%)
    ppermute x28, waiting for transfers between devices, swap(): return lax.ppermute(value, axis, [(i, i ^ k) for i in range(4)])  40.7 us
    ppermute x28, starting transfers between devices, swap(): return lax.ppermute(value, axis, [(i, i ^ k) for i in range(4)])  15.8 us
    pallas_call x35, Pallas kernels, call(): pl.pallas_call(kernel, out_shape=[jax.ShapeDtypeStruct(shape, dtype) for...  15.4 us
    ppermute x1, waiting for transfers between devices, shards(): root_out = lax.ppermute(root_rows, both, back[0])  7.44 us
    ppermute x1, starting transfers between devices, shards(): side = lax.ppermute(side, both, turn)  5.41 us
    ppermute x1, starting transfers between devices, shards(): forest_out = lax.ppermute(forest_rows, both, back[0])  3.12 us
    ppermute x2, waiting for transfers between devices, shards(): terms[h] = (total, lax.ppermute(total, 'layer', [(0, 1), (1, 0)]))  2.74 us
    ppermute x1, starting transfers between devices, shards(): root_out = lax.ppermute(root_rows, both, back[0])  2.61 us
  transfers between devices with their start and end apart: 33, of which 26 were waited for; matrix products, arithmetic and copies ran while one was open for 1% of the time, Pallas kernels for 13%

profile of v4, /device:TPU:6, one launch (start us, length us, event | category | flops | bytes accessed | tf_op | source)
XLA Modules:
  0.0 100.4 jit_solution(18444077716794517700)
XLA Ops:
  0.7 2.1 %shard_map.77 = (bf16[2,4,32,256]{3,2,1,0:T(8,128)(2,1)}, bf16[352,512]{1,0:T(8,128)(2,1)}, bf16[352,512]{1,0:T(8,128)(2,1)}, bf16[256,512]{1,0:T(8,128)(2,1)}) custom-call(bf16[3,4,32,512]{3,2,1,0:T(8,128)(2,1)} %bitcast.10, bf16[4,32,512]{2,1,0:T(8,128)(2,1)} %bitcast.12, f32[3,128,128]{2,1,0:T(8,128)} %bitcast.11, f32[128,128]{1,0:T(8,128)} %bitcast.13), custom_call_target="tpu_custom_call" | custom-call | bytes 7380000 | tf_op jit(solution)/shard_map/pallas_call | solution.py:29
  2.9 0.6 collective-permute-start.1
  3.5 5.4 %collective-permute-start = (bf16[2,4,32,256]{3,2,1,0:T(8,128)(2,1)}, bf16[2,4,32,256]{3,2,1,0:T(8,128)(2,1)}, u32[]{:S(2)}, u32[]{:S(2)}) collective-permute-start(bf16[2,4,32,256]{3,2,1,0:T(8,128)(2,1)} %get-tuple-element.110), channel_id=1, source_target_pairs={{0,0},{1,4},{2,8},{3,12},{4,1},{5,5},{6,9},{7,13},{8,2},{9,6},{10,... | collective-permute-start | bytes 393224 | tf_op jit(solution)/shard_map/ppermute | solution.py:399
  8.9 1.2 %collective-permute-start.5 = (bf16[352,512]{1,0:T(8,128)(2,1)}, bf16[352,512]{1,0:T(8,128)(2,1)S(1)}, u32[]{:S(2)}, u32[]{:S(2)}) collective-permute-start(bf16[352,512]{1,0:T(8,128)(2,1)} %get-tuple-element.115), channel_id=1, source_target_pairs={{0,4},{4,0},{8,12},{12,8},{1,5},{5,1},{9,13},{13,9},{2,6},{6,2},{1... | collective-permute-start | bytes 1081352 | tf_op jit(solution)/shard_map/ppermute | solution.py:341
  10.1 0.8 copy.8.refs_0_
  10.9 1.9 %copy-done.1 = bf16[1,6,1,1,4,4,128,128]{7,6,5,4,3,2,1,0:T(8,128)(2,1)S(1)} copy-done((bf16[1,6,1,1,4,4,128,128]{7,6,5,4,3,2,1,0:T(8,128)(2,1)S(1)}, bf16[1,6,1,1,4,4,128,128]{7,6,5,4,3,2,1,0:T(8,128)(2,1)}, u32[]{:S(2)}) %copy-start.1) | copy-done | bytes 3145752
  12.8 1.8 %shard_map.78 = (bf16[6,4,128,512]{3,2,1,0:T(8,128)(2,1)S(1)}, f32[8,128]{1,0:T(8,128)S(1)}) custom-call(s32[6,4,4]{2,1,0:T(4,128)S(1)} %copy.8.refs_0_, bf16[6,4,4,128,128]{4,3,2,1,0:T(8,128)(2,1)S(1)} %bitcast.9), custom_call_target="tpu_custom_call" | custom-call | bytes 6641999 | tf_op jit(solution)/shard_map/pallas_call | solution.py:29
  14.6 1.6 %collective-permute-done.refs_0_ = bf16[2,4,32,256]{3,2,1,0:T(8,128)(2,1)} collective-permute-done((bf16[2,4,32,256]{3,2,1,0:T(8,128)(2,1)}, bf16[2,4,32,256]{3,2,1,0:T(8,128)(2,1)}, u32[]{:S(2)}, u32[]{:S(2)}) %collective-permute-start) | collective-permute-done | bytes 131104 | tf_op jit(solution)/shard_map/ppermute | solution.py:399
  16.7 1.0 %collective-permute-done.7.refs_0_ = s32[6,4,4]{2,1,0:T(4,128)S(1)} collective-permute-done((s32[6,4,4]{2,1,0:T(4,128)S(1)}, s32[6,4,4]{2,1,0:T(4,128)S(1)}, u32[]{:S(2)}, u32[]{:S(2)}) %collective-permute-start.7) | collective-permute-done | bytes 416 | tf_op jit(solution)/shard_map/ppermute | solution.py:341
  17.9 3.5 %collective-permute-done.3.refs_2_ = bf16[2,4,32,256]{3,2,1,0:T(8,128)(2,1)S(1)} collective-permute-done((bf16[2,4,32,256]{3,2,1,0:T(8,128)(2,1)}, bf16[2,4,32,256]{3,2,1,0:T(8,128)(2,1)S(1)}, u32[]{:S(2)}, u32[]{:S(2)}) %collective-permute-start.3) | collective-permute-done | bytes 131104 | tf_op jit(solution)/shard_map/ppermute | solution.py:341
  21.4 0.9 shard_map.79
  22.7 1.7 %shard_map.80 = (bf16[512,128]{1,0:T(8,128)(2,1)S(1)}, bf16[512,128]{1,0:T(8,128)(2,1)S(1)}, bf16[3,2,4,32,256]{4,3,2,1,0:T(8,128)(2,1)S(1)}, f32[256,128]{1,0:T...) custom-call(bf16[2,4,32,256]{3,2,1,0:T(8,128)(2,1)} %collective-permute-done.refs_0_, ...), custom_call_target="tpu_custom_call" | custom-call | bytes 5535000 | tf_op jit(solution)/shard_map/pallas_call | solution.py:29
  24.5 0.7 collective-permute-start.10
  25.6 1.5 %collective-permute-start.9 = (bf16[512,128]{1,0:T(8,128)(2,1)S(1)}, bf16[512,128]{1,0:T(8,128)(2,1)S(1)}, u32[]{:S(2)}, u32[]{:S(2)}) collective-permute-start(bf16[512,128]{1,0:T(8,128)(2,1)S(1)} %get-tuple-element.128), channel_id=1, source_target_pairs={{0,1},{1,0},{2,3},{3,2},{4,5},{5,4},{6,7},{7,6},{8,9},{9,8},{10,11... | collective-permute-start | bytes 393224 | tf_op jit(solution)/shard_map/ppermute | solution.py:341
  27.1 1.6 %shard_map.82 = (bf16[5,4,128,512]{3,2,1,0:T(8,128)(2,1)S(1)}, f32[8,128]{1,0:T(8,128)S(1)}) custom-call(s32[6,4,4]{2,1,0:T(4,128)S(1)} %collective-permute-done.7.refs_0_, bf16[6,4,4,128,128]{4,3,2,1,0:T(8,128)(2,1)S(1)} %collective-permute-done.8.refs_1_, f32[8,128]{1,0:T(8,128)S(1)} %get-tuple-element.125.refs_2_), custom_call_target="tpu_custom_call" | custom-call | bytes 5535000 | tf_op jit(solution)/shard_map/pallas_call | solution.py:29
  28.7 2.2 %collective-permute-done.10.refs_1_ = bf16[512,128]{1,0:T(8,128)(2,1)S(1)} collective-permute-done((bf16[512,128]{1,0:T(8,128)(2,1)S(1)}, bf16[512,128]{1,0:T(8,128)(2,1)S(1)}, u32[]{:S(2)}, u32[]{:S(2)}) %collective-permute-start.10) | collective-permute-done | bytes 131104 | tf_op jit(solution)/shard_map/ppermute | solution.py:341
  31.2 1.6 %collective-permute-done.9.refs_1_ = bf16[512,128]{1,0:T(8,128)(2,1)S(1)} collective-permute-done((bf16[512,128]{1,0:T(8,128)(2,1)S(1)}, bf16[512,128]{1,0:T(8,128)(2,1)S(1)}, u32[]{:S(2)}, u32[]{:S(2)}) %collective-permute-start.9) | collective-permute-done | bytes 131104 | tf_op jit(solution)/shard_map/ppermute | solution.py:341
  32.9 1.1 %collective-permute-start.13 = (bf16[256,128]{1,0:T(8,128)(2,1)S(1)}, bf16[256,128]{1,0:T(8,128)(2,1)S(1)}, u32[]{:S(2)}, u32[]{:S(2)}) collective-permute-start(bf16[256,128]{1,0:T(8,128)(2,1)S(1)} %get-tuple-element.145), channel_id=1, source_target_pairs={{0,2},{1,3},{2,0},{3,1},{4,6},{5,7},{6,4},{7,5},{8,10},{9,11},{10,... | collective-permute-start | bytes 196616 | tf_op jit(solution)/shard_map/ppermute | solution.py:341
  34.0 0.8 shard_map.85
  34.7 0.8 shard_map.86
  35.5 3.3 %collective-permute-done.11.refs_2_ = bf16[256,128]{1,0:T(8,128)(2,1)S(1)} collective-permute-done((bf16[256,128]{1,0:T(8,128)(2,1)S(1)}, bf16[256,128]{1,0:T(8,128)(2,1)S(1)}, u32[]{:S(2)}, u32[]{:S(2)}) %collective-permute-start.11) | collective-permute-done | bytes 65568 | tf_op jit(solution)/shard_map/ppermute | solution.py:341
  39.9 1.5 %collective-permute-start.14 = (bf16[256,128]{1,0:T(8,128)(2,1)S(1)}, bf16[256,128]{1,0:T(8,128)(2,1)S(1)}, u32[]{:S(2)}, u32[]{:S(2)}) collective-permute-start(bf16[256,128]{1,0:T(8,128)(2,1)S(1)} %get-tuple-element.150.refs_0_), channel_id=1, source_target_pairs={{0,8},{4,12},{8,0},{12,4},{1,9},{5,13},{9,1},{13,5},{2,10},{6,14},... | collective-permute-start | bytes 196616 | tf_op jit(solution)/shard_map/ppermute | solution.py:341
  41.4 2.1 %collective-permute-done.12.refs_1_ = bf16[256,128]{1,0:T(8,128)(2,1)S(1)} collective-permute-done((bf16[256,128]{1,0:T(8,128)(2,1)S(1)}, bf16[256,128]{1,0:T(8,128)(2,1)S(1)}, u32[]{:S(2)}, u32[]{:S(2)}) %collective-permute-start.12) | collective-permute-done | bytes 65568 | tf_op jit(solution)/shard_map/ppermute | solution.py:341
  44.7 1.9 %collective-permute-start.15 = (bf16[512,128]{1,0:T(8,128)(2,1)S(1)}, bf16[512,128]{1,0:T(8,128)(2,1)S(1)}, u32[]{:S(2)}, u32[]{:S(2)}) collective-permute-start(bf16[512,128]{1,0:T(8,128)(2,1)S(1)} %get-tuple-element.154), channel_id=1, source_target_pairs={{0,1},{1,0},{2,3},{3,2},{4,5},{5,4},{6,7},{7,6},{8,9},{9,8},{10,11... | collective-permute-start | bytes 393224 | tf_op jit(solution)/shard_map/ppermute | solution.py:341
  46.6 3.2 %collective-permute-done.16.refs_1_ = bf16[512,128]{1,0:T(8,128)(2,1)S(1)} collective-permute-done((bf16[512,128]{1,0:T(8,128)(2,1)S(1)}, bf16[512,128]{1,0:T(8,128)(2,1)S(1)}, u32[]{:S(2)}, u32[]{:S(2)}) %collective-permute-start.16) | collective-permute-done | bytes 131104 | tf_op jit(solution)/shard_map/ppermute | solution.py:341
  49.9 1.3 %collective-permute-done.15.refs_1_ = bf16[512,128]{1,0:T(8,128)(2,1)S(1)} collective-permute-done((bf16[512,128]{1,0:T(8,128)(2,1)S(1)}, bf16[512,128]{1,0:T(8,128)(2,1)S(1)}, u32[]{:S(2)}, u32[]{:S(2)}) %collective-permute-start.15) | collective-permute-done | bytes 131104 | tf_op jit(solution)/shard_map/ppermute | solution.py:341
  51.2 1.7 %collective-permute-start.19 = (bf16[256,128]{1,0:T(8,128)(2,1)S(1)}, bf16[256,128]{1,0:T(8,128)(2,1)S(1)}, u32[]{:S(2)}, u32[]{:S(2)}) collective-permute-start(bf16[256,128]{1,0:T(8,128)(2,1)S(1)} %get-tuple-element.173), channel_id=1, source_target_pairs={{0,2},{1,3},{2,0},{3,1},{4,6},{5,7},{6,4},{7,5},{8,10},{9,11},{10,... | collective-permute-start | bytes 196616 | tf_op jit(solution)/shard_map/ppermute | solution.py:341
  53.8 1.7 %collective-permute-done.17.refs_2_ = bf16[256,128]{1,0:T(8,128)(2,1)S(1)} collective-permute-done((bf16[256,128]{1,0:T(8,128)(2,1)S(1)}, bf16[256,128]{1,0:T(8,128)(2,1)S(1)}, u32[]{:S(2)}, u32[]{:S(2)}) %collective-permute-start.17) | collective-permute-done | bytes 65568 | tf_op jit(solution)/shard_map/ppermute | solution.py:341
  56.0 1.2 %collective-permute-done.19.refs_2_ = bf16[256,128]{1,0:T(8,128)(2,1)S(1)} collective-permute-done((bf16[256,128]{1,0:T(8,128)(2,1)S(1)}, bf16[256,128]{1,0:T(8,128)(2,1)S(1)}, u32[]{:S(2)}, u32[]{:S(2)}) %collective-permute-start.19) | collective-permute-done | bytes 65568 | tf_op jit(solution)/shard_map/ppermute | solution.py:341
  57.5 0.6 collective-permute-start.20
  58.1 1.9 %collective-permute-done.18.refs_1_ = bf16[256,128]{1,0:T(8,128)(2,1)S(1)} collective-permute-done((bf16[256,128]{1,0:T(8,128)(2,1)S(1)}, bf16[256,128]{1,0:T(8,128)(2,1)S(1)}, u32[]{:S(2)}, u32[]{:S(2)}) %collective-permute-start.18) | collective-permute-done | bytes 65568 | tf_op jit(solution)/shard_map/ppermute | solution.py:341
  60.6 1.3 %collective-permute-done.20.refs_1_ = bf16[256,128]{1,0:T(8,128)(2,1)S(1)} collective-permute-done((bf16[256,128]{1,0:T(8,128)(2,1)S(1)}, bf16[256,128]{1,0:T(8,128)(2,1)S(1)}, u32[]{:S(2)}, u32[]{:S(2)}) %collective-permute-start.20) | collective-permute-done | bytes 65568 | tf_op jit(solution)/shard_map/ppermute | solution.py:341
  62.5 0.8 collective-permute-start.24
  63.3 2.2 %collective-permute-done.22.refs_1_ = bf16[512,128]{1,0:T(8,128)(2,1)S(1)} collective-permute-done((bf16[512,128]{1,0:T(8,128)(2,1)S(1)}, bf16[512,128]{1,0:T(8,128)(2,1)S(1)}, u32[]{:S(2)}, u32[]{:S(2)}) %collective-permute-start.22) | collective-permute-done | bytes 131104 | tf_op jit(solution)/shard_map/ppermute | solution.py:341
  65.6 3.5 %collective-permute-done.24.refs_1_ = bf16[512,128]{1,0:T(8,128)(2,1)S(1)} collective-permute-done((bf16[512,128]{1,0:T(8,128)(2,1)S(1)}, bf16[512,128]{1,0:T(8,128)(2,1)S(1)}, u32[]{:S(2)}, u32[]{:S(2)}) %collective-permute-start.24) | collective-permute-done | bytes 131104 | tf_op jit(solution)/shard_map/ppermute | solution.py:341
  69.1 0.6 collective-permute-start.27
  69.8 1.1 %collective-permute-done.23.refs_2_ = bf16[256,128]{1,0:T(8,128)(2,1)S(1)} collective-permute-done((bf16[256,128]{1,0:T(8,128)(2,1)S(1)}, bf16[256,128]{1,0:T(8,128)(2,1)S(1)}, u32[]{:S(2)}, u32[]{:S(2)}) %collective-permute-start.23) | collective-permute-done | bytes 65568 | tf_op jit(solution)/shard_map/ppermute | solution.py:341
  71.0 3.1 %collective-permute-start.25 = (bf16[3,4,32,512]{3,2,1,0:T(8,128)(2,1)S(1)}, bf16[3,4,32,512]{3,2,1,0:T(8,128)(2,1)S(1)}, u32[]{:S(2)}, u32[]{:S(2)}) collective-permute-start(bf16[3,4,32,512]{3,2,1,0:T(8,128)(2,1)S(1)} %get-tuple-element.200), channel_id=1, source_target_pairs={{0,0},{1,4},{2,8},{3,12},{4,3},{5,7},{6,11},{7,15},{8,2},{9,6},{10... | collective-permute-start | bytes 1179656 | tf_op jit(solution)/shard_map/ppermute | solution.py:554
  74.1 0.6 collective-permute-start.26
  75.1 1.3 %collective-permute-start.29 = (bf16[256,128]{1,0:T(8,128)(2,1)S(1)}, bf16[256,128]{1,0:T(8,128)(2,1)S(1)}, u32[]{:S(2)}, u32[]{:S(2)}) collective-permute-start(bf16[256,128]{1,0:T(8,128)(2,1)S(1)} %get-tuple-element.207.refs_0_), channel_id=1, source_target_pairs={{0,16},{16,0},{1,17},{17,1},{2,18},{18,2},{3,19},{19,3},{4,20},{20... | collective-permute-start | bytes 196616 | tf_op jit(solution)/shard_map/ppermute | solution.py:551
  76.3 2.2 %collective-permute-done.26.refs_1_ = bf16[256,128]{1,0:T(8,128)(2,1)S(1)} collective-permute-done((bf16[256,128]{1,0:T(8,128)(2,1)S(1)}, bf16[256,128]{1,0:T(8,128)(2,1)S(1)}, u32[]{:S(2)}, u32[]{:S(2)}) %collective-permute-start.26) | collective-permute-done | bytes 65568 | tf_op jit(solution)/shard_map/ppermute | solution.py:551
  79.6 1.5 %collective-permute-start.30 = (bf16[256,128]{1,0:T(8,128)(2,1)S(1)}, bf16[256,128]{1,0:T(8,128)(2,1)S(1)}, u32[]{:S(2)}, u32[]{:S(2)}) collective-permute-start(bf16[256,128]{1,0:T(8,128)(2,1)S(1)} %get-tuple-element.209.refs_2_), channel_id=1, source_target_pairs={{0,8},{4,12},{8,0},{12,4},{1,9},{5,13},{9,1},{13,5},{2,10},{6,14},... | collective-permute-start | bytes 196616 | tf_op jit(solution)/shard_map/ppermute | solution.py:341
  81.1 5.6 %collective-permute-done.28.refs_1_ = bf16[256,128]{1,0:T(8,128)(2,1)S(1)} collective-permute-done((bf16[256,128]{1,0:T(8,128)(2,1)S(1)}, bf16[256,128]{1,0:T(8,128)(2,1)S(1)}, u32[]{:S(2)}, u32[]{:S(2)}) %collective-permute-start.28) | collective-permute-done | bytes 65568 | tf_op jit(solution)/shard_map/ppermute | solution.py:341
  86.8 1.3 %collective-permute-done.30.refs_3_ = bf16[256,128]{1,0:T(8,128)(2,1)S(1)} collective-permute-done((bf16[256,128]{1,0:T(8,128)(2,1)S(1)}, bf16[256,128]{1,0:T(8,128)(2,1)S(1)}, u32[]{:S(2)}, u32[]{:S(2)}) %collective-permute-start.30) | collective-permute-done | bytes 65568 | tf_op jit(solution)/shard_map/ppermute | solution.py:341
  88.2 1.2 %collective-permute-done.31.refs_1_ = bf16[1,4,32,256]{3,2,1,0:T(8,128)(2,1)S(1)} collective-permute-done((bf16[1,4,32,256]{3,2,1,0:T(8,128)(2,1)S(1)}, bf16[1,4,32,256]{3,2,1,0:T(8,128)(2,1)S(1)}, u32[]{:S(2)}, u32[]{:S(2)}) %collective-permute-start.31) | collective-permute-done | bytes 65568 | tf_op jit(solution)/shard_map/ppermute | solution.py:341
  89.5 2.6 %collective-permute-start.32 = (bf16[1,4,32,512]{3,2,1,0:T(8,128)(2,1)S(1)}, bf16[1,4,32,512]{3,2,1,0:T(8,128)(2,1)S(1)}, u32[]{:S(2)}, u32[]{:S(2)}) collective-permute-start(bf16[1,4,32,512]{3,2,1,0:T(8,128)(2,1)S(1)} %get-tuple-element.214), channel_id=1, source_target_pairs={{0,0},{1,4},{2,8},{3,12},{4,3},{5,7},{6,11},{7,15},{8,2},{9,6},{10... | collective-permute-start | bytes 393224 | tf_op jit(solution)/shard_map/ppermute | solution.py:560
  92.1 7.4 %collective-permute-done.32.refs_1_ = bf16[1,4,32,512]{3,2,1,0:T(8,128)(2,1)S(1)} collective-permute-done((bf16[1,4,32,512]{3,2,1,0:T(8,128)(2,1)S(1)}, bf16[1,4,32,512]{3,2,1,0:T(8,128)(2,1)S(1)}, u32[]{:S(2)}, u32[]{:S(2)}) %collective-permute-start.32) | collective-permute-done | bytes 131104 | tf_op jit(solution)/shard_map/ppermute | solution.py:560
  99.5 0.8 shard_map.111
  (58 shorter events, 8.9 us)
Async XLA Ops:
  0.6 20.7 %collective-permute-start.8 = (bf16[6,4,4,128,128]{4,3,2,1,0:T(8,128)(2,1)}, bf16[6,4,4,128,128]{4,3,2,1,0:T(8,128)(2,1)S(1)}, u32[]{:S(2)}, u32[]{:S(2)}) collective-permute-start(bf16[6,4,4,128,128]{4,3,2,1,0:T(8,128)(2,1)} %bitcast.8), channel_id=1, source_target_pairs={{0,4},{4,0},{8,12},{12,8},{1,5},{5,1},{9,13},{13,9},{2,6},{6,2},{1... | collective-permute-start | bytes 9437192 | tf_op jit(solution)/shard_map/ppermute | solution.py:341
  2.9 13.3 %collective-permute-start.1 = (bf16[256,512]{1,0:T(8,128)(2,1)}, bf16[256,512]{1,0:T(8,128)(2,1)}, u32[]{:S(2)}, u32[]{:S(2)}) collective-permute-start(bf16[256,512]{1,0:T(8,128)(2,1)} %get-tuple-element.111), channel_id=1, source_target_pairs={{0,8},{4,12},{8,0},{12,4},{1,9},{5,13},{9,1},{13,5},{2,10},{6,14},... | collective-permute-start | bytes 786440 | tf_op jit(solution)/shard_map/ppermute | solution.py:341
  3.5 12.7 %collective-permute-start = (bf16[2,4,32,256]{3,2,1,0:T(8,128)(2,1)}, bf16[2,4,32,256]{3,2,1,0:T(8,128)(2,1)}, u32[]{:S(2)}, u32[]{:S(2)}) collective-permute-start(bf16[2,4,32,256]{3,2,1,0:T(8,128)(2,1)} %get-tuple-element.110), channel_id=1, source_target_pairs={{0,0},{1,4},{2,8},{3,12},{4,1},{5,5},{6,9},{7,13},{8,2},{9,6},{10,... | collective-permute-start | bytes 393224 | tf_op jit(solution)/shard_map/ppermute | solution.py:399
  8.9 13.4 %collective-permute-start.5 = (bf16[352,512]{1,0:T(8,128)(2,1)}, bf16[352,512]{1,0:T(8,128)(2,1)S(1)}, u32[]{:S(2)}, u32[]{:S(2)}) collective-permute-start(bf16[352,512]{1,0:T(8,128)(2,1)} %get-tuple-element.115), channel_id=1, source_target_pairs={{0,4},{4,0},{8,12},{12,8},{1,5},{5,1},{9,13},{13,9},{2,6},{6,2},{1... | collective-permute-start | bytes 1081352 | tf_op jit(solution)/shard_map/ppermute | solution.py:341
  10.9 1.9 %copy-start.1 = (bf16[1,6,1,1,4,4,128,128]{7,6,5,4,3,2,1,0:T(8,128)(2,1)S(1)}, bf16[1,6,1,1,4,4,128,128]{7,6,5,4,3,2,1,0:T(8,128)(2,1)}, u32[]{:S(2)}) copy-start(bf16[1,6,1,1,4,4,128,128]{7,6,5,4,3,2,1,0:T(8,128)(2,1)} %param.8) | copy-start | bytes 9437188
  12.8 9.9 %copy-start = (bf16[352,512]{1,0:T(8,128)(2,1)S(1)}, bf16[352,512]{1,0:T(8,128)(2,1)}, u32[]{:S(2)}) copy-start(bf16[352,512]{1,0:T(8,128)(2,1)} %get-tuple-element.114.refs_4_.refs_3_.refs_2_) | copy-start | bytes 1081348
  16.2 5.2 %collective-permute-start.3 = (bf16[2,4,32,256]{3,2,1,0:T(8,128)(2,1)}, bf16[2,4,32,256]{3,2,1,0:T(8,128)(2,1)S(1)}, u32[]{:S(2)}, u32[]{:S(2)}) collective-permute-start(bf16[2,4,32,256]{3,2,1,0:T(8,128)(2,1)} %collective-permute-done.refs_0_), channel_id=1, source_target_pairs={{0,8},{4,12},{8,0},{12,4},{1,9},{5,13},{9,1},{13,5},{2,10},{6,14},... | collective-permute-start | bytes 393224 | tf_op jit(solution)/shard_map/ppermute | solution.py:341
  16.2 6.5 %collective-permute-start.6 = (bf16[256,512]{1,0:T(8,128)(2,1)}, bf16[256,512]{1,0:T(8,128)(2,1)S(1)}, u32[]{:S(2)}, u32[]{:S(2)}) collective-permute-start(bf16[256,512]{1,0:T(8,128)(2,1)} %collective-permute-done.1.refs_6_), channel_id=1, source_target_pairs={{0,4},{4,0},{8,12},{12,8},{1,5},{5,1},{9,13},{13,9},{2,6},{6,2},{1... | collective-permute-start | bytes 786440 | tf_op jit(solution)/shard_map/ppermute | solution.py:341
  16.2 1.5 %collective-permute-start.7 = (s32[6,4,4]{2,1,0:T(4,128)S(1)}, s32[6,4,4]{2,1,0:T(4,128)S(1)}, u32[]{:S(2)}, u32[]{:S(2)}) collective-permute-start(s32[6,4,4]{2,1,0:T(4,128)S(1)} %copy.8.refs_0_), channel_id=1, source_target_pairs={{0,4},{4,0},{8,12},{12,8},{1,5},{5,1},{9,13},{13,9},{2,6},{6,2},{1... | collective-permute-start | bytes 1160 | tf_op jit(solution)/shard_map/ppermute | solution.py:341
  17.7 4.6 %collective-permute-start.2 = (bf16[2,4,32,256]{3,2,1,0:T(8,128)(2,1)}, bf16[2,4,32,256]{3,2,1,0:T(8,128)(2,1)S(1)}, u32[]{:S(2)}, u32[]{:S(2)}) collective-permute-start(bf16[2,4,32,256]{3,2,1,0:T(8,128)(2,1)} %collective-permute-done.refs_0_), channel_id=1, source_target_pairs={{0,4},{4,0},{8,12},{12,8},{1,5},{5,1},{9,13},{13,9},{2,6},{6,2},{1... | collective-permute-start | bytes 393224 | tf_op jit(solution)/shard_map/ppermute | solution.py:341
  21.4 1.3 %collective-permute-start.4 = (bf16[2,4,32,256]{3,2,1,0:T(8,128)(2,1)S(1)}, bf16[2,4,32,256]{3,2,1,0:T(8,128)(2,1)S(1)}, u32[]{:S(2)}, u32[]{:S(2)}) collective-permute-start(bf16[2,4,32,256]{3,2,1,0:T(8,128)(2,1)S(1)} %collective-permute-done.3.refs_2_), channel_id=1, source_target_pairs={{0,4},{4,0},{8,12},{12,8},{1,5},{5,1},{9,13},{13,9},{2,6},{6,2},{1... | collective-permute-start | bytes 393224 | tf_op jit(solution)/shard_map/ppermute | solution.py:341
  24.5 6.4 %collective-permute-start.10 = (bf16[512,128]{1,0:T(8,128)(2,1)S(1)}, bf16[512,128]{1,0:T(8,128)(2,1)S(1)}, u32[]{:S(2)}, u32[]{:S(2)}) collective-permute-start(bf16[512,128]{1,0:T(8,128)(2,1)S(1)} %get-tuple-element.130), channel_id=1, source_target_pairs={{0,1},{1,0},{2,3},{3,2},{4,5},{5,4},{6,7},{7,6},{8,9},{9,8},{10,11... | collective-permute-start | bytes 393224 | tf_op jit(solution)/shard_map/ppermute | solution.py:341
  25.6 7.3 %collective-permute-start.9 = (bf16[512,128]{1,0:T(8,128)(2,1)S(1)}, bf16[512,128]{1,0:T(8,128)(2,1)S(1)}, u32[]{:S(2)}, u32[]{:S(2)}) collective-permute-start(bf16[512,128]{1,0:T(8,128)(2,1)S(1)} %get-tuple-element.128), channel_id=1, source_target_pairs={{0,1},{1,0},{2,3},{3,2},{4,5},{5,4},{6,7},{7,6},{8,9},{9,8},{10,11... | collective-permute-start | bytes 393224 | tf_op jit(solution)/shard_map/ppermute | solution.py:341
  30.9 7.9 %collective-permute-start.11 = (bf16[256,128]{1,0:T(8,128)(2,1)S(1)}, bf16[256,128]{1,0:T(8,128)(2,1)S(1)}, u32[]{:S(2)}, u32[]{:S(2)}) collective-permute-start(bf16[256,128]{1,0:T(8,128)(2,1)S(1)} %get-tuple-element.140), channel_id=1, source_target_pairs={{0,2},{1,3},{2,0},{3,1},{4,6},{5,7},{6,4},{7,5},{8,10},{9,11},{10,... | collective-permute-start | bytes 196616 | tf_op jit(solution)/shard_map/ppermute | solution.py:341
  32.9 6.7 %collective-permute-start.13 = (bf16[256,128]{1,0:T(8,128)(2,1)S(1)}, bf16[256,128]{1,0:T(8,128)(2,1)S(1)}, u32[]{:S(2)}, u32[]{:S(2)}) collective-permute-start(bf16[256,128]{1,0:T(8,128)(2,1)S(1)} %get-tuple-element.145), channel_id=1, source_target_pairs={{0,2},{1,3},{2,0},{3,1},{4,6},{5,7},{6,4},{7,5},{8,10},{9,11},{10,... | collective-permute-start | bytes 196616 | tf_op jit(solution)/shard_map/ppermute | solution.py:341
  39.0 4.5 %collective-permute-start.12 = (bf16[256,128]{1,0:T(8,128)(2,1)S(1)}, bf16[256,128]{1,0:T(8,128)(2,1)S(1)}, u32[]{:S(2)}, u32[]{:S(2)}) collective-permute-start(bf16[256,128]{1,0:T(8,128)(2,1)S(1)} %get-tuple-element.142.refs_0_), channel_id=1, source_target_pairs={{0,8},{4,12},{8,0},{12,4},{1,9},{5,13},{9,1},{13,5},{2,10},{6,14},... | collective-permute-start | bytes 196616 | tf_op jit(solution)/shard_map/ppermute | solution.py:341
  39.9 4.3 %collective-permute-start.14 = (bf16[256,128]{1,0:T(8,128)(2,1)S(1)}, bf16[256,128]{1,0:T(8,128)(2,1)S(1)}, u32[]{:S(2)}, u32[]{:S(2)}) collective-permute-start(bf16[256,128]{1,0:T(8,128)(2,1)S(1)} %get-tuple-element.150.refs_0_), channel_id=1, source_target_pairs={{0,8},{4,12},{8,0},{12,4},{1,9},{5,13},{9,1},{13,5},{2,10},{6,14},... | collective-permute-start | bytes 196616 | tf_op jit(solution)/shard_map/ppermute | solution.py:341
  44.0 5.8 %collective-permute-start.16 = (bf16[512,128]{1,0:T(8,128)(2,1)S(1)}, bf16[512,128]{1,0:T(8,128)(2,1)S(1)}, u32[]{:S(2)}, u32[]{:S(2)}) collective-permute-start(bf16[512,128]{1,0:T(8,128)(2,1)S(1)} %get-tuple-element.156), channel_id=1, source_target_pairs={{0,1},{1,0},{2,3},{3,2},{4,5},{5,4},{6,7},{7,6},{8,9},{9,8},{10,11... | collective-permute-start | bytes 393224 | tf_op jit(solution)/shard_map/ppermute | solution.py:341
  44.7 6.5 %collective-permute-start.15 = (bf16[512,128]{1,0:T(8,128)(2,1)S(1)}, bf16[512,128]{1,0:T(8,128)(2,1)S(1)}, u32[]{:S(2)}, u32[]{:S(2)}) collective-permute-start(bf16[512,128]{1,0:T(8,128)(2,1)S(1)} %get-tuple-element.154), channel_id=1, source_target_pairs={{0,1},{1,0},{2,3},{3,2},{4,5},{5,4},{6,7},{7,6},{8,9},{9,8},{10,11... | collective-permute-start | bytes 393224 | tf_op jit(solution)/shard_map/ppermute | solution.py:341
  49.8 5.7 %collective-permute-start.17 = (bf16[256,128]{1,0:T(8,128)(2,1)S(1)}, bf16[256,128]{1,0:T(8,128)(2,1)S(1)}, u32[]{:S(2)}, u32[]{:S(2)}) collective-permute-start(bf16[256,128]{1,0:T(8,128)(2,1)S(1)} %get-tuple-element.168), channel_id=1, source_target_pairs={{0,2},{1,3},{2,0},{3,1},{4,6},{5,7},{6,4},{7,5},{8,10},{9,11},{10,... | collective-permute-start | bytes 196616 | tf_op jit(solution)/shard_map/ppermute | solution.py:341
  51.2 6.0 %collective-permute-start.19 = (bf16[256,128]{1,0:T(8,128)(2,1)S(1)}, bf16[256,128]{1,0:T(8,128)(2,1)S(1)}, u32[]{:S(2)}, u32[]{:S(2)}) collective-permute-start(bf16[256,128]{1,0:T(8,128)(2,1)S(1)} %get-tuple-element.173), channel_id=1, source_target_pairs={{0,2},{1,3},{2,0},{3,1},{4,6},{5,7},{6,4},{7,5},{8,10},{9,11},{10,... | collective-permute-start | bytes 196616 | tf_op jit(solution)/shard_map/ppermute | solution.py:341
  55.7 4.3 %collective-permute-start.18 = (bf16[256,128]{1,0:T(8,128)(2,1)S(1)}, bf16[256,128]{1,0:T(8,128)(2,1)S(1)}, u32[]{:S(2)}, u32[]{:S(2)}) collective-permute-start(bf16[256,128]{1,0:T(8,128)(2,1)S(1)} %get-tuple-element.170.refs_0_), channel_id=1, source_target_pairs={{0,8},{4,12},{8,0},{12,4},{1,9},{5,13},{9,1},{13,5},{2,10},{6,14},... | collective-permute-start | bytes 196616 | tf_op jit(solution)/shard_map/ppermute | solution.py:341
  57.5 4.3 %collective-permute-start.20 = (bf16[256,128]{1,0:T(8,128)(2,1)S(1)}, bf16[256,128]{1,0:T(8,128)(2,1)S(1)}, u32[]{:S(2)}, u32[]{:S(2)}) collective-permute-start(bf16[256,128]{1,0:T(8,128)(2,1)S(1)} %get-tuple-element.177.refs_0_), channel_id=1, source_target_pairs={{0,8},{4,12},{8,0},{12,4},{1,9},{5,13},{9,1},{13,5},{2,10},{6,14},... | collective-permute-start | bytes 196616 | tf_op jit(solution)/shard_map/ppermute | solution.py:341
  60.5 5.0 %collective-permute-start.22 = (bf16[512,128]{1,0:T(8,128)(2,1)S(1)}, bf16[512,128]{1,0:T(8,128)(2,1)S(1)}, u32[]{:S(2)}, u32[]{:S(2)}) collective-permute-start(bf16[512,128]{1,0:T(8,128)(2,1)S(1)} %get-tuple-element.191), channel_id=1, source_target_pairs={{0,1},{1,0},{2,3},{3,2},{4,5},{5,4},{6,7},{7,6},{8,9},{9,8},{10,11... | collective-permute-start | bytes 393224 | tf_op jit(solution)/shard_map/ppermute | solution.py:341
  62.4 8.5 %collective-permute-start.21 = (bf16[3,4,32,256]{3,2,1,0:T(8,128)(2,1)S(1)}, bf16[3,4,32,256]{3,2,1,0:T(8,128)(2,1)S(1)}, u32[]{:S(2)}, u32[]{:S(2)}) collective-permute-start(bf16[3,4,32,256]{3,2,1,0:T(8,128)(2,1)S(1)} %get-tuple-element.189), channel_id=1, source_target_pairs={{0,4},{4,0},{8,12},{12,8},{1,5},{5,1},{9,13},{13,9},{2,6},{6,2},{1... | collective-permute-start | bytes 589832 | tf_op jit(solution)/shard_map/ppermute | solution.py:341
  62.5 6.6 %collective-permute-start.24 = (bf16[512,128]{1,0:T(8,128)(2,1)S(1)}, bf16[512,128]{1,0:T(8,128)(2,1)S(1)}, u32[]{:S(2)}, u32[]{:S(2)}) collective-permute-start(bf16[512,128]{1,0:T(8,128)(2,1)S(1)} %get-tuple-element.196), channel_id=1, source_target_pairs={{0,1},{1,0},{2,3},{3,2},{4,5},{5,4},{6,7},{7,6},{8,9},{9,8},{10,11... | collective-permute-start | bytes 393224 | tf_op jit(solution)/shard_map/ppermute | solution.py:341
  65.5 5.4 %collective-permute-start.23 = (bf16[256,128]{1,0:T(8,128)(2,1)S(1)}, bf16[256,128]{1,0:T(8,128)(2,1)S(1)}, u32[]{:S(2)}, u32[]{:S(2)}) collective-permute-start(bf16[256,128]{1,0:T(8,128)(2,1)S(1)} %get-tuple-element.194), channel_id=1, source_target_pairs={{0,2},{1,3},{2,0},{3,1},{4,6},{5,7},{6,4},{7,5},{8,10},{9,11},{10,... | collective-permute-start | bytes 196616 | tf_op jit(solution)/shard_map/ppermute | solution.py:341
  69.1 5.9 %collective-permute-start.27 = (bf16[256,128]{1,0:T(8,128)(2,1)S(1)}, bf16[256,128]{1,0:T(8,128)(2,1)S(1)}, u32[]{:S(2)}, u32[]{:S(2)}) collective-permute-start(bf16[256,128]{1,0:T(8,128)(2,1)S(1)} %get-tuple-element.203), channel_id=1, source_target_pairs={{0,2},{1,3},{2,0},{3,1},{4,6},{5,7},{6,4},{7,5},{8,10},{9,11},{10,... | collective-permute-start | bytes 196616 | tf_op jit(solution)/shard_map/ppermute | solution.py:341
  71.0 28.5 %collective-permute-start.25 = (bf16[3,4,32,512]{3,2,1,0:T(8,128)(2,1)S(1)}, bf16[3,4,32,512]{3,2,1,0:T(8,128)(2,1)S(1)}, u32[]{:S(2)}, u32[]{:S(2)}) collective-permute-start(bf16[3,4,32,512]{3,2,1,0:T(8,128)(2,1)S(1)} %get-tuple-element.200), channel_id=1, source_target_pairs={{0,0},{1,4},{2,8},{3,12},{4,3},{5,7},{6,11},{7,15},{8,2},{9,6},{10... | collective-permute-start | bytes 1179656 | tf_op jit(solution)/shard_map/ppermute | solution.py:554
  74.1 4.4 %collective-permute-start.26 = (bf16[256,128]{1,0:T(8,128)(2,1)S(1)}, bf16[256,128]{1,0:T(8,128)(2,1)S(1)}, u32[]{:S(2)}, u32[]{:S(2)}) collective-permute-start(bf16[256,128]{1,0:T(8,128)(2,1)S(1)} %get-tuple-element.201.refs_0_), channel_id=1, source_target_pairs={{0,16},{16,0},{1,17},{17,1},{2,18},{18,2},{3,19},{19,3},{4,20},{20... | collective-permute-start | bytes 196616 | tf_op jit(solution)/shard_map/ppermute | solution.py:551
  75.1 4.3 %collective-permute-start.29 = (bf16[256,128]{1,0:T(8,128)(2,1)S(1)}, bf16[256,128]{1,0:T(8,128)(2,1)S(1)}, u32[]{:S(2)}, u32[]{:S(2)}) collective-permute-start(bf16[256,128]{1,0:T(8,128)(2,1)S(1)} %get-tuple-element.207.refs_0_), channel_id=1, source_target_pairs={{0,16},{16,0},{1,17},{17,1},{2,18},{18,2},{3,19},{19,3},{4,20},{20... | collective-permute-start | bytes 196616 | tf_op jit(solution)/shard_map/ppermute | solution.py:551
  78.8 8.0 %collective-permute-start.28 = (bf16[256,128]{1,0:T(8,128)(2,1)S(1)}, bf16[256,128]{1,0:T(8,128)(2,1)S(1)}, u32[]{:S(2)}, u32[]{:S(2)}) collective-permute-start(bf16[256,128]{1,0:T(8,128)(2,1)S(1)} %get-tuple-element.206.refs_0_), channel_id=1, source_target_pairs={{0,8},{4,12},{8,0},{12,4},{1,9},{5,13},{9,1},{13,5},{2,10},{6,14},... | collective-permute-start | bytes 196616 | tf_op jit(solution)/shard_map/ppermute | solution.py:341
  79.6 8.5 %collective-permute-start.30 = (bf16[256,128]{1,0:T(8,128)(2,1)S(1)}, bf16[256,128]{1,0:T(8,128)(2,1)S(1)}, u32[]{:S(2)}, u32[]{:S(2)}) collective-permute-start(bf16[256,128]{1,0:T(8,128)(2,1)S(1)} %get-tuple-element.209.refs_2_), channel_id=1, source_target_pairs={{0,8},{4,12},{8,0},{12,4},{1,9},{5,13},{9,1},{13,5},{2,10},{6,14},... | collective-permute-start | bytes 196616 | tf_op jit(solution)/shard_map/ppermute | solution.py:341
  88.1 1.3 %collective-permute-start.31 = (bf16[1,4,32,256]{3,2,1,0:T(8,128)(2,1)S(1)}, bf16[1,4,32,256]{3,2,1,0:T(8,128)(2,1)S(1)}, u32[]{:S(2)}, u32[]{:S(2)}) collective-permute-start(bf16[1,4,32,256]{3,2,1,0:T(8,128)(2,1)S(1)} %get-tuple-element.212), channel_id=1, source_target_pairs={{0,4},{4,0},{8,12},{12,8},{1,5},{5,1},{9,13},{13,9},{2,6},{6,2},{1... | collective-permute-start | bytes 196616 | tf_op jit(solution)/shard_map/ppermute | solution.py:341
  89.5 10.1 %collective-permute-start.32 = (bf16[1,4,32,512]{3,2,1,0:T(8,128)(2,1)S(1)}, bf16[1,4,32,512]{3,2,1,0:T(8,128)(2,1)S(1)}, u32[]{:S(2)}, u32[]{:S(2)}) collective-permute-start(bf16[1,4,32,512]{3,2,1,0:T(8,128)(2,1)S(1)} %get-tuple-element.214), channel_id=1, source_target_pairs={{0,0},{1,4},{2,8},{3,12},{4,3},{5,7},{6,11},{7,15},{8,2},{9,6},{10... | collective-permute-start | bytes 393224 | tf_op jit(solution)/shard_map/ppermute | solution.py:560

commit v5 on v4

--- a/solution.py
+++ b/solution.py
@@ -517,9 +517,10 @@
             )
         outs[h] = o0, o2, first_message
         came[h] = send(outs[h])
-    others = masked(1, 5, 1)
     for h in every:
         terms[h] = add(outs[h], came[h])
+        if h == 0:
+            others = masked(1, 5, 1)
     for h in every:
         early(h)
     for h in every:

time: 101 us -> 100 us (0.990)
  waiting for transfers between devices: 52.5 us -> 51.3 us
    ppermute x28, waiting for transfers between devices: 40.7 us -> 38.2 us  [swap(): return lax.ppermute(value, axis, [(i, i ^ k) for i in range(4)])]
    ppermute x2, waiting for transfers between devices: 2.74 us -> 3.89 us  [shards(): terms[h] = (total, lax.ppermute(total, 'layer', [(0, 1), (1, 0)]))]
  transfers between devices with their start and end apart: 33 -> 33, of which waited for: 26 -> 25; matrix products, arithmetic and copies ran while one was open for 1% -> 1% of each run, Pallas kernels for 13% -> 13%
where the time goes in v5:
time: 100 us; the launch traced here: 99.9 us
  waiting for transfers between devices  51.3 us (51%)
  starting transfers between devices  29.5 us (30%)
  Pallas kernels  15.4 us (15%)
  local copies, waits for them, and re-layouts  2.69 us (3%)
    ppermute x28, waiting for transfers between devices, swap(): return lax.ppermute(value, axis, [(i, i ^ k) for i in range(4)])  38.2 us
    ppermute x28, starting transfers between devices, swap(): return lax.ppermute(value, axis, [(i, i ^ k) for i in range(4)])  16.6 us
    pallas_call x35, Pallas kernels, call(): pl.pallas_call(kernel, out_shape=[jax.ShapeDtypeStruct(shape, dtype) for...  15.4 us
    ppermute x1, waiting for transfers between devices, shards(): root_out = lax.ppermute(root_rows, both, back[0])  7.61 us
    ppermute x1, starting transfers between devices, shards(): side = lax.ppermute(side, both, turn)  5.41 us
    ppermute x2, waiting for transfers between devices, shards(): terms[h] = (total, lax.ppermute(total, 'layer', [(0, 1), (1, 0)]))  3.89 us
    ppermute x1, starting transfers between devices, shards(): forest_out = lax.ppermute(forest_rows, both, back[0])  3.12 us
    ppermute x1, starting transfers between devices, shards(): root_out = lax.ppermute(root_rows, both, back[0])  2.44 us
  transfers between devices with their start and end apart: 33, of which 25 were waited for; matrix products, arithmetic and copies ran while one was open for 1% of the time, Pallas kernels for 13%

profile of v5, /device:TPU:6, one launch (start us, length us, event | category | flops | bytes accessed | tf_op | source)
XLA Modules:
  0.0 99.9 jit_solution(12117880348225630639)
XLA Ops:
  0.7 2.1 %shard_map.77 = (bf16[2,4,32,256]{3,2,1,0:T(8,128)(2,1)}, bf16[352,512]{1,0:T(8,128)(2,1)}, bf16[352,512]{1,0:T(8,128)(2,1)}, bf16[256,512]{1,0:T(8,128)(2,1)}) custom-call(bf16[3,4,32,512]{3,2,1,0:T(8,128)(2,1)} %bitcast.10, bf16[4,32,512]{2,1,0:T(8,128)(2,1)} %bitcast.12, f32[3,128,128]{2,1,0:T(8,128)} %bitcast.11, f32[128,128]{1,0:T(8,128)} %bitcast.13), custom_call_target="tpu_custom_call" | custom-call | bytes 7380000 | tf_op jit(solution)/shard_map/pallas_call | solution.py:29
  3.5 5.4 %collective-permute-start = (bf16[2,4,32,256]{3,2,1,0:T(8,128)(2,1)}, bf16[2,4,32,256]{3,2,1,0:T(8,128)(2,1)}, u32[]{:S(2)}, u32[]{:S(2)}) collective-permute-start(bf16[2,4,32,256]{3,2,1,0:T(8,128)(2,1)} %get-tuple-element.110), channel_id=1, source_target_pairs={{0,0},{1,4},{2,8},{3,12},{4,1},{5,5},{6,9},{7,13},{8,2},{9,6},{10,... | collective-permute-start | bytes 393224 | tf_op jit(solution)/shard_map/ppermute | solution.py:399
  8.9 1.2 %collective-permute-start.5 = (bf16[352,512]{1,0:T(8,128)(2,1)}, bf16[352,512]{1,0:T(8,128)(2,1)S(1)}, u32[]{:S(2)}, u32[]{:S(2)}) collective-permute-start(bf16[352,512]{1,0:T(8,128)(2,1)} %get-tuple-element.115), channel_id=1, source_target_pairs={{0,4},{4,0},{8,12},{12,8},{1,5},{5,1},{9,13},{13,9},{2,6},{6,2},{1... | collective-permute-start | bytes 1081352 | tf_op jit(solution)/shard_map/ppermute | solution.py:341
  10.1 0.8 copy.8.refs_0_
  10.9 1.9 %copy-done.1 = bf16[1,6,1,1,4,4,128,128]{7,6,5,4,3,2,1,0:T(8,128)(2,1)S(1)} copy-done((bf16[1,6,1,1,4,4,128,128]{7,6,5,4,3,2,1,0:T(8,128)(2,1)S(1)}, bf16[1,6,1,1,4,4,128,128]{7,6,5,4,3,2,1,0:T(8,128)(2,1)}, u32[]{:S(2)}) %copy-start.1) | copy-done | bytes 3145752
  12.8 1.8 %shard_map.78 = (bf16[6,4,128,512]{3,2,1,0:T(8,128)(2,1)S(1)}, f32[8,128]{1,0:T(8,128)S(1)}) custom-call(s32[6,4,4]{2,1,0:T(4,128)S(1)} %copy.8.refs_0_, bf16[6,4,4,128,128]{4,3,2,1,0:T(8,128)(2,1)S(1)} %bitcast.9), custom_call_target="tpu_custom_call" | custom-call | bytes 6641999 | tf_op jit(solution)/shard_map/pallas_call | solution.py:29
  14.6 1.6 %collective-permute-done.refs_0_ = bf16[2,4,32,256]{3,2,1,0:T(8,128)(2,1)} collective-permute-done((bf16[2,4,32,256]{3,2,1,0:T(8,128)(2,1)}, bf16[2,4,32,256]{3,2,1,0:T(8,128)(2,1)}, u32[]{:S(2)}, u32[]{:S(2)}) %collective-permute-start) | collective-permute-done | bytes 131104 | tf_op jit(solution)/shard_map/ppermute | solution.py:399
  16.7 1.0 %collective-permute-done.7.refs_0_ = s32[6,4,4]{2,1,0:T(4,128)S(1)} collective-permute-done((s32[6,4,4]{2,1,0:T(4,128)S(1)}, s32[6,4,4]{2,1,0:T(4,128)S(1)}, u32[]{:S(2)}, u32[]{:S(2)}) %collective-permute-start.7) | collective-permute-done | bytes 416 | tf_op jit(solution)/shard_map/ppermute | solution.py:341
  17.9 3.5 %collective-permute-done.3.refs_2_ = bf16[2,4,32,256]{3,2,1,0:T(8,128)(2,1)S(1)} collective-permute-done((bf16[2,4,32,256]{3,2,1,0:T(8,128)(2,1)}, bf16[2,4,32,256]{3,2,1,0:T(8,128)(2,1)S(1)}, u32[]{:S(2)}, u32[]{:S(2)}) %collective-permute-start.3) | collective-permute-done | bytes 131104 | tf_op jit(solution)/shard_map/ppermute | solution.py:341
  21.4 0.9 shard_map.79
  22.7 1.7 %shard_map.80 = (bf16[512,128]{1,0:T(8,128)(2,1)S(1)}, bf16[512,128]{1,0:T(8,128)(2,1)S(1)}, bf16[3,2,4,32,256]{4,3,2,1,0:T(8,128)(2,1)S(1)}, f32[256,128]{1,0:T...) custom-call(bf16[2,4,32,256]{3,2,1,0:T(8,128)(2,1)} %collective-permute-done.refs_0_, ...), custom_call_target="tpu_custom_call" | custom-call | bytes 5535000 | tf_op jit(solution)/shard_map/pallas_call | solution.py:29
  24.5 0.7 collective-permute-start.9
  25.6 1.5 %collective-permute-start.10 = (bf16[512,128]{1,0:T(8,128)(2,1)S(1)}, bf16[512,128]{1,0:T(8,128)(2,1)S(1)}, u32[]{:S(2)}, u32[]{:S(2)}) collective-permute-start(bf16[512,128]{1,0:T(8,128)(2,1)S(1)} %get-tuple-element.131), channel_id=1, source_target_pairs={{0,1},{1,0},{2,3},{3,2},{4,5},{5,4},{6,7},{7,6},{8,9},{9,8},{10,11... | collective-permute-start | bytes 393224 | tf_op jit(solution)/shard_map/ppermute | solution.py:341
  27.1 3.8 %collective-permute-done.9.refs_1_ = bf16[512,128]{1,0:T(8,128)(2,1)S(1)} collective-permute-done((bf16[512,128]{1,0:T(8,128)(2,1)S(1)}, bf16[512,128]{1,0:T(8,128)(2,1)S(1)}, u32[]{:S(2)}, u32[]{:S(2)}) %collective-permute-start.9) | collective-permute-done | bytes 131104 | tf_op jit(solution)/shard_map/ppermute | solution.py:341
  31.2 1.6 %shard_map.83 = (bf16[5,4,128,512]{3,2,1,0:T(8,128)(2,1)S(1)}, f32[8,128]{1,0:T(8,128)S(1)}) custom-call(s32[6,4,4]{2,1,0:T(4,128)S(1)} %collective-permute-done.7.refs_0_, bf16[6,4,4,128,128]{4,3,2,1,0:T(8,128)(2,1)S(1)} %collective-permute-done.8.refs_1_, f32[8,128]{1,0:T(8,128)S(1)} %get-tuple-element.128.refs_2_), custom_call_target="tpu_custom_call" | custom-call | bytes 5535000 | tf_op jit(solution)/shard_map/pallas_call | solution.py:29
  32.9 2.7 %collective-permute-start.13 = (bf16[256,128]{1,0:T(8,128)(2,1)S(1)}, bf16[256,128]{1,0:T(8,128)(2,1)S(1)}, u32[]{:S(2)}, u32[]{:S(2)}) collective-permute-start(bf16[256,128]{1,0:T(8,128)(2,1)S(1)} %get-tuple-element.145), channel_id=1, source_target_pairs={{0,2},{1,3},{2,0},{3,1},{4,6},{5,7},{6,4},{7,5},{8,10},{9,11},{10,... | collective-permute-start | bytes 196616 | tf_op jit(solution)/shard_map/ppermute | solution.py:341
  35.6 0.8 shard_map.85
  36.4 0.8 shard_map.86
  37.1 0.9 collective-permute-done.11.refs_2_
  38.4 1.3 %collective-permute-done.13.refs_2_ = bf16[256,128]{1,0:T(8,128)(2,1)S(1)} collective-permute-done((bf16[256,128]{1,0:T(8,128)(2,1)S(1)}, bf16[256,128]{1,0:T(8,128)(2,1)S(1)}, u32[]{:S(2)}, u32[]{:S(2)}) %collective-permute-start.13) | collective-permute-done | bytes 65568 | tf_op jit(solution)/shard_map/ppermute | solution.py:341
  39.9 0.8 collective-permute-start.14
  40.7 2.1 %collective-permute-done.12.refs_1_ = bf16[256,128]{1,0:T(8,128)(2,1)S(1)} collective-permute-done((bf16[256,128]{1,0:T(8,128)(2,1)S(1)}, bf16[256,128]{1,0:T(8,128)(2,1)S(1)}, u32[]{:S(2)}, u32[]{:S(2)}) %collective-permute-start.12) | collective-permute-done | bytes 65568 | tf_op jit(solution)/shard_map/ppermute | solution.py:341
  43.3 0.9 collective-permute-done.14.refs_1_
  44.6 1.2 %collective-permute-start.15 = (bf16[512,128]{1,0:T(8,128)(2,1)S(1)}, bf16[512,128]{1,0:T(8,128)(2,1)S(1)}, u32[]{:S(2)}, u32[]{:S(2)}) collective-permute-start(bf16[512,128]{1,0:T(8,128)(2,1)S(1)} %get-tuple-element.154), channel_id=1, source_target_pairs={{0,1},{1,0},{2,3},{3,2},{4,5},{5,4},{6,7},{7,6},{8,9},{9,8},{10,11... | collective-permute-start | bytes 393224 | tf_op jit(solution)/shard_map/ppermute | solution.py:341
  45.9 3.2 %collective-permute-done.16.refs_1_ = bf16[512,128]{1,0:T(8,128)(2,1)S(1)} collective-permute-done((bf16[512,128]{1,0:T(8,128)(2,1)S(1)}, bf16[512,128]{1,0:T(8,128)(2,1)S(1)}, u32[]{:S(2)}, u32[]{:S(2)}) %collective-permute-start.16) | collective-permute-done | bytes 131104 | tf_op jit(solution)/shard_map/ppermute | solution.py:341
  49.3 1.2 %collective-permute-done.15.refs_1_ = bf16[512,128]{1,0:T(8,128)(2,1)S(1)} collective-permute-done((bf16[512,128]{1,0:T(8,128)(2,1)S(1)}, bf16[512,128]{1,0:T(8,128)(2,1)S(1)}, u32[]{:S(2)}, u32[]{:S(2)}) %collective-permute-start.15) | collective-permute-done | bytes 131104 | tf_op jit(solution)/shard_map/ppermute | solution.py:341
  50.5 1.7 %collective-permute-start.19 = (bf16[256,128]{1,0:T(8,128)(2,1)S(1)}, bf16[256,128]{1,0:T(8,128)(2,1)S(1)}, u32[]{:S(2)}, u32[]{:S(2)}) collective-permute-start(bf16[256,128]{1,0:T(8,128)(2,1)S(1)} %get-tuple-element.173), channel_id=1, source_target_pairs={{0,2},{1,3},{2,0},{3,1},{4,6},{5,7},{6,4},{7,5},{8,10},{9,11},{10,... | collective-permute-start | bytes 196616 | tf_op jit(solution)/shard_map/ppermute | solution.py:341
  53.1 1.7 %collective-permute-done.17.refs_2_ = bf16[256,128]{1,0:T(8,128)(2,1)S(1)} collective-permute-done((bf16[256,128]{1,0:T(8,128)(2,1)S(1)}, bf16[256,128]{1,0:T(8,128)(2,1)S(1)}, u32[]{:S(2)}, u32[]{:S(2)}) %collective-permute-start.17) | collective-permute-done | bytes 65568 | tf_op jit(solution)/shard_map/ppermute | solution.py:341
  55.6 0.7 collective-permute-done.19.refs_2_
  56.5 0.9 collective-permute-start.20
  57.4 1.9 %collective-permute-done.18.refs_1_ = bf16[256,128]{1,0:T(8,128)(2,1)S(1)} collective-permute-done((bf16[256,128]{1,0:T(8,128)(2,1)S(1)}, bf16[256,128]{1,0:T(8,128)(2,1)S(1)}, u32[]{:S(2)}, u32[]{:S(2)}) %collective-permute-start.18) | collective-permute-done | bytes 65568 | tf_op jit(solution)/shard_map/ppermute | solution.py:341
  59.9 1.0 %collective-permute-done.20.refs_1_ = bf16[256,128]{1,0:T(8,128)(2,1)S(1)} collective-permute-done((bf16[256,128]{1,0:T(8,128)(2,1)S(1)}, bf16[256,128]{1,0:T(8,128)(2,1)S(1)}, u32[]{:S(2)}, u32[]{:S(2)}) %collective-permute-start.20) | collective-permute-done | bytes 65568 | tf_op jit(solution)/shard_map/ppermute | solution.py:341
  61.6 1.1 %collective-permute-start.24 = (bf16[512,128]{1,0:T(8,128)(2,1)S(1)}, bf16[512,128]{1,0:T(8,128)(2,1)S(1)}, u32[]{:S(2)}, u32[]{:S(2)}) collective-permute-start(bf16[512,128]{1,0:T(8,128)(2,1)S(1)} %get-tuple-element.196), channel_id=1, source_target_pairs={{0,1},{1,0},{2,3},{3,2},{4,5},{5,4},{6,7},{7,6},{8,9},{9,8},{10,11... | collective-permute-start | bytes 393224 | tf_op jit(solution)/shard_map/ppermute | solution.py:341
  62.6 2.3 %collective-permute-done.22.refs_1_ = bf16[512,128]{1,0:T(8,128)(2,1)S(1)} collective-permute-done((bf16[512,128]{1,0:T(8,128)(2,1)S(1)}, bf16[512,128]{1,0:T(8,128)(2,1)S(1)}, u32[]{:S(2)}, u32[]{:S(2)}) %collective-permute-start.22) | collective-permute-done | bytes 131104 | tf_op jit(solution)/shard_map/ppermute | solution.py:341
  65.0 3.3 %collective-permute-done.24.refs_1_ = bf16[512,128]{1,0:T(8,128)(2,1)S(1)} collective-permute-done((bf16[512,128]{1,0:T(8,128)(2,1)S(1)}, bf16[512,128]{1,0:T(8,128)(2,1)S(1)}, u32[]{:S(2)}, u32[]{:S(2)}) %collective-permute-start.24) | collective-permute-done | bytes 131104 | tf_op jit(solution)/shard_map/ppermute | solution.py:341
  68.3 0.8 collective-permute-start.27
  69.1 1.1 %collective-permute-done.23.refs_2_ = bf16[256,128]{1,0:T(8,128)(2,1)S(1)} collective-permute-done((bf16[256,128]{1,0:T(8,128)(2,1)S(1)}, bf16[256,128]{1,0:T(8,128)(2,1)S(1)}, u32[]{:S(2)}, u32[]{:S(2)}) %collective-permute-start.23) | collective-permute-done | bytes 65568 | tf_op jit(solution)/shard_map/ppermute | solution.py:341
  70.3 3.1 %collective-permute-start.25 = (bf16[3,4,32,512]{3,2,1,0:T(8,128)(2,1)S(1)}, bf16[3,4,32,512]{3,2,1,0:T(8,128)(2,1)S(1)}, u32[]{:S(2)}, u32[]{:S(2)}) collective-permute-start(bf16[3,4,32,512]{3,2,1,0:T(8,128)(2,1)S(1)} %get-tuple-element.200), channel_id=1, source_target_pairs={{0,0},{1,4},{2,8},{3,12},{4,3},{5,7},{6,11},{7,15},{8,2},{9,6},{10... | collective-permute-start | bytes 1179656 | tf_op jit(solution)/shard_map/ppermute | solution.py:555
  74.3 1.3 %collective-permute-start.29 = (bf16[256,128]{1,0:T(8,128)(2,1)S(1)}, bf16[256,128]{1,0:T(8,128)(2,1)S(1)}, u32[]{:S(2)}, u32[]{:S(2)}) collective-permute-start(bf16[256,128]{1,0:T(8,128)(2,1)S(1)} %get-tuple-element.207.refs_0_), channel_id=1, source_target_pairs={{0,16},{16,0},{1,17},{17,1},{2,18},{18,2},{3,19},{19,3},{4,20},{20... | collective-permute-start | bytes 196616 | tf_op jit(solution)/shard_map/ppermute | solution.py:552
  75.6 2.8 %collective-permute-done.26.refs_1_ = bf16[256,128]{1,0:T(8,128)(2,1)S(1)} collective-permute-done((bf16[256,128]{1,0:T(8,128)(2,1)S(1)}, bf16[256,128]{1,0:T(8,128)(2,1)S(1)}, u32[]{:S(2)}, u32[]{:S(2)}) %collective-permute-start.26) | collective-permute-done | bytes 65568 | tf_op jit(solution)/shard_map/ppermute | solution.py:552
  78.8 1.1 %collective-permute-done.29.refs_1_ = bf16[256,128]{1,0:T(8,128)(2,1)S(1)} collective-permute-done((bf16[256,128]{1,0:T(8,128)(2,1)S(1)}, bf16[256,128]{1,0:T(8,128)(2,1)S(1)}, u32[]{:S(2)}, u32[]{:S(2)}) %collective-permute-start.29) | collective-permute-done | bytes 65568 | tf_op jit(solution)/shard_map/ppermute | solution.py:552
  80.1 1.0 %collective-permute-start.30 = (bf16[256,128]{1,0:T(8,128)(2,1)S(1)}, bf16[256,128]{1,0:T(8,128)(2,1)S(1)}, u32[]{:S(2)}, u32[]{:S(2)}) collective-permute-start(bf16[256,128]{1,0:T(8,128)(2,1)S(1)} %get-tuple-element.209.refs_2_), channel_id=1, source_target_pairs={{0,8},{4,12},{8,0},{12,4},{1,9},{5,13},{9,1},{13,5},{2,10},{6,14},... | collective-permute-start | bytes 196616 | tf_op jit(solution)/shard_map/ppermute | solution.py:341
  81.1 5.2 %collective-permute-done.28.refs_1_ = bf16[256,128]{1,0:T(8,128)(2,1)S(1)} collective-permute-done((bf16[256,128]{1,0:T(8,128)(2,1)S(1)}, bf16[256,128]{1,0:T(8,128)(2,1)S(1)}, u32[]{:S(2)}, u32[]{:S(2)}) %collective-permute-start.28) | collective-permute-done | bytes 65568 | tf_op jit(solution)/shard_map/ppermute | solution.py:341
  86.3 1.3 %collective-permute-done.30.refs_3_ = bf16[256,128]{1,0:T(8,128)(2,1)S(1)} collective-permute-done((bf16[256,128]{1,0:T(8,128)(2,1)S(1)}, bf16[256,128]{1,0:T(8,128)(2,1)S(1)}, u32[]{:S(2)}, u32[]{:S(2)}) %collective-permute-start.30) | collective-permute-done | bytes 65568 | tf_op jit(solution)/shard_map/ppermute | solution.py:341
  87.7 1.2 %collective-permute-done.31.refs_1_ = bf16[1,4,32,256]{3,2,1,0:T(8,128)(2,1)S(1)} collective-permute-done((bf16[1,4,32,256]{3,2,1,0:T(8,128)(2,1)S(1)}, bf16[1,4,32,256]{3,2,1,0:T(8,128)(2,1)S(1)}, u32[]{:S(2)}, u32[]{:S(2)}) %collective-permute-start.31) | collective-permute-done | bytes 65568 | tf_op jit(solution)/shard_map/ppermute | solution.py:341
  89.0 2.4 %collective-permute-start.32 = (bf16[1,4,32,512]{3,2,1,0:T(8,128)(2,1)S(1)}, bf16[1,4,32,512]{3,2,1,0:T(8,128)(2,1)S(1)}, u32[]{:S(2)}, u32[]{:S(2)}) collective-permute-start(bf16[1,4,32,512]{3,2,1,0:T(8,128)(2,1)S(1)} %get-tuple-element.214), channel_id=1, source_target_pairs={{0,0},{1,4},{2,8},{3,12},{4,3},{5,7},{6,11},{7,15},{8,2},{9,6},{10... | collective-permute-start | bytes 393224 | tf_op jit(solution)/shard_map/ppermute | solution.py:561
  91.4 7.6 %collective-permute-done.32.refs_1_ = bf16[1,4,32,512]{3,2,1,0:T(8,128)(2,1)S(1)} collective-permute-done((bf16[1,4,32,512]{3,2,1,0:T(8,128)(2,1)S(1)}, bf16[1,4,32,512]{3,2,1,0:T(8,128)(2,1)S(1)}, u32[]{:S(2)}, u32[]{:S(2)}) %collective-permute-start.32) | collective-permute-done | bytes 131104 | tf_op jit(solution)/shard_map/ppermute | solution.py:561
  99.1 0.8 shard_map.111
  (58 shorter events, 9.2 us)
Async XLA Ops:
  0.6 20.7 %collective-permute-start.8 = (bf16[6,4,4,128,128]{4,3,2,1,0:T(8,128)(2,1)}, bf16[6,4,4,128,128]{4,3,2,1,0:T(8,128)(2,1)S(1)}, u32[]{:S(2)}, u32[]{:S(2)}) collective-permute-start(bf16[6,4,4,128,128]{4,3,2,1,0:T(8,128)(2,1)} %bitcast.8), channel_id=1, source_target_pairs={{0,4},{4,0},{8,12},{12,8},{1,5},{5,1},{9,13},{13,9},{2,6},{6,2},{1... | collective-permute-start | bytes 9437192 | tf_op jit(solution)/shard_map/ppermute | solution.py:341
  2.9 13.3 %collective-permute-start.1 = (bf16[256,512]{1,0:T(8,128)(2,1)}, bf16[256,512]{1,0:T(8,128)(2,1)}, u32[]{:S(2)}, u32[]{:S(2)}) collective-permute-start(bf16[256,512]{1,0:T(8,128)(2,1)} %get-tuple-element.111), channel_id=1, source_target_pairs={{0,8},{4,12},{8,0},{12,4},{1,9},{5,13},{9,1},{13,5},{2,10},{6,14},... | collective-permute-start | bytes 786440 | tf_op jit(solution)/shard_map/ppermute | solution.py:341
  3.5 12.7 %collective-permute-start = (bf16[2,4,32,256]{3,2,1,0:T(8,128)(2,1)}, bf16[2,4,32,256]{3,2,1,0:T(8,128)(2,1)}, u32[]{:S(2)}, u32[]{:S(2)}) collective-permute-start(bf16[2,4,32,256]{3,2,1,0:T(8,128)(2,1)} %get-tuple-element.110), channel_id=1, source_target_pairs={{0,0},{1,4},{2,8},{3,12},{4,1},{5,5},{6,9},{7,13},{8,2},{9,6},{10,... | collective-permute-start | bytes 393224 | tf_op jit(solution)/shard_map/ppermute | solution.py:399
  8.9 13.4 %collective-permute-start.5 = (bf16[352,512]{1,0:T(8,128)(2,1)}, bf16[352,512]{1,0:T(8,128)(2,1)S(1)}, u32[]{:S(2)}, u32[]{:S(2)}) collective-permute-start(bf16[352,512]{1,0:T(8,128)(2,1)} %get-tuple-element.115), channel_id=1, source_target_pairs={{0,4},{4,0},{8,12},{12,8},{1,5},{5,1},{9,13},{13,9},{2,6},{6,2},{1... | collective-permute-start | bytes 1081352 | tf_op jit(solution)/shard_map/ppermute | solution.py:341
  10.9 1.9 %copy-start.1 = (bf16[1,6,1,1,4,4,128,128]{7,6,5,4,3,2,1,0:T(8,128)(2,1)S(1)}, bf16[1,6,1,1,4,4,128,128]{7,6,5,4,3,2,1,0:T(8,128)(2,1)}, u32[]{:S(2)}) copy-start(bf16[1,6,1,1,4,4,128,128]{7,6,5,4,3,2,1,0:T(8,128)(2,1)} %param.8) | copy-start | bytes 9437188
  12.8 9.9 %copy-start = (bf16[352,512]{1,0:T(8,128)(2,1)S(1)}, bf16[352,512]{1,0:T(8,128)(2,1)}, u32[]{:S(2)}) copy-start(bf16[352,512]{1,0:T(8,128)(2,1)} %get-tuple-element.114.refs_4_.refs_3_.refs_2_) | copy-start | bytes 1081348
  16.2 5.2 %collective-permute-start.3 = (bf16[2,4,32,256]{3,2,1,0:T(8,128)(2,1)}, bf16[2,4,32,256]{3,2,1,0:T(8,128)(2,1)S(1)}, u32[]{:S(2)}, u32[]{:S(2)}) collective-permute-start(bf16[2,4,32,256]{3,2,1,0:T(8,128)(2,1)} %collective-permute-done.refs_0_), channel_id=1, source_target_pairs={{0,8},{4,12},{8,0},{12,4},{1,9},{5,13},{9,1},{13,5},{2,10},{6,14},... | collective-permute-start | bytes 393224 | tf_op jit(solution)/shard_map/ppermute | solution.py:341
  16.2 6.5 %collective-permute-start.6 = (bf16[256,512]{1,0:T(8,128)(2,1)}, bf16[256,512]{1,0:T(8,128)(2,1)S(1)}, u32[]{:S(2)}, u32[]{:S(2)}) collective-permute-start(bf16[256,512]{1,0:T(8,128)(2,1)} %collective-permute-done.1.refs_6_), channel_id=1, source_target_pairs={{0,4},{4,0},{8,12},{12,8},{1,5},{5,1},{9,13},{13,9},{2,6},{6,2},{1... | collective-permute-start | bytes 786440 | tf_op jit(solution)/shard_map/ppermute | solution.py:341
  16.2 1.5 %collective-permute-start.7 = (s32[6,4,4]{2,1,0:T(4,128)S(1)}, s32[6,4,4]{2,1,0:T(4,128)S(1)}, u32[]{:S(2)}, u32[]{:S(2)}) collective-permute-start(s32[6,4,4]{2,1,0:T(4,128)S(1)} %copy.8.refs_0_), channel_id=1, source_target_pairs={{0,4},{4,0},{8,12},{12,8},{1,5},{5,1},{9,13},{13,9},{2,6},{6,2},{1... | collective-permute-start | bytes 1160 | tf_op jit(solution)/shard_map/ppermute | solution.py:341
  17.7 4.6 %collective-permute-start.2 = (bf16[2,4,32,256]{3,2,1,0:T(8,128)(2,1)}, bf16[2,4,32,256]{3,2,1,0:T(8,128)(2,1)S(1)}, u32[]{:S(2)}, u32[]{:S(2)}) collective-permute-start(bf16[2,4,32,256]{3,2,1,0:T(8,128)(2,1)} %collective-permute-done.refs_0_), channel_id=1, source_target_pairs={{0,4},{4,0},{8,12},{12,8},{1,5},{5,1},{9,13},{13,9},{2,6},{6,2},{1... | collective-permute-start | bytes 393224 | tf_op jit(solution)/shard_map/ppermute | solution.py:341
  21.4 1.3 %collective-permute-start.4 = (bf16[2,4,32,256]{3,2,1,0:T(8,128)(2,1)S(1)}, bf16[2,4,32,256]{3,2,1,0:T(8,128)(2,1)S(1)}, u32[]{:S(2)}, u32[]{:S(2)}) collective-permute-start(bf16[2,4,32,256]{3,2,1,0:T(8,128)(2,1)S(1)} %collective-permute-done.3.refs_2_), channel_id=1, source_target_pairs={{0,4},{4,0},{8,12},{12,8},{1,5},{5,1},{9,13},{13,9},{2,6},{6,2},{1... | collective-permute-start | bytes 393224 | tf_op jit(solution)/shard_map/ppermute | solution.py:341
  24.5 6.4 %collective-permute-start.9 = (bf16[512,128]{1,0:T(8,128)(2,1)S(1)}, bf16[512,128]{1,0:T(8,128)(2,1)S(1)}, u32[]{:S(2)}, u32[]{:S(2)}) collective-permute-start(bf16[512,128]{1,0:T(8,128)(2,1)S(1)} %get-tuple-element.124), channel_id=1, source_target_pairs={{0,1},{1,0},{2,3},{3,2},{4,5},{5,4},{6,7},{7,6},{8,9},{9,8},{10,11... | collective-permute-start | bytes 393224 | tf_op jit(solution)/shard_map/ppermute | solution.py:341
  25.6 7.3 %collective-permute-start.10 = (bf16[512,128]{1,0:T(8,128)(2,1)S(1)}, bf16[512,128]{1,0:T(8,128)(2,1)S(1)}, u32[]{:S(2)}, u32[]{:S(2)}) collective-permute-start(bf16[512,128]{1,0:T(8,128)(2,1)S(1)} %get-tuple-element.131), channel_id=1, source_target_pairs={{0,1},{1,0},{2,3},{3,2},{4,5},{5,4},{6,7},{7,6},{8,9},{9,8},{10,11... | collective-permute-start | bytes 393224 | tf_op jit(solution)/shard_map/ppermute | solution.py:341
  30.9 7.2 %collective-permute-start.11 = (bf16[256,128]{1,0:T(8,128)(2,1)S(1)}, bf16[256,128]{1,0:T(8,128)(2,1)S(1)}, u32[]{:S(2)}, u32[]{:S(2)}) collective-permute-start(bf16[256,128]{1,0:T(8,128)(2,1)S(1)} %get-tuple-element.140), channel_id=1, source_target_pairs={{0,2},{1,3},{2,0},{3,1},{4,6},{5,7},{6,4},{7,5},{8,10},{9,11},{10,... | collective-permute-start | bytes 196616 | tf_op jit(solution)/shard_map/ppermute | solution.py:341
  32.9 6.7 %collective-permute-start.13 = (bf16[256,128]{1,0:T(8,128)(2,1)S(1)}, bf16[256,128]{1,0:T(8,128)(2,1)S(1)}, u32[]{:S(2)}, u32[]{:S(2)}) collective-permute-start(bf16[256,128]{1,0:T(8,128)(2,1)S(1)} %get-tuple-element.145), channel_id=1, source_target_pairs={{0,2},{1,3},{2,0},{3,1},{4,6},{5,7},{6,4},{7,5},{8,10},{9,11},{10,... | collective-permute-start | bytes 196616 | tf_op jit(solution)/shard_map/ppermute | solution.py:341
  38.3 4.5 %collective-permute-start.12 = (bf16[256,128]{1,0:T(8,128)(2,1)S(1)}, bf16[256,128]{1,0:T(8,128)(2,1)S(1)}, u32[]{:S(2)}, u32[]{:S(2)}) collective-permute-start(bf16[256,128]{1,0:T(8,128)(2,1)S(1)} %get-tuple-element.142.refs_0_), channel_id=1, source_target_pairs={{0,8},{4,12},{8,0},{12,4},{1,9},{5,13},{9,1},{13,5},{2,10},{6,14},... | collective-permute-start | bytes 196616 | tf_op jit(solution)/shard_map/ppermute | solution.py:341
  39.9 4.3 %collective-permute-start.14 = (bf16[256,128]{1,0:T(8,128)(2,1)S(1)}, bf16[256,128]{1,0:T(8,128)(2,1)S(1)}, u32[]{:S(2)}, u32[]{:S(2)}) collective-permute-start(bf16[256,128]{1,0:T(8,128)(2,1)S(1)} %get-tuple-element.150.refs_0_), channel_id=1, source_target_pairs={{0,8},{4,12},{8,0},{12,4},{1,9},{5,13},{9,1},{13,5},{2,10},{6,14},... | collective-permute-start | bytes 196616 | tf_op jit(solution)/shard_map/ppermute | solution.py:341
  43.2 5.8 %collective-permute-start.16 = (bf16[512,128]{1,0:T(8,128)(2,1)S(1)}, bf16[512,128]{1,0:T(8,128)(2,1)S(1)}, u32[]{:S(2)}, u32[]{:S(2)}) collective-permute-start(bf16[512,128]{1,0:T(8,128)(2,1)S(1)} %get-tuple-element.156), channel_id=1, source_target_pairs={{0,1},{1,0},{2,3},{3,2},{4,5},{5,4},{6,7},{7,6},{8,9},{9,8},{10,11... | collective-permute-start | bytes 393224 | tf_op jit(solution)/shard_map/ppermute | solution.py:341
  44.6 5.8 %collective-permute-start.15 = (bf16[512,128]{1,0:T(8,128)(2,1)S(1)}, bf16[512,128]{1,0:T(8,128)(2,1)S(1)}, u32[]{:S(2)}, u32[]{:S(2)}) collective-permute-start(bf16[512,128]{1,0:T(8,128)(2,1)S(1)} %get-tuple-element.154), channel_id=1, source_target_pairs={{0,1},{1,0},{2,3},{3,2},{4,5},{5,4},{6,7},{7,6},{8,9},{9,8},{10,11... | collective-permute-start | bytes 393224 | tf_op jit(solution)/shard_map/ppermute | solution.py:341
  49.1 5.7 %collective-permute-start.17 = (bf16[256,128]{1,0:T(8,128)(2,1)S(1)}, bf16[256,128]{1,0:T(8,128)(2,1)S(1)}, u32[]{:S(2)}, u32[]{:S(2)}) collective-permute-start(bf16[256,128]{1,0:T(8,128)(2,1)S(1)} %get-tuple-element.168), channel_id=1, source_target_pairs={{0,2},{1,3},{2,0},{3,1},{4,6},{5,7},{6,4},{7,5},{8,10},{9,11},{10,... | collective-permute-start | bytes 196616 | tf_op jit(solution)/shard_map/ppermute | solution.py:341
  50.5 5.8 %collective-permute-start.19 = (bf16[256,128]{1,0:T(8,128)(2,1)S(1)}, bf16[256,128]{1,0:T(8,128)(2,1)S(1)}, u32[]{:S(2)}, u32[]{:S(2)}) collective-permute-start(bf16[256,128]{1,0:T(8,128)(2,1)S(1)} %get-tuple-element.173), channel_id=1, source_target_pairs={{0,2},{1,3},{2,0},{3,1},{4,6},{5,7},{6,4},{7,5},{8,10},{9,11},{10,... | collective-permute-start | bytes 196616 | tf_op jit(solution)/shard_map/ppermute | solution.py:341
  55.0 4.3 %collective-permute-start.18 = (bf16[256,128]{1,0:T(8,128)(2,1)S(1)}, bf16[256,128]{1,0:T(8,128)(2,1)S(1)}, u32[]{:S(2)}, u32[]{:S(2)}) collective-permute-start(bf16[256,128]{1,0:T(8,128)(2,1)S(1)} %get-tuple-element.170.refs_0_), channel_id=1, source_target_pairs={{0,8},{4,12},{8,0},{12,4},{1,9},{5,13},{9,1},{13,5},{2,10},{6,14},... | collective-permute-start | bytes 196616 | tf_op jit(solution)/shard_map/ppermute | solution.py:341
  56.5 4.3 %collective-permute-start.20 = (bf16[256,128]{1,0:T(8,128)(2,1)S(1)}, bf16[256,128]{1,0:T(8,128)(2,1)S(1)}, u32[]{:S(2)}, u32[]{:S(2)}) collective-permute-start(bf16[256,128]{1,0:T(8,128)(2,1)S(1)} %get-tuple-element.177.refs_0_), channel_id=1, source_target_pairs={{0,8},{4,12},{8,0},{12,4},{1,9},{5,13},{9,1},{13,5},{2,10},{6,14},... | collective-permute-start | bytes 196616 | tf_op jit(solution)/shard_map/ppermute | solution.py:341
  59.8 5.1 %collective-permute-start.22 = (bf16[512,128]{1,0:T(8,128)(2,1)S(1)}, bf16[512,128]{1,0:T(8,128)(2,1)S(1)}, u32[]{:S(2)}, u32[]{:S(2)}) collective-permute-start(bf16[512,128]{1,0:T(8,128)(2,1)S(1)} %get-tuple-element.191), channel_id=1, source_target_pairs={{0,1},{1,0},{2,3},{3,2},{4,5},{5,4},{6,7},{7,6},{8,9},{9,8},{10,11... | collective-permute-start | bytes 393224 | tf_op jit(solution)/shard_map/ppermute | solution.py:341
  61.5 8.8 %collective-permute-start.21 = (bf16[3,4,32,256]{3,2,1,0:T(8,128)(2,1)S(1)}, bf16[3,4,32,256]{3,2,1,0:T(8,128)(2,1)S(1)}, u32[]{:S(2)}, u32[]{:S(2)}) collective-permute-start(bf16[3,4,32,256]{3,2,1,0:T(8,128)(2,1)S(1)} %get-tuple-element.189), channel_id=1, source_target_pairs={{0,4},{4,0},{8,12},{12,8},{1,5},{5,1},{9,13},{13,9},{2,6},{6,2},{1... | collective-permute-start | bytes 589832 | tf_op jit(solution)/shard_map/ppermute | solution.py:341
  61.6 6.8 %collective-permute-start.24 = (bf16[512,128]{1,0:T(8,128)(2,1)S(1)}, bf16[512,128]{1,0:T(8,128)(2,1)S(1)}, u32[]{:S(2)}, u32[]{:S(2)}) collective-permute-start(bf16[512,128]{1,0:T(8,128)(2,1)S(1)} %get-tuple-element.196), channel_id=1, source_target_pairs={{0,1},{1,0},{2,3},{3,2},{4,5},{5,4},{6,7},{7,6},{8,9},{9,8},{10,11... | collective-permute-start | bytes 393224 | tf_op jit(solution)/shard_map/ppermute | solution.py:341
  64.9 5.3 %collective-permute-start.23 = (bf16[256,128]{1,0:T(8,128)(2,1)S(1)}, bf16[256,128]{1,0:T(8,128)(2,1)S(1)}, u32[]{:S(2)}, u32[]{:S(2)}) collective-permute-start(bf16[256,128]{1,0:T(8,128)(2,1)S(1)} %get-tuple-element.194), channel_id=1, source_target_pairs={{0,2},{1,3},{2,0},{3,1},{4,6},{5,7},{6,4},{7,5},{8,10},{9,11},{10,... | collective-permute-start | bytes 196616 | tf_op jit(solution)/shard_map/ppermute | solution.py:341
  68.3 5.9 %collective-permute-start.27 = (bf16[256,128]{1,0:T(8,128)(2,1)S(1)}, bf16[256,128]{1,0:T(8,128)(2,1)S(1)}, u32[]{:S(2)}, u32[]{:S(2)}) collective-permute-start(bf16[256,128]{1,0:T(8,128)(2,1)S(1)} %get-tuple-element.203), channel_id=1, source_target_pairs={{0,2},{1,3},{2,0},{3,1},{4,6},{5,7},{6,4},{7,5},{8,10},{9,11},{10,... | collective-permute-start | bytes 196616 | tf_op jit(solution)/shard_map/ppermute | solution.py:341
  70.3 28.8 %collective-permute-start.25 = (bf16[3,4,32,512]{3,2,1,0:T(8,128)(2,1)S(1)}, bf16[3,4,32,512]{3,2,1,0:T(8,128)(2,1)S(1)}, u32[]{:S(2)}, u32[]{:S(2)}) collective-permute-start(bf16[3,4,32,512]{3,2,1,0:T(8,128)(2,1)S(1)} %get-tuple-element.200), channel_id=1, source_target_pairs={{0,0},{1,4},{2,8},{3,12},{4,3},{5,7},{6,11},{7,15},{8,2},{9,6},{10... | collective-permute-start | bytes 1179656 | tf_op jit(solution)/shard_map/ppermute | solution.py:555
  73.4 5.0 %collective-permute-start.26 = (bf16[256,128]{1,0:T(8,128)(2,1)S(1)}, bf16[256,128]{1,0:T(8,128)(2,1)S(1)}, u32[]{:S(2)}, u32[]{:S(2)}) collective-permute-start(bf16[256,128]{1,0:T(8,128)(2,1)S(1)} %get-tuple-element.201.refs_0_), channel_id=1, source_target_pairs={{0,16},{16,0},{1,17},{17,1},{2,18},{18,2},{3,19},{19,3},{4,20},{20... | collective-permute-start | bytes 196616 | tf_op jit(solution)/shard_map/ppermute | solution.py:552
  74.3 5.5 %collective-permute-start.29 = (bf16[256,128]{1,0:T(8,128)(2,1)S(1)}, bf16[256,128]{1,0:T(8,128)(2,1)S(1)}, u32[]{:S(2)}, u32[]{:S(2)}) collective-permute-start(bf16[256,128]{1,0:T(8,128)(2,1)S(1)} %get-tuple-element.207.refs_0_), channel_id=1, source_target_pairs={{0,16},{16,0},{1,17},{17,1},{2,18},{18,2},{3,19},{19,3},{4,20},{20... | collective-permute-start | bytes 196616 | tf_op jit(solution)/shard_map/ppermute | solution.py:552
  78.7 7.6 %collective-permute-start.28 = (bf16[256,128]{1,0:T(8,128)(2,1)S(1)}, bf16[256,128]{1,0:T(8,128)(2,1)S(1)}, u32[]{:S(2)}, u32[]{:S(2)}) collective-permute-start(bf16[256,128]{1,0:T(8,128)(2,1)S(1)} %get-tuple-element.206.refs_0_), channel_id=1, source_target_pairs={{0,8},{4,12},{8,0},{12,4},{1,9},{5,13},{9,1},{13,5},{2,10},{6,14},... | collective-permute-start | bytes 196616 | tf_op jit(solution)/shard_map/ppermute | solution.py:341
  80.1 7.6 %collective-permute-start.30 = (bf16[256,128]{1,0:T(8,128)(2,1)S(1)}, bf16[256,128]{1,0:T(8,128)(2,1)S(1)}, u32[]{:S(2)}, u32[]{:S(2)}) collective-permute-start(bf16[256,128]{1,0:T(8,128)(2,1)S(1)} %get-tuple-element.209.refs_2_), channel_id=1, source_target_pairs={{0,8},{4,12},{8,0},{12,4},{1,9},{5,13},{9,1},{13,5},{2,10},{6,14},... | collective-permute-start | bytes 196616 | tf_op jit(solution)/shard_map/ppermute | solution.py:341
  87.6 1.3 %collective-permute-start.31 = (bf16[1,4,32,256]{3,2,1,0:T(8,128)(2,1)S(1)}, bf16[1,4,32,256]{3,2,1,0:T(8,128)(2,1)S(1)}, u32[]{:S(2)}, u32[]{:S(2)}) collective-permute-start(bf16[1,4,32,256]{3,2,1,0:T(8,128)(2,1)S(1)} %get-tuple-element.212), channel_id=1, source_target_pairs={{0,4},{4,0},{8,12},{12,8},{1,5},{5,1},{9,13},{13,9},{2,6},{6,2},{1... | collective-permute-start | bytes 196616 | tf_op jit(solution)/shard_map/ppermute | solution.py:341
  89.0 10.1 %collective-permute-start.32 = (bf16[1,4,32,512]{3,2,1,0:T(8,128)(2,1)S(1)}, bf16[1,4,32,512]{3,2,1,0:T(8,128)(2,1)S(1)}, u32[]{:S(2)}, u32[]{:S(2)}) collective-permute-start(bf16[1,4,32,512]{3,2,1,0:T(8,128)(2,1)S(1)} %get-tuple-element.214), channel_id=1, source_target_pairs={{0,0},{1,4},{2,8},{3,12},{4,3},{5,7},{6,11},{7,15},{8,2},{9,6},{10... | collective-permute-start | bytes 393224 | tf_op jit(solution)/shard_map/ppermute | solution.py:561

commit v6 on v5

--- a/solution.py
+++ b/solution.py
@@ -529,7 +529,6 @@
         middle(h, 3, acc2)
     for h in every:
         terms[h] = add(outs[h], came[h])
-    for h in every:
         later(h)
     for h in every:
         pieces[h] = solve(2, *terms[h])

time: 100 us -> 101 us (1.010)
  starting transfers between devices: 29.5 us -> 31.5 us
  waiting for transfers between devices: 51.3 us -> 50.1 us
    ppermute x28, starting transfers between devices: 16.6 us -> 18.3 us  [swap(): return lax.ppermute(value, axis, [(i, i ^ k) for i in range(4)])]
  transfers between devices with their start and end apart: 33 -> 33, of which waited for: 25 -> 24; matrix products, arithmetic and copies ran while one was open for 1% -> 1% of each run, Pallas kernels for 13% -> 13%
where the time goes in v6:
time: 101 us
  waiting for transfers between devices  50.1 us (50%)
  starting transfers between devices  31.5 us (31%)
  Pallas kernels  15.4 us (15%)
  local copies, waits for them, and re-layouts  2.69 us (3%)
    ppermute x28, waiting for transfers between devices, swap(): return lax.ppermute(value, axis, [(i, i ^ k) for i in range(4)])  37.9 us
    ppermute x28, starting transfers between devices, swap(): return lax.ppermute(value, axis, [(i, i ^ k) for i in range(4)])  18.3 us
    pallas_call x35, Pallas kernels, call(): pl.pallas_call(kernel, out_shape=[jax.ShapeDtypeStruct(shape, dtype) for...  15.4 us
    ppermute x1, waiting for transfers between devices, shards(): root_out = lax.ppermute(root_rows, both, back[0])  7.46 us
    ppermute x1, starting transfers between devices, shards(): side = lax.ppermute(side, both, turn)  5.41 us
    ppermute x2, waiting for transfers between devices, shards(): terms[h] = (total, lax.ppermute(total, 'layer', [(0, 1), (1, 0)]))  3.13 us
    ppermute x1, starting transfers between devices, shards(): forest_out = lax.ppermute(forest_rows, both, back[0])  2.97 us
    ppermute x1, starting transfers between devices, shards(): root_out = lax.ppermute(root_rows, both, back[0])  2.59 us
  transfers between devices with their start and end apart: 33, of which 24 were waited for; matrix products, arithmetic and copies ran while one was open for 1% of the time, Pallas kernels for 13%

profile of v6, /device:TPU:6, one launch (start us, length us, event | category | flops | bytes accessed | tf_op | source)
XLA Modules:
  0.0 100.6 jit_solution(8639438314528069587)
XLA Ops:
  0.7 2.1 %shard_map.77 = (bf16[2,4,32,256]{3,2,1,0:T(8,128)(2,1)}, bf16[352,512]{1,0:T(8,128)(2,1)}, bf16[352,512]{1,0:T(8,128)(2,1)}, bf16[256,512]{1,0:T(8,128)(2,1)}) custom-call(bf16[3,4,32,512]{3,2,1,0:T(8,128)(2,1)} %bitcast.10, bf16[4,32,512]{2,1,0:T(8,128)(2,1)} %bitcast.12, f32[3,128,128]{2,1,0:T(8,128)} %bitcast.11, f32[128,128]{1,0:T(8,128)} %bitcast.13), custom_call_target="tpu_custom_call" | custom-call | bytes 7380000 | tf_op jit(solution)/shard_map/pallas_call | solution.py:29
  3.5 5.4 %collective-permute-start = (bf16[2,4,32,256]{3,2,1,0:T(8,128)(2,1)}, bf16[2,4,32,256]{3,2,1,0:T(8,128)(2,1)}, u32[]{:S(2)}, u32[]{:S(2)}) collective-permute-start(bf16[2,4,32,256]{3,2,1,0:T(8,128)(2,1)} %get-tuple-element.110), channel_id=1, source_target_pairs={{0,0},{1,4},{2,8},{3,12},{4,1},{5,5},{6,9},{7,13},{8,2},{9,6},{10,... | collective-permute-start | bytes 393224 | tf_op jit(solution)/shard_map/ppermute | solution.py:399
  8.9 1.2 %collective-permute-start.5 = (bf16[352,512]{1,0:T(8,128)(2,1)}, bf16[352,512]{1,0:T(8,128)(2,1)S(1)}, u32[]{:S(2)}, u32[]{:S(2)}) collective-permute-start(bf16[352,512]{1,0:T(8,128)(2,1)} %get-tuple-element.115), channel_id=1, source_target_pairs={{0,4},{4,0},{8,12},{12,8},{1,5},{5,1},{9,13},{13,9},{2,6},{6,2},{1... | collective-permute-start | bytes 1081352 | tf_op jit(solution)/shard_map/ppermute | solution.py:341
  10.1 0.8 copy.8.refs_0_
  10.9 1.9 %copy-done.1 = bf16[1,6,1,1,4,4,128,128]{7,6,5,4,3,2,1,0:T(8,128)(2,1)S(1)} copy-done((bf16[1,6,1,1,4,4,128,128]{7,6,5,4,3,2,1,0:T(8,128)(2,1)S(1)}, bf16[1,6,1,1,4,4,128,128]{7,6,5,4,3,2,1,0:T(8,128)(2,1)}, u32[]{:S(2)}) %copy-start.1) | copy-done | bytes 3145752
  12.8 1.8 %shard_map.78 = (bf16[6,4,128,512]{3,2,1,0:T(8,128)(2,1)S(1)}, f32[8,128]{1,0:T(8,128)S(1)}) custom-call(s32[6,4,4]{2,1,0:T(4,128)S(1)} %copy.8.refs_0_, bf16[6,4,4,128,128]{4,3,2,1,0:T(8,128)(2,1)S(1)} %bitcast.9), custom_call_target="tpu_custom_call" | custom-call | bytes 6641999 | tf_op jit(solution)/shard_map/pallas_call | solution.py:29
  14.6 1.6 %collective-permute-done.refs_0_ = bf16[2,4,32,256]{3,2,1,0:T(8,128)(2,1)} collective-permute-done((bf16[2,4,32,256]{3,2,1,0:T(8,128)(2,1)}, bf16[2,4,32,256]{3,2,1,0:T(8,128)(2,1)}, u32[]{:S(2)}, u32[]{:S(2)}) %collective-permute-start) | collective-permute-done | bytes 131104 | tf_op jit(solution)/shard_map/ppermute | solution.py:399
  16.7 1.0 %collective-permute-done.7.refs_0_ = s32[6,4,4]{2,1,0:T(4,128)S(1)} collective-permute-done((s32[6,4,4]{2,1,0:T(4,128)S(1)}, s32[6,4,4]{2,1,0:T(4,128)S(1)}, u32[]{:S(2)}, u32[]{:S(2)}) %collective-permute-start.7) | collective-permute-done | bytes 416 | tf_op jit(solution)/shard_map/ppermute | solution.py:341
  17.9 3.5 %collective-permute-done.3.refs_2_ = bf16[2,4,32,256]{3,2,1,0:T(8,128)(2,1)S(1)} collective-permute-done((bf16[2,4,32,256]{3,2,1,0:T(8,128)(2,1)}, bf16[2,4,32,256]{3,2,1,0:T(8,128)(2,1)S(1)}, u32[]{:S(2)}, u32[]{:S(2)}) %collective-permute-start.3) | collective-permute-done | bytes 131104 | tf_op jit(solution)/shard_map/ppermute | solution.py:341
  21.4 0.9 shard_map.79
  22.7 1.7 %shard_map.80 = (bf16[512,128]{1,0:T(8,128)(2,1)S(1)}, bf16[512,128]{1,0:T(8,128)(2,1)S(1)}, bf16[3,2,4,32,256]{4,3,2,1,0:T(8,128)(2,1)S(1)}, f32[256,128]{1,0:T...) custom-call(bf16[2,4,32,256]{3,2,1,0:T(8,128)(2,1)} %collective-permute-done.refs_0_, ...), custom_call_target="tpu_custom_call" | custom-call | bytes 5535000 | tf_op jit(solution)/shard_map/pallas_call | solution.py:29
  24.5 0.7 collective-permute-start.9
  25.6 1.5 %collective-permute-start.10 = (bf16[512,128]{1,0:T(8,128)(2,1)S(1)}, bf16[512,128]{1,0:T(8,128)(2,1)S(1)}, u32[]{:S(2)}, u32[]{:S(2)}) collective-permute-start(bf16[512,128]{1,0:T(8,128)(2,1)S(1)} %get-tuple-element.131), channel_id=1, source_target_pairs={{0,1},{1,0},{2,3},{3,2},{4,5},{5,4},{6,7},{7,6},{8,9},{9,8},{10,11... | collective-permute-start | bytes 393224 | tf_op jit(solution)/shard_map/ppermute | solution.py:341
  27.1 3.8 %collective-permute-done.9.refs_1_ = bf16[512,128]{1,0:T(8,128)(2,1)S(1)} collective-permute-done((bf16[512,128]{1,0:T(8,128)(2,1)S(1)}, bf16[512,128]{1,0:T(8,128)(2,1)S(1)}, u32[]{:S(2)}, u32[]{:S(2)}) %collective-permute-start.9) | collective-permute-done | bytes 131104 | tf_op jit(solution)/shard_map/ppermute | solution.py:341
  31.2 1.6 %shard_map.83 = (bf16[5,4,128,512]{3,2,1,0:T(8,128)(2,1)S(1)}, f32[8,128]{1,0:T(8,128)S(1)}) custom-call(s32[6,4,4]{2,1,0:T(4,128)S(1)} %collective-permute-done.7.refs_0_, bf16[6,4,4,128,128]{4,3,2,1,0:T(8,128)(2,1)S(1)} %collective-permute-done.8.refs_1_, f32[8,128]{1,0:T(8,128)S(1)} %get-tuple-element.128.refs_2_), custom_call_target="tpu_custom_call" | custom-call | bytes 5535000 | tf_op jit(solution)/shard_map/pallas_call | solution.py:29
  32.9 2.7 %collective-permute-start.13 = (bf16[256,128]{1,0:T(8,128)(2,1)S(1)}, bf16[256,128]{1,0:T(8,128)(2,1)S(1)}, u32[]{:S(2)}, u32[]{:S(2)}) collective-permute-start(bf16[256,128]{1,0:T(8,128)(2,1)S(1)} %get-tuple-element.145), channel_id=1, source_target_pairs={{0,2},{1,3},{2,0},{3,1},{4,6},{5,7},{6,4},{7,5},{8,10},{9,11},{10,... | collective-permute-start | bytes 196616 | tf_op jit(solution)/shard_map/ppermute | solution.py:341
  35.6 0.8 shard_map.85
  36.4 0.8 shard_map.86
  37.1 0.9 collective-permute-done.11.refs_2_
  38.4 1.3 %collective-permute-done.13.refs_2_ = bf16[256,128]{1,0:T(8,128)(2,1)S(1)} collective-permute-done((bf16[256,128]{1,0:T(8,128)(2,1)S(1)}, bf16[256,128]{1,0:T(8,128)(2,1)S(1)}, u32[]{:S(2)}, u32[]{:S(2)}) %collective-permute-start.13) | collective-permute-done | bytes 65568 | tf_op jit(solution)/shard_map/ppermute | solution.py:341
  39.9 0.8 collective-permute-start.15
  40.7 2.1 %collective-permute-done.12.refs_1_ = bf16[256,128]{1,0:T(8,128)(2,1)S(1)} collective-permute-done((bf16[256,128]{1,0:T(8,128)(2,1)S(1)}, bf16[256,128]{1,0:T(8,128)(2,1)S(1)}, u32[]{:S(2)}, u32[]{:S(2)}) %collective-permute-start.12) | collective-permute-done | bytes 65568 | tf_op jit(solution)/shard_map/ppermute | solution.py:341
  43.3 0.9 collective-permute-done.15.refs_1_
  44.6 1.2 %collective-permute-start.16 = (bf16[512,128]{1,0:T(8,128)(2,1)S(1)}, bf16[512,128]{1,0:T(8,128)(2,1)S(1)}, u32[]{:S(2)}, u32[]{:S(2)}) collective-permute-start(bf16[512,128]{1,0:T(8,128)(2,1)S(1)} %get-tuple-element.162), channel_id=1, source_target_pairs={{0,1},{1,0},{2,3},{3,2},{4,5},{5,4},{6,7},{7,6},{8,9},{9,8},{10,11... | collective-permute-start | bytes 393224 | tf_op jit(solution)/shard_map/ppermute | solution.py:341
  45.9 3.2 %collective-permute-done.14.refs_1_ = bf16[512,128]{1,0:T(8,128)(2,1)S(1)} collective-permute-done((bf16[512,128]{1,0:T(8,128)(2,1)S(1)}, bf16[512,128]{1,0:T(8,128)(2,1)S(1)}, u32[]{:S(2)}, u32[]{:S(2)}) %collective-permute-start.14) | collective-permute-done | bytes 131104 | tf_op jit(solution)/shard_map/ppermute | solution.py:341
  49.7 0.7 collective-permute-done.16.refs_1_
  50.5 2.1 %collective-permute-start.19 = (bf16[256,128]{1,0:T(8,128)(2,1)S(1)}, bf16[256,128]{1,0:T(8,128)(2,1)S(1)}, u32[]{:S(2)}, u32[]{:S(2)}) collective-permute-start(bf16[256,128]{1,0:T(8,128)(2,1)S(1)} %get-tuple-element.173), channel_id=1, source_target_pairs={{0,2},{1,3},{2,0},{3,1},{4,6},{5,7},{6,4},{7,5},{8,10},{9,11},{10,... | collective-permute-start | bytes 196616 | tf_op jit(solution)/shard_map/ppermute | solution.py:341
  53.1 1.7 %collective-permute-done.17.refs_2_ = bf16[256,128]{1,0:T(8,128)(2,1)S(1)} collective-permute-done((bf16[256,128]{1,0:T(8,128)(2,1)S(1)}, bf16[256,128]{1,0:T(8,128)(2,1)S(1)}, u32[]{:S(2)}, u32[]{:S(2)}) %collective-permute-start.17) | collective-permute-done | bytes 65568 | tf_op jit(solution)/shard_map/ppermute | solution.py:341
  55.0 0.6 collective-permute-start.18
  55.6 0.9 collective-permute-done.19.refs_2_
  56.8 0.6 collective-permute-start.20
  57.4 1.9 %collective-permute-done.18.refs_1_ = bf16[256,128]{1,0:T(8,128)(2,1)S(1)} collective-permute-done((bf16[256,128]{1,0:T(8,128)(2,1)S(1)}, bf16[256,128]{1,0:T(8,128)(2,1)S(1)}, u32[]{:S(2)}, u32[]{:S(2)}) %collective-permute-start.18) | collective-permute-done | bytes 65568 | tf_op jit(solution)/shard_map/ppermute | solution.py:341
  60.0 1.1 %collective-permute-done.20.refs_1_ = bf16[256,128]{1,0:T(8,128)(2,1)S(1)} collective-permute-done((bf16[256,128]{1,0:T(8,128)(2,1)S(1)}, bf16[256,128]{1,0:T(8,128)(2,1)S(1)}, u32[]{:S(2)}, u32[]{:S(2)}) %collective-permute-start.20) | collective-permute-done | bytes 65568 | tf_op jit(solution)/shard_map/ppermute | solution.py:341
  61.8 0.8 collective-permute-start.24
  62.6 2.2 %collective-permute-done.22.refs_1_ = bf16[512,128]{1,0:T(8,128)(2,1)S(1)} collective-permute-done((bf16[512,128]{1,0:T(8,128)(2,1)S(1)}, bf16[512,128]{1,0:T(8,128)(2,1)S(1)}, u32[]{:S(2)}, u32[]{:S(2)}) %collective-permute-start.22) | collective-permute-done | bytes 131104 | tf_op jit(solution)/shard_map/ppermute | solution.py:341
  64.9 3.5 %collective-permute-done.24.refs_1_ = bf16[512,128]{1,0:T(8,128)(2,1)S(1)} collective-permute-done((bf16[512,128]{1,0:T(8,128)(2,1)S(1)}, bf16[512,128]{1,0:T(8,128)(2,1)S(1)}, u32[]{:S(2)}, u32[]{:S(2)}) %collective-permute-start.24) | collective-permute-done | bytes 131104 | tf_op jit(solution)/shard_map/ppermute | solution.py:341
  68.4 1.8 %collective-permute-start.27 = (bf16[256,128]{1,0:T(8,128)(2,1)S(1)}, bf16[256,128]{1,0:T(8,128)(2,1)S(1)}, u32[]{:S(2)}, u32[]{:S(2)}) collective-permute-start(bf16[256,128]{1,0:T(8,128)(2,1)S(1)} %get-tuple-element.203), channel_id=1, source_target_pairs={{0,2},{1,3},{2,0},{3,1},{4,6},{5,7},{6,4},{7,5},{8,10},{9,11},{10,... | collective-permute-start | bytes 196616 | tf_op jit(solution)/shard_map/ppermute | solution.py:341
  70.2 0.9 collective-permute-done.23.refs_2_
  71.2 3.0 %collective-permute-start.25 = (bf16[3,4,32,512]{3,2,1,0:T(8,128)(2,1)S(1)}, bf16[3,4,32,512]{3,2,1,0:T(8,128)(2,1)S(1)}, u32[]{:S(2)}, u32[]{:S(2)}) collective-permute-start(bf16[3,4,32,512]{3,2,1,0:T(8,128)(2,1)S(1)} %get-tuple-element.200), channel_id=1, source_target_pairs={{0,0},{1,4},{2,8},{3,12},{4,3},{5,7},{6,11},{7,15},{8,2},{9,6},{10... | collective-permute-start | bytes 1179656 | tf_op jit(solution)/shard_map/ppermute | solution.py:554
  74.8 1.6 %collective-permute-start.29 = (bf16[256,128]{1,0:T(8,128)(2,1)S(1)}, bf16[256,128]{1,0:T(8,128)(2,1)S(1)}, u32[]{:S(2)}, u32[]{:S(2)}) collective-permute-start(bf16[256,128]{1,0:T(8,128)(2,1)S(1)} %get-tuple-element.207.refs_0_), channel_id=1, source_target_pairs={{0,16},{16,0},{1,17},{17,1},{2,18},{18,2},{3,19},{19,3},{4,20},{20... | collective-permute-start | bytes 196616 | tf_op jit(solution)/shard_map/ppermute | solution.py:551
  76.4 2.7 %collective-permute-done.26.refs_1_ = bf16[256,128]{1,0:T(8,128)(2,1)S(1)} collective-permute-done((bf16[256,128]{1,0:T(8,128)(2,1)S(1)}, bf16[256,128]{1,0:T(8,128)(2,1)S(1)}, u32[]{:S(2)}, u32[]{:S(2)}) %collective-permute-start.26) | collective-permute-done | bytes 65568 | tf_op jit(solution)/shard_map/ppermute | solution.py:551
  80.1 1.7 %collective-permute-start.30 = (bf16[256,128]{1,0:T(8,128)(2,1)S(1)}, bf16[256,128]{1,0:T(8,128)(2,1)S(1)}, u32[]{:S(2)}, u32[]{:S(2)}) collective-permute-start(bf16[256,128]{1,0:T(8,128)(2,1)S(1)} %get-tuple-element.209.refs_2_), channel_id=1, source_target_pairs={{0,8},{4,12},{8,0},{12,4},{1,9},{5,13},{9,1},{13,5},{2,10},{6,14},... | collective-permute-start | bytes 196616 | tf_op jit(solution)/shard_map/ppermute | solution.py:341
  81.7 5.3 %collective-permute-done.28.refs_1_ = bf16[256,128]{1,0:T(8,128)(2,1)S(1)} collective-permute-done((bf16[256,128]{1,0:T(8,128)(2,1)S(1)}, bf16[256,128]{1,0:T(8,128)(2,1)S(1)}, u32[]{:S(2)}, u32[]{:S(2)}) %collective-permute-start.28) | collective-permute-done | bytes 65568 | tf_op jit(solution)/shard_map/ppermute | solution.py:341
  87.0 1.3 %collective-permute-done.30.refs_3_ = bf16[256,128]{1,0:T(8,128)(2,1)S(1)} collective-permute-done((bf16[256,128]{1,0:T(8,128)(2,1)S(1)}, bf16[256,128]{1,0:T(8,128)(2,1)S(1)}, u32[]{:S(2)}, u32[]{:S(2)}) %collective-permute-start.30) | collective-permute-done | bytes 65568 | tf_op jit(solution)/shard_map/ppermute | solution.py:341
  88.5 1.2 %collective-permute-done.31.refs_1_ = bf16[1,4,32,256]{3,2,1,0:T(8,128)(2,1)S(1)} collective-permute-done((bf16[1,4,32,256]{3,2,1,0:T(8,128)(2,1)S(1)}, bf16[1,4,32,256]{3,2,1,0:T(8,128)(2,1)S(1)}, u32[]{:S(2)}, u32[]{:S(2)}) %collective-permute-start.31) | collective-permute-done | bytes 65568 | tf_op jit(solution)/shard_map/ppermute | solution.py:341
  89.7 2.6 %collective-permute-start.32 = (bf16[1,4,32,512]{3,2,1,0:T(8,128)(2,1)S(1)}, bf16[1,4,32,512]{3,2,1,0:T(8,128)(2,1)S(1)}, u32[]{:S(2)}, u32[]{:S(2)}) collective-permute-start(bf16[1,4,32,512]{3,2,1,0:T(8,128)(2,1)S(1)} %get-tuple-element.214), channel_id=1, source_target_pairs={{0,0},{1,4},{2,8},{3,12},{4,3},{5,7},{6,11},{7,15},{8,2},{9,6},{10... | collective-permute-start | bytes 393224 | tf_op jit(solution)/shard_map/ppermute | solution.py:560
  92.3 7.5 %collective-permute-done.32.refs_1_ = bf16[1,4,32,512]{3,2,1,0:T(8,128)(2,1)S(1)} collective-permute-done((bf16[1,4,32,512]{3,2,1,0:T(8,128)(2,1)S(1)}, bf16[1,4,32,512]{3,2,1,0:T(8,128)(2,1)S(1)}, u32[]{:S(2)}, u32[]{:S(2)}) %collective-permute-start.32) | collective-permute-done | bytes 131104 | tf_op jit(solution)/shard_map/ppermute | solution.py:560
  99.8 0.8 shard_map.111
  (58 shorter events, 8.8 us)
Async XLA Ops:
  0.6 20.7 %collective-permute-start.8 = (bf16[6,4,4,128,128]{4,3,2,1,0:T(8,128)(2,1)}, bf16[6,4,4,128,128]{4,3,2,1,0:T(8,128)(2,1)S(1)}, u32[]{:S(2)}, u32[]{:S(2)}) collective-permute-start(bf16[6,4,4,128,128]{4,3,2,1,0:T(8,128)(2,1)} %bitcast.8), channel_id=1, source_target_pairs={{0,4},{4,0},{8,12},{12,8},{1,5},{5,1},{9,13},{13,9},{2,6},{6,2},{1... | collective-permute-start | bytes 9437192 | tf_op jit(solution)/shard_map/ppermute | solution.py:341
  2.9 13.3 %collective-permute-start.1 = (bf16[256,512]{1,0:T(8,128)(2,1)}, bf16[256,512]{1,0:T(8,128)(2,1)}, u32[]{:S(2)}, u32[]{:S(2)}) collective-permute-start(bf16[256,512]{1,0:T(8,128)(2,1)} %get-tuple-element.111), channel_id=1, source_target_pairs={{0,8},{4,12},{8,0},{12,4},{1,9},{5,13},{9,1},{13,5},{2,10},{6,14},... | collective-permute-start | bytes 786440 | tf_op jit(solution)/shard_map/ppermute | solution.py:341
  3.5 12.7 %collective-permute-start = (bf16[2,4,32,256]{3,2,1,0:T(8,128)(2,1)}, bf16[2,4,32,256]{3,2,1,0:T(8,128)(2,1)}, u32[]{:S(2)}, u32[]{:S(2)}) collective-permute-start(bf16[2,4,32,256]{3,2,1,0:T(8,128)(2,1)} %get-tuple-element.110), channel_id=1, source_target_pairs={{0,0},{1,4},{2,8},{3,12},{4,1},{5,5},{6,9},{7,13},{8,2},{9,6},{10,... | collective-permute-start | bytes 393224 | tf_op jit(solution)/shard_map/ppermute | solution.py:399
  8.9 13.4 %collective-permute-start.5 = (bf16[352,512]{1,0:T(8,128)(2,1)}, bf16[352,512]{1,0:T(8,128)(2,1)S(1)}, u32[]{:S(2)}, u32[]{:S(2)}) collective-permute-start(bf16[352,512]{1,0:T(8,128)(2,1)} %get-tuple-element.115), channel_id=1, source_target_pairs={{0,4},{4,0},{8,12},{12,8},{1,5},{5,1},{9,13},{13,9},{2,6},{6,2},{1... | collective-permute-start | bytes 1081352 | tf_op jit(solution)/shard_map/ppermute | solution.py:341
  10.9 1.9 %copy-start.1 = (bf16[1,6,1,1,4,4,128,128]{7,6,5,4,3,2,1,0:T(8,128)(2,1)S(1)}, bf16[1,6,1,1,4,4,128,128]{7,6,5,4,3,2,1,0:T(8,128)(2,1)}, u32[]{:S(2)}) copy-start(bf16[1,6,1,1,4,4,128,128]{7,6,5,4,3,2,1,0:T(8,128)(2,1)} %param.8) | copy-start | bytes 9437188
  12.8 9.9 %copy-start = (bf16[352,512]{1,0:T(8,128)(2,1)S(1)}, bf16[352,512]{1,0:T(8,128)(2,1)}, u32[]{:S(2)}) copy-start(bf16[352,512]{1,0:T(8,128)(2,1)} %get-tuple-element.114.refs_4_.refs_3_.refs_2_) | copy-start | bytes 1081348
  16.2 5.2 %collective-permute-start.3 = (bf16[2,4,32,256]{3,2,1,0:T(8,128)(2,1)}, bf16[2,4,32,256]{3,2,1,0:T(8,128)(2,1)S(1)}, u32[]{:S(2)}, u32[]{:S(2)}) collective-permute-start(bf16[2,4,32,256]{3,2,1,0:T(8,128)(2,1)} %collective-permute-done.refs_0_), channel_id=1, source_target_pairs={{0,8},{4,12},{8,0},{12,4},{1,9},{5,13},{9,1},{13,5},{2,10},{6,14},... | collective-permute-start | bytes 393224 | tf_op jit(solution)/shard_map/ppermute | solution.py:341
  16.2 6.5 %collective-permute-start.6 = (bf16[256,512]{1,0:T(8,128)(2,1)}, bf16[256,512]{1,0:T(8,128)(2,1)S(1)}, u32[]{:S(2)}, u32[]{:S(2)}) collective-permute-start(bf16[256,512]{1,0:T(8,128)(2,1)} %collective-permute-done.1.refs_6_), channel_id=1, source_target_pairs={{0,4},{4,0},{8,12},{12,8},{1,5},{5,1},{9,13},{13,9},{2,6},{6,2},{1... | collective-permute-start | bytes 786440 | tf_op jit(solution)/shard_map/ppermute | solution.py:341
  16.2 1.5 %collective-permute-start.7 = (s32[6,4,4]{2,1,0:T(4,128)S(1)}, s32[6,4,4]{2,1,0:T(4,128)S(1)}, u32[]{:S(2)}, u32[]{:S(2)}) collective-permute-start(s32[6,4,4]{2,1,0:T(4,128)S(1)} %copy.8.refs_0_), channel_id=1, source_target_pairs={{0,4},{4,0},{8,12},{12,8},{1,5},{5,1},{9,13},{13,9},{2,6},{6,2},{1... | collective-permute-start | bytes 1160 | tf_op jit(solution)/shard_map/ppermute | solution.py:341
  17.7 4.6 %collective-permute-start.2 = (bf16[2,4,32,256]{3,2,1,0:T(8,128)(2,1)}, bf16[2,4,32,256]{3,2,1,0:T(8,128)(2,1)S(1)}, u32[]{:S(2)}, u32[]{:S(2)}) collective-permute-start(bf16[2,4,32,256]{3,2,1,0:T(8,128)(2,1)} %collective-permute-done.refs_0_), channel_id=1, source_target_pairs={{0,4},{4,0},{8,12},{12,8},{1,5},{5,1},{9,13},{13,9},{2,6},{6,2},{1... | collective-permute-start | bytes 393224 | tf_op jit(solution)/shard_map/ppermute | solution.py:341
  21.4 1.3 %collective-permute-start.4 = (bf16[2,4,32,256]{3,2,1,0:T(8,128)(2,1)S(1)}, bf16[2,4,32,256]{3,2,1,0:T(8,128)(2,1)S(1)}, u32[]{:S(2)}, u32[]{:S(2)}) collective-permute-start(bf16[2,4,32,256]{3,2,1,0:T(8,128)(2,1)S(1)} %collective-permute-done.3.refs_2_), channel_id=1, source_target_pairs={{0,4},{4,0},{8,12},{12,8},{1,5},{5,1},{9,13},{13,9},{2,6},{6,2},{1... | collective-permute-start | bytes 393224 | tf_op jit(solution)/shard_map/ppermute | solution.py:341
  24.5 6.4 %collective-permute-start.9 = (bf16[512,128]{1,0:T(8,128)(2,1)S(1)}, bf16[512,128]{1,0:T(8,128)(2,1)S(1)}, u32[]{:S(2)}, u32[]{:S(2)}) collective-permute-start(bf16[512,128]{1,0:T(8,128)(2,1)S(1)} %get-tuple-element.124), channel_id=1, source_target_pairs={{0,1},{1,0},{2,3},{3,2},{4,5},{5,4},{6,7},{7,6},{8,9},{9,8},{10,11... | collective-permute-start | bytes 393224 | tf_op jit(solution)/shard_map/ppermute | solution.py:341
  25.6 7.3 %collective-permute-start.10 = (bf16[512,128]{1,0:T(8,128)(2,1)S(1)}, bf16[512,128]{1,0:T(8,128)(2,1)S(1)}, u32[]{:S(2)}, u32[]{:S(2)}) collective-permute-start(bf16[512,128]{1,0:T(8,128)(2,1)S(1)} %get-tuple-element.131), channel_id=1, source_target_pairs={{0,1},{1,0},{2,3},{3,2},{4,5},{5,4},{6,7},{7,6},{8,9},{9,8},{10,11... | collective-permute-start | bytes 393224 | tf_op jit(solution)/shard_map/ppermute | solution.py:341
  30.9 7.2 %collective-permute-start.11 = (bf16[256,128]{1,0:T(8,128)(2,1)S(1)}, bf16[256,128]{1,0:T(8,128)(2,1)S(1)}, u32[]{:S(2)}, u32[]{:S(2)}) collective-permute-start(bf16[256,128]{1,0:T(8,128)(2,1)S(1)} %get-tuple-element.140), channel_id=1, source_target_pairs={{0,2},{1,3},{2,0},{3,1},{4,6},{5,7},{6,4},{7,5},{8,10},{9,11},{10,... | collective-permute-start | bytes 196616 | tf_op jit(solution)/shard_map/ppermute | solution.py:341
  32.9 6.7 %collective-permute-start.13 = (bf16[256,128]{1,0:T(8,128)(2,1)S(1)}, bf16[256,128]{1,0:T(8,128)(2,1)S(1)}, u32[]{:S(2)}, u32[]{:S(2)}) collective-permute-start(bf16[256,128]{1,0:T(8,128)(2,1)S(1)} %get-tuple-element.145), channel_id=1, source_target_pairs={{0,2},{1,3},{2,0},{3,1},{4,6},{5,7},{6,4},{7,5},{8,10},{9,11},{10,... | collective-permute-start | bytes 196616 | tf_op jit(solution)/shard_map/ppermute | solution.py:341
  38.3 4.5 %collective-permute-start.12 = (bf16[256,128]{1,0:T(8,128)(2,1)S(1)}, bf16[256,128]{1,0:T(8,128)(2,1)S(1)}, u32[]{:S(2)}, u32[]{:S(2)}) collective-permute-start(bf16[256,128]{1,0:T(8,128)(2,1)S(1)} %get-tuple-element.142.refs_0_), channel_id=1, source_target_pairs={{0,8},{4,12},{8,0},{12,4},{1,9},{5,13},{9,1},{13,5},{2,10},{6,14},... | collective-permute-start | bytes 196616 | tf_op jit(solution)/shard_map/ppermute | solution.py:341
  39.9 4.3 %collective-permute-start.15 = (bf16[256,128]{1,0:T(8,128)(2,1)S(1)}, bf16[256,128]{1,0:T(8,128)(2,1)S(1)}, u32[]{:S(2)}, u32[]{:S(2)}) collective-permute-start(bf16[256,128]{1,0:T(8,128)(2,1)S(1)} %get-tuple-element.152.refs_0_), channel_id=1, source_target_pairs={{0,8},{4,12},{8,0},{12,4},{1,9},{5,13},{9,1},{13,5},{2,10},{6,14},... | collective-permute-start | bytes 196616 | tf_op jit(solution)/shard_map/ppermute | solution.py:341
  43.2 5.8 %collective-permute-start.14 = (bf16[512,128]{1,0:T(8,128)(2,1)S(1)}, bf16[512,128]{1,0:T(8,128)(2,1)S(1)}, u32[]{:S(2)}, u32[]{:S(2)}) collective-permute-start(bf16[512,128]{1,0:T(8,128)(2,1)S(1)} %get-tuple-element.151), channel_id=1, source_target_pairs={{0,1},{1,0},{2,3},{3,2},{4,5},{5,4},{6,7},{7,6},{8,9},{9,8},{10,11... | collective-permute-start | bytes 393224 | tf_op jit(solution)/shard_map/ppermute | solution.py:341
  44.6 5.8 %collective-permute-start.16 = (bf16[512,128]{1,0:T(8,128)(2,1)S(1)}, bf16[512,128]{1,0:T(8,128)(2,1)S(1)}, u32[]{:S(2)}, u32[]{:S(2)}) collective-permute-start(bf16[512,128]{1,0:T(8,128)(2,1)S(1)} %get-tuple-element.162), channel_id=1, source_target_pairs={{0,1},{1,0},{2,3},{3,2},{4,5},{5,4},{6,7},{7,6},{8,9},{9,8},{10,11... | collective-permute-start | bytes 393224 | tf_op jit(solution)/shard_map/ppermute | solution.py:341
  49.1 5.7 %collective-permute-start.17 = (bf16[256,128]{1,0:T(8,128)(2,1)S(1)}, bf16[256,128]{1,0:T(8,128)(2,1)S(1)}, u32[]{:S(2)}, u32[]{:S(2)}) collective-permute-start(bf16[256,128]{1,0:T(8,128)(2,1)S(1)} %get-tuple-element.168), channel_id=1, source_target_pairs={{0,2},{1,3},{2,0},{3,1},{4,6},{5,7},{6,4},{7,5},{8,10},{9,11},{10,... | collective-permute-start | bytes 196616 | tf_op jit(solution)/shard_map/ppermute | solution.py:341
  50.5 6.0 %collective-permute-start.19 = (bf16[256,128]{1,0:T(8,128)(2,1)S(1)}, bf16[256,128]{1,0:T(8,128)(2,1)S(1)}, u32[]{:S(2)}, u32[]{:S(2)}) collective-permute-start(bf16[256,128]{1,0:T(8,128)(2,1)S(1)} %get-tuple-element.173), channel_id=1, source_target_pairs={{0,2},{1,3},{2,0},{3,1},{4,6},{5,7},{6,4},{7,5},{8,10},{9,11},{10,... | collective-permute-start | bytes 196616 | tf_op jit(solution)/shard_map/ppermute | solution.py:341
  55.0 4.3 %collective-permute-start.18 = (bf16[256,128]{1,0:T(8,128)(2,1)S(1)}, bf16[256,128]{1,0:T(8,128)(2,1)S(1)}, u32[]{:S(2)}, u32[]{:S(2)}) collective-permute-start(bf16[256,128]{1,0:T(8,128)(2,1)S(1)} %get-tuple-element.170.refs_0_), channel_id=1, source_target_pairs={{0,8},{4,12},{8,0},{12,4},{1,9},{5,13},{9,1},{13,5},{2,10},{6,14},... | collective-permute-start | bytes 196616 | tf_op jit(solution)/shard_map/ppermute | solution.py:341
  56.8 4.3 %collective-permute-start.20 = (bf16[256,128]{1,0:T(8,128)(2,1)S(1)}, bf16[256,128]{1,0:T(8,128)(2,1)S(1)}, u32[]{:S(2)}, u32[]{:S(2)}) collective-permute-start(bf16[256,128]{1,0:T(8,128)(2,1)S(1)} %get-tuple-element.177.refs_0_), channel_id=1, source_target_pairs={{0,8},{4,12},{8,0},{12,4},{1,9},{5,13},{9,1},{13,5},{2,10},{6,14},... | collective-permute-start | bytes 196616 | tf_op jit(solution)/shard_map/ppermute | solution.py:341
  59.8 5.0 %collective-permute-start.22 = (bf16[512,128]{1,0:T(8,128)(2,1)S(1)}, bf16[512,128]{1,0:T(8,128)(2,1)S(1)}, u32[]{:S(2)}, u32[]{:S(2)}) collective-permute-start(bf16[512,128]{1,0:T(8,128)(2,1)S(1)} %get-tuple-element.191), channel_id=1, source_target_pairs={{0,1},{1,0},{2,3},{3,2},{4,5},{5,4},{6,7},{7,6},{8,9},{9,8},{10,11... | collective-permute-start | bytes 393224 | tf_op jit(solution)/shard_map/ppermute | solution.py:341
  61.7 9.4 %collective-permute-start.21 = (bf16[3,4,32,256]{3,2,1,0:T(8,128)(2,1)S(1)}, bf16[3,4,32,256]{3,2,1,0:T(8,128)(2,1)S(1)}, u32[]{:S(2)}, u32[]{:S(2)}) collective-permute-start(bf16[3,4,32,256]{3,2,1,0:T(8,128)(2,1)S(1)} %get-tuple-element.189), channel_id=1, source_target_pairs={{0,4},{4,0},{8,12},{12,8},{1,5},{5,1},{9,13},{13,9},{2,6},{6,2},{1... | collective-permute-start | bytes 589832 | tf_op jit(solution)/shard_map/ppermute | solution.py:341
  61.8 6.6 %collective-permute-start.24 = (bf16[512,128]{1,0:T(8,128)(2,1)S(1)}, bf16[512,128]{1,0:T(8,128)(2,1)S(1)}, u32[]{:S(2)}, u32[]{:S(2)}) collective-permute-start(bf16[512,128]{1,0:T(8,128)(2,1)S(1)} %get-tuple-element.196), channel_id=1, source_target_pairs={{0,1},{1,0},{2,3},{3,2},{4,5},{5,4},{6,7},{7,6},{8,9},{9,8},{10,11... | collective-permute-start | bytes 393224 | tf_op jit(solution)/shard_map/ppermute | solution.py:341
  64.8 6.3 %collective-permute-start.23 = (bf16[256,128]{1,0:T(8,128)(2,1)S(1)}, bf16[256,128]{1,0:T(8,128)(2,1)S(1)}, u32[]{:S(2)}, u32[]{:S(2)}) collective-permute-start(bf16[256,128]{1,0:T(8,128)(2,1)S(1)} %get-tuple-element.194), channel_id=1, source_target_pairs={{0,2},{1,3},{2,0},{3,1},{4,6},{5,7},{6,4},{7,5},{8,10},{9,11},{10,... | collective-permute-start | bytes 196616 | tf_op jit(solution)/shard_map/ppermute | solution.py:341
  68.4 6.3 %collective-permute-start.27 = (bf16[256,128]{1,0:T(8,128)(2,1)S(1)}, bf16[256,128]{1,0:T(8,128)(2,1)S(1)}, u32[]{:S(2)}, u32[]{:S(2)}) collective-permute-start(bf16[256,128]{1,0:T(8,128)(2,1)S(1)} %get-tuple-element.203), channel_id=1, source_target_pairs={{0,2},{1,3},{2,0},{3,1},{4,6},{5,7},{6,4},{7,5},{8,10},{9,11},{10,... | collective-permute-start | bytes 196616 | tf_op jit(solution)/shard_map/ppermute | solution.py:341
  71.2 28.6 %collective-permute-start.25 = (bf16[3,4,32,512]{3,2,1,0:T(8,128)(2,1)S(1)}, bf16[3,4,32,512]{3,2,1,0:T(8,128)(2,1)S(1)}, u32[]{:S(2)}, u32[]{:S(2)}) collective-permute-start(bf16[3,4,32,512]{3,2,1,0:T(8,128)(2,1)S(1)} %get-tuple-element.200), channel_id=1, source_target_pairs={{0,0},{1,4},{2,8},{3,12},{4,3},{5,7},{6,11},{7,15},{8,2},{9,6},{10... | collective-permute-start | bytes 1179656 | tf_op jit(solution)/shard_map/ppermute | solution.py:554
  74.2 4.9 %collective-permute-start.26 = (bf16[256,128]{1,0:T(8,128)(2,1)S(1)}, bf16[256,128]{1,0:T(8,128)(2,1)S(1)}, u32[]{:S(2)}, u32[]{:S(2)}) collective-permute-start(bf16[256,128]{1,0:T(8,128)(2,1)S(1)} %get-tuple-element.201.refs_0_), channel_id=1, source_target_pairs={{0,16},{16,0},{1,17},{17,1},{2,18},{18,2},{3,19},{19,3},{4,20},{20... | collective-permute-start | bytes 196616 | tf_op jit(solution)/shard_map/ppermute | solution.py:551
  74.8 5.0 %collective-permute-start.29 = (bf16[256,128]{1,0:T(8,128)(2,1)S(1)}, bf16[256,128]{1,0:T(8,128)(2,1)S(1)}, u32[]{:S(2)}, u32[]{:S(2)}) collective-permute-start(bf16[256,128]{1,0:T(8,128)(2,1)S(1)} %get-tuple-element.207.refs_0_), channel_id=1, source_target_pairs={{0,16},{16,0},{1,17},{17,1},{2,18},{18,2},{3,19},{19,3},{4,20},{20... | collective-permute-start | bytes 196616 | tf_op jit(solution)/shard_map/ppermute | solution.py:551
  79.4 7.7 %collective-permute-start.28 = (bf16[256,128]{1,0:T(8,128)(2,1)S(1)}, bf16[256,128]{1,0:T(8,128)(2,1)S(1)}, u32[]{:S(2)}, u32[]{:S(2)}) collective-permute-start(bf16[256,128]{1,0:T(8,128)(2,1)S(1)} %get-tuple-element.206.refs_0_), channel_id=1, source_target_pairs={{0,8},{4,12},{8,0},{12,4},{1,9},{5,13},{9,1},{13,5},{2,10},{6,14},... | collective-permute-start | bytes 196616 | tf_op jit(solution)/shard_map/ppermute | solution.py:341
  80.1 8.3 %collective-permute-start.30 = (bf16[256,128]{1,0:T(8,128)(2,1)S(1)}, bf16[256,128]{1,0:T(8,128)(2,1)S(1)}, u32[]{:S(2)}, u32[]{:S(2)}) collective-permute-start(bf16[256,128]{1,0:T(8,128)(2,1)S(1)} %get-tuple-element.209.refs_2_), channel_id=1, source_target_pairs={{0,8},{4,12},{8,0},{12,4},{1,9},{5,13},{9,1},{13,5},{2,10},{6,14},... | collective-permute-start | bytes 196616 | tf_op jit(solution)/shard_map/ppermute | solution.py:341
  88.4 1.3 %collective-permute-start.31 = (bf16[1,4,32,256]{3,2,1,0:T(8,128)(2,1)S(1)}, bf16[1,4,32,256]{3,2,1,0:T(8,128)(2,1)S(1)}, u32[]{:S(2)}, u32[]{:S(2)}) collective-permute-start(bf16[1,4,32,256]{3,2,1,0:T(8,128)(2,1)S(1)} %get-tuple-element.212), channel_id=1, source_target_pairs={{0,4},{4,0},{8,12},{12,8},{1,5},{5,1},{9,13},{13,9},{2,6},{6,2},{1... | collective-permute-start | bytes 196616 | tf_op jit(solution)/shard_map/ppermute | solution.py:341
  89.7 10.1 %collective-permute-start.32 = (bf16[1,4,32,512]{3,2,1,0:T(8,128)(2,1)S(1)}, bf16[1,4,32,512]{3,2,1,0:T(8,128)(2,1)S(1)}, u32[]{:S(2)}, u32[]{:S(2)}) collective-permute-start(bf16[1,4,32,512]{3,2,1,0:T(8,128)(2,1)S(1)} %get-tuple-element.214), channel_id=1, source_target_pairs={{0,0},{1,4},{2,8},{3,12},{4,3},{5,7},{6,11},{7,15},{8,2},{9,6},{10... | collective-permute-start | bytes 393224 | tf_op jit(solution)/shard_map/ppermute | solution.py:560
